TPU v7x, 32 devices: a whole 2x2x4 slice. The times are simulated.
32 devices in a mesh: parts: 2 (over y), row: 4 (over z), loop: 4 (over x, core).
Axes of the slice: x: 2, y: 2, z: 4, core: 2. Of those that a mesh axis runs over, the one named last changes fastest.
Arguments:
- geometry: float32 [7, 16384], P(None, ('parts', 'row', 'loop')), parts along dimension 1, as said below
- adjoint: float32 [64, 16384], P(None, ('parts', 'row', 'loop')), parts along dimension 1, may hold values from -1.8 to 1.8
- forward: float32 [64, 16384], P(None, ('parts', 'row', 'loop')), parts along dimension 1, may hold values from -1.8 to 1.8
- owner_map: int32 [4, 16384], P(None, ('parts', 'row', 'loop')), parts along dimension 1, may hold values from 0 to 511
- owner_weight: float32 [4, 16384], P(None, ('parts', 'row', 'loop')), parts along dimension 1, may hold values from 0.1 to 1
Outputs:
- shape_gradient: float32 [6, 1024], P(None, ('parts', 'row', 'loop')), parts along dimension 1
There are 2 independent parts, one for each index of `parts`. A program takes and returns all parts, laid end to end along the dimension named above; each array names one. Nothing has to cross between parts.
Inputs may be any that keep to these rules, and one draw needn't show every extreme that they name: Rows 0 to 2 of geometry are centroids in metres on a hull surface, with the axial coordinate (row 0) not falling with the panel number; rows 3 to 5 are its unit outward normals, row 6 areas between 0.004 and 0.04.
All inputs are finite; a program needn't handle non-finite values.
Results may differ from a plain program's by a relative error of at most 0.0003.
Values sent between devices are 32-bit elements; how exact they have to be, the bound alone decides.
No kernel may reach another device: no remote copies, remote signals or barrier semaphores. Data moves between devices by JAX's collectives and lax.ppermute only.
A program may use at most 64 MiB of HBM per device.

v0:
```python
import math

import jax
import jax.numpy as jnp
from jax import lax
from jax.sharding import PartitionSpec as P

CP_DEV = 32


FOUR_PI = 4.0 * math.pi
WAVENUM = 2.0 * math.pi * 6000.0 / 1500.0


def coupled_sum(target_geo, source_geo, panel_area, real_part, imag_part):
    offset = target_geo[0:3, :, None] - source_geo[0:3, None, :]
    radius = jnp.sqrt(jnp.sum(offset * offset, axis=0) + panel_area[None, :])
    inverse = 1.0 / radius
    phases = WAVENUM * radius
    green_re = jnp.cos(phases) * inverse / FOUR_PI
    green_im = jnp.sin(phases) * inverse / FOUR_PI
    slope_re = -WAVENUM * green_im - green_re * inverse
    slope_im = WAVENUM * green_re - green_im * inverse
    src_proj = -jnp.sum(offset * source_geo[3:6, None, :], axis=0) * inverse
    tgt_proj = jnp.sum(offset * target_geo[3:6, :, None], axis=0) * inverse
    kern_re = panel_area[None, :] * (slope_re * src_proj - slope_im * tgt_proj / WAVENUM)
    kern_im = panel_area[None, :] * (slope_im * src_proj + slope_re * tgt_proj / WAVENUM)
    return jnp.sum(kern_re * real_part - kern_im * imag_part)


def source_table(forward):
    half_rows = forward.shape[0] // 2
    rotated = jnp.concatenate([forward[half_rows:], -forward[:half_rows]], axis=0)
    return jnp.concatenate([forward, rotated], axis=1)


def tile_grads(target_geo, target_adj, source_geo, src_table):
    width = source_geo.shape[1]
    products = lax.dot_general(
        target_adj,
        src_table,
        (((0,), (0,)), ((), ())),
        precision=lax.Precision.HIGHEST,
        preferred_element_type=jnp.float32,
    )
    grad_fn = jax.grad(coupled_sum, argnums=(0, 1))
    return grad_fn(
        target_geo[0:6], source_geo[0:6], source_geo[6], products[:, :width], products[:, width:]
    )


def owner_add(totals, owners, weights, panel_grad):
    weighted = weights[:, None, :] * panel_grad[None, :, :]
    flat = jnp.transpose(weighted, (1, 0, 2)).reshape(6, -1)
    return totals.at[:, owners.reshape(-1)].add(flat)


def on_device(geometry, adjoint, forward, owner_map, owner_weight):
    src_table = source_table(forward)
    loop_size = lax.axis_size("loop")
    cp_total = CP_DEV * lax.axis_size("row") * loop_size
    empty_cp = jnp.zeros((6, cp_total), jnp.float32)
    tgt_grad, src_grad = tile_grads(
        lax.all_gather(geometry, "loop", axis=1, tiled=True),
        lax.all_gather(adjoint, "loop", axis=1, tiled=True),
        geometry,
        src_table,
    )
    all_targets = tgt_grad
    src_total, all_targets = (src_grad, all_targets)
    own_targets = lax.psum_scatter(all_targets, "loop", scatter_dimension=1, tiled=True)
    partial_cp = owner_add(empty_cp, owner_map, owner_weight, src_total + own_targets)
    return lax.psum_scatter(partial_cp, ("row", "loop"), scatter_dimension=1, tiled=True)


def solution(mesh):
    in_specs = (
        P(None, ("parts", "row", "loop")),
        P(None, ("parts", "row", "loop")),
        P(None, ("parts", "row", "loop")),
        P(None, ("parts", "row", "loop")),
        P(None, ("parts", "row", "loop")),
    )
    out_specs = P(None, ("parts", "row", "loop"))
    return jax.shard_map(
        on_device, mesh=mesh, in_specs=in_specs, out_specs=out_specs, check_vma=False
    )
```

profile of v0, /device:TPU:0, one launch (start us, length us, event | category | flops | bytes accessed | tf_op | source)
XLA Modules:
  0.0 209.4 jit_solution(8980265237414914424)
XLA Ops:
  6.5 0.0 reduce-scatter.3.cloned.1.call-start
  6.5 6.4 %all_gather.6 = f32[7,2048]{1,0:T(8,128)S(1)} all-gather(f32[7,512]{1,0:T(8,128)} %param.5), channel_id=1, replica_groups=mesh['parts'=2,'row'=4,'loop'=4] {'loop'}, dimensions={1}, use_global_device_ids=true | all-gather | bytes 71680 | tf_op jit(solution)/shard_map/all_gather | solution.py:64
  13.0 0.8 fusion.20
  13.7 0.7 slice.35
  14.5 9.3 %fusion = (f32[2048,512]{1,0:T(8,128)}, f32[2048,512]{1,0:T(8,128)}, f32[2048,512]{1,0:T(8,128)}) fusion(f32[3,512]{1,0:T(4,128)S(1)} %get-tuple-element.20, f32[3,2048]{1,0:T(4,128)S(1)} %get-tuple-element.18, f32[3,2048]{1,0:T(4,128)S(1)} %get-tuple-element.17, f32[3,512]{1,0:T(4,128)S(1)} %get-tuple-element.19), kind=kLoop, calls=%fused_computation.8 | loop fusion | flops 18874368 | bytes 12644352 | tf_op jit(solution)/shard_map/jvp()/reduce_sum | solution.py:17
  23.8 5.4 %copy.10 = f32[2048,512]{0,1:T(8,128)} copy(f32[2048,512]{1,0:T(8,128)} %get-tuple-element.9) | data formatting | bytes 8388608 | tf_op jit(solution)/shard_map/jvp()/reduce_sum | solution.py:17
  29.2 5.4 %copy.13 = f32[2048,512]{0,1:T(8,128)} copy(f32[2048,512]{1,0:T(8,128)} %get-tuple-element.11) | data formatting | bytes 8388608 | tf_op jit(solution)/shard_map/jvp()/reduce_sum | solution.py:24
  34.5 0.0 copy-start.3
  34.6 0.0 copy-start.4
  34.6 5.5 %copy.14 = f32[2048,512]{0,1:T(8,128)} copy(f32[2048,512]{1,0:T(8,128)} %get-tuple-element.10) | data formatting | bytes 8388608 | tf_op jit(solution)/shard_map/jvp()/reduce_sum | solution.py:25
  40.0 0.0 copy-done.3
  40.0 0.0 copy-done.4
  40.1 7.8 %all_gather.7 = f32[64,2048]{1,0:T(8,128)S(1)} all-gather(f32[64,512]{1,0:T(8,128)S(1)} %copy-done.4), channel_id=1, replica_groups=mesh['parts'=2,'row'=4,'loop'=4] {'loop'}, dimensions={1}, use_global_device_ids=true | all-gather | bytes 655360 | tf_op jit(solution)/shard_map/all_gather | solution.py:65
  47.9 0.0 copy-start
  47.9 0.0 copy-start.1
  47.9 0.0 copy-start.2
  47.9 6.9 %convolution_bitcast_fusion = f32[2048,1024]{0,1:T(8,128)S(1)} fusion(f32[64,2048]{1,0:T(8,128)S(1)} %all_gather.7, f32[32,512]{1,0:T(8,128)S(1)} %get-tuple-element.16, f32[32,512]{1,0:T(8,128)S(1)} %get-tuple-element.15, f32[64,512]{1,0:T(8,128)S(1)} %copy-done.3), kind=kOutput, calls=%fused_computation.15 | convolution fusion | flops 1610743808 | bytes 9175040 | tf_op jit(solution)/shard_map/dot_general | solution.py:39
  54.8 0.0 copy-done
  54.8 0.0 copy-done.1
  54.8 0.0 copy-done.2
  54.8 30.4 %multiply_negate_fusion = (f32[2048,512]{0,1:T(8,128)}, f32[2048,512]{0,1:T(8,128)}, f32[2048,512]{0,1:T(8,128)}) fusion(f32[2048,1024]{0,1:T(8,128)S(1)} %convolution_bitcast_fusion, f32[2048,512]{0,1:T(8,128)S(1)} %copy-done, f32[512]{0:T(512)S(1)} %broadcast_multiply_fusion, f32[512]{0:T(512)S(1)} %bitcast.19, f32[2048,512]{0,1:T(8,128)S(1)} %copy-done.2, ...), kind=kLoop, calls=%fused_computation.21 | loop fusion | flops 74448896 | bytes 33558528 | tf_op jit(solution)/shard_map/transpose(jvp())/neg | solution.py:24
  85.2 5.3 %copy.11 = f32[2048,512]{1,0:T(8,128)} copy(f32[2048,512]{0,1:T(8,128)} %get-tuple-element.12) | data formatting | bytes 8388608 | tf_op jit(solution)/shard_map/transpose(jvp())/neg | solution.py:24
  90.5 5.4 %copy.12 = f32[2048,512]{1,0:T(8,128)} copy(f32[2048,512]{0,1:T(8,128)} %get-tuple-element.14) | data formatting | bytes 8388608 | tf_op jit(solution)/shard_map/transpose(jvp())/mul | solution.py:25
  95.9 5.3 %copy.16 = f32[2048,512]{1,0:T(8,128)} copy(f32[2048,512]{0,1:T(8,128)} %get-tuple-element.13) | data formatting | bytes 8388608 | tf_op jit(solution)/shard_map/transpose(jvp())/mul | solution.py:17
  101.3 0.0 copy-start.5
  101.3 0.0 copy-start.6
  101.3 9.5 %fusion.6 = (f32[3,512]{1,0:T(4,128)S(1)}, f32[3,2048]{1,0:T(4,128)S(1)}, f32[3,512]{1,0:T(4,128)S(1)}, f32[3,2048]{1,0:T(4,128)S(1)}) fusion(f32[2048,512]{1,0:T(8,128)} %copy.16, f32[3,512]{1,0:T(4,128)S(1)} %get-tuple-element.19, f32[3,2048]{1,0:T(4,128)S(1)} %get-tuple-element.17, f32[2048,512]{1,0:T(8,128)} %copy.12, f32[2048,512]{1,0:T(8,128)} %copy.11, ...), kind=kLoop, calls=%fused_computation.14 | loop fusion | flops 40879104 | bytes 12705792 | tf_op jit(solution)/shard_map/transpose(jvp())/reduce_sum | solution.py:16
  110.7 0.6 pad_add_fusion
  111.4 0.0 reduce-scatter.3.cloned.1.call-update
  111.4 0.0 reduce-scatter.5.cloned.1.call-start
  111.4 0.0 copy-done.5
  111.5 0.0 copy-done.6
  111.5 20.8 %reduce-scatter.3.cloned.1.call-done = f32[6,512]{1,0:T(8,128)} async-done(((f32[6,2048]{1,0:T(8,128)}), f32[6,512]{1,0:T(8,128)}) %reduce-scatter.3.cloned.1.call-update) | async-done | bytes 12304 | tf_op jit(solution)/shard_map/reduce_scatter | solution.py:71
  132.4 0.7 add_add_fusion.1
  133.1 0.1 copy.17
  133.2 0.3 bitcast_multiply_fusion
  133.6 12.2 %scatter_custom_fusion = f32[6,512]{0,1:T(8,128)} fusion(s32[2048]{0:T(1024)S(1)} %bitcast.22, f32[6,2048]{0,1:T(8,128)S(1)} %bitcast_multiply_fusion, f32[]{:T(128)} %constant.8.clone.1), kind=kCustom, calls=%fused_computation.30 | custom fusion | flops 12288 | bytes 1060868 | tf_op jit(solution)/shard_map/scatter-add | solution.py:55
  145.7 0.0 reduce-scatter.5.cloned.1.call-update
  145.8 55.5 %reduce-scatter.5.cloned.1.call-done = f32[6,32]{0,1:T(8,128)} async-done(((f32[6,512]{0,1:T(8,128)}), f32[6,32]{0,1:T(8,128)}) %reduce-scatter.5.cloned.1.call-update) | async-done | bytes 784 | tf_op jit(solution)/shard_map/reduce_scatter | solution.py:73
  201.2 1.4 copy.18
  (7 shorter events, 0.1 us)
Async XLA Ops:
  6.5 125.8 %reduce-scatter.3.cloned.1.call-start = ((), (), s32[]{:S(2)}) async-start(), calls=%async_computation.2 | async-start | bytes 81920 | tf_op jit(solution)/shard_map/reduce_scatter | solution.py:71
  34.5 5.5 %copy-start.3 = (f32[64,512]{1,0:T(8,128)S(1)}, f32[64,512]{1,0:T(8,128)}, u32[]{:S(2)}) copy-start(f32[64,512]{1,0:T(8,128)} %param.7) | copy-start | bytes 393220
  34.6 5.5 %copy-start.4 = (f32[64,512]{1,0:T(8,128)S(1)}, f32[64,512]{1,0:T(8,128)}, u32[]{:S(2)}) copy-start(f32[64,512]{1,0:T(8,128)} %param.6) | copy-start | bytes 393220
  47.9 6.9 %copy-start = (f32[2048,512]{0,1:T(8,128)S(1)}, f32[2048,512]{0,1:T(8,128)}, u32[]{:S(2)}) copy-start(f32[2048,512]{0,1:T(8,128)} %copy.10) | copy-start | bytes 12582916
  47.9 6.9 %copy-start.1 = (f32[2048,512]{0,1:T(8,128)S(1)}, f32[2048,512]{0,1:T(8,128)}, u32[]{:S(2)}) copy-start(f32[2048,512]{0,1:T(8,128)} %copy.13) | copy-start | bytes 12582916
  47.9 6.9 %copy-start.2 = (f32[2048,512]{0,1:T(8,128)S(1)}, f32[2048,512]{0,1:T(8,128)}, u32[]{:S(2)}) copy-start(f32[2048,512]{0,1:T(8,128)} %copy.14) | copy-start | bytes 12582916
  101.3 10.2 %copy-start.5 = (s32[4,512]{1,0:T(4,128)S(1)}, s32[4,512]{1,0:T(4,128)}, u32[]{:S(2)}) copy-start(s32[4,512]{1,0:T(4,128)} %param.8) | copy-start | bytes 24580
  101.3 10.2 %copy-start.6 = (f32[4,512]{1,0:T(4,128)S(1)}, f32[4,512]{1,0:T(4,128)}, u32[]{:S(2)}) copy-start(f32[4,512]{1,0:T(4,128)} %param.9) | copy-start | bytes 24580
  111.4 89.8 %reduce-scatter.5.cloned.1.call-start = ((), (), s32[]{:S(2)}) async-start(), calls=%async_computation.3 | async-start | bytes 278528 | tf_op jit(solution)/shard_map/reduce_scatter | solution.py:73
Sparse Core Ops, SparseCore 0:
  111.5 20.7 reduce-scatter.2
  145.9 55.2 reduce-scatter.4
where the time goes:
time: 210 us; the launch traced here: 209 us
  waiting for transfers between devices  76.3 us (36%)
  other arithmetic  63 us (30%)
  local copies, waits for them, and re-layouts  35.4 us (17%)
  blocking collectives  14.2 us (7%)
  between operations  13.5 us (6%)
  matrix products  6.89 us (3%)
    reduce_scatter x1, waiting for transfers between devices, on_device(): lax.psum_scatter(partial_cp, ('row', 'loop'), scatter_dimension=1, tiled=...  55.5 us
    neg x1, other arithmetic, coupled_sum(): src_proj = -jnp.sum(offset * source_geo[3:6, None, :], axis=0) * inverse  30.4 us
    reduce_scatter x1, waiting for transfers between devices, on_device(): lax.psum_scatter(all_targets, 'loop', scatter_dimension=1, tiled=True)  20.8 us
    scatter-add x1, other arithmetic, owner_add(): return totals.at[:, owners.reshape(-1)].add(flat)  12.2 us
    reduce_sum x1, other arithmetic, coupled_sum(): offset = target_geo[0:3, :, None] - source_geo[0:3, None, :]  9.47 us
    reduce_sum x1, other arithmetic, coupled_sum(): radius = jnp.sqrt(jnp.sum(offset * offset, axis=0) + panel_area[None, :])  9.29 us
    all_gather x1, blocking collectives, on_device(): lax.all_gather(adjoint, 'loop', axis=1, tiled=True)  7.83 us
    dot_general x1, matrix products, tile_grads(): lax.dot_general(target_adj, src_table, (((0,), (0,)), ((), ())), precisio...  6.89 us
  transfers between devices with their start and end apart: 2, of which 2 were waited for; matrix products, arithmetic and copies ran while one was open for 0% of the time, Pallas kernels for 0%

commit v1 on v0

v1 whole, which is shorter than its diff:
```python
import functools
import math

import jax
import jax.numpy as jnp
from jax import lax
from jax.experimental import pallas as pl
from jax.experimental.pallas import tpu as pltpu
from jax.sharding import PartitionSpec as P

WAVENUM = 2.0 * math.pi * 6000.0 / 1500.0
TURNS = WAVENUM / (2.0 * math.pi)
PAIR_SCALE = WAVENUM**3 / (4.0 * math.pi * TURNS)
F32 = jnp.float32
BF16 = jnp.bfloat16
TI = 256
TJ = 256
SUB = 16
LANE = 128

SIN_C = None
COS_C = None


def _fit(fn, odd, terms):
    import numpy as np

    nodes = 0.5 * np.cos(np.pi * (np.arange(400) + 0.5) / 400)
    cols = np.stack([nodes ** (2 * n + odd) for n in range(terms)], axis=1)
    coef = np.linalg.lstsq(cols, fn(nodes), rcond=None)[0]
    return [float(np.float32(c)) for c in coef]


def _tables():
    import numpy as np

    s = _fit(lambda t: math.sqrt(2.0) * np.sin(np.pi * t), 1, 5)
    c = _fit(lambda t: math.sqrt(2.0) * np.cos(np.pi * t), 0, 5)
    return s, c


SIN_C, COS_C = _tables()


def horner(coef, y):
    acc = coef[-1] * y + coef[-2]
    for c in coef[-3::-1]:
        acc = acc * y + c
    return acc


def hi_part(x):
    return x.astype(BF16).astype(F32)


def split3(x):
    one = hi_part(x)
    rest = x - one
    two = hi_part(rest)
    return one, two, rest - two


SPLIT_PAIRS = ((0, 0), (0, 1), (1, 0), (0, 2), (2, 0), (1, 1), (1, 2), (2, 1))


def rows8(x, n, a, b):
    return jnp.concatenate([x, n, a, b], axis=0)


def target_rows(geo, center):
    x = (geo[0:3] - center) * TURNS
    m = geo[3:6] * (1.0 / WAVENUM)
    ones = jnp.ones_like(x[0:1])
    xm = jnp.sum(x * m, axis=0, keepdims=True)
    return x, m, split3(rows8(x, m, ones, xm))


def target_table(adj, rows):
    hi = hi_part(adj)
    lo = adj - hi
    return jnp.concatenate([hi, hi, lo] + [rows[a] for a, _ in SPLIT_PAIRS], axis=0)


def source_rows(geo, center):
    x = (geo[0:3] - center) * TURNS
    n = geo[3:6]
    return x, n


def source_table(geo, fwd, x, n):
    area = geo[6:7]
    scaled = fwd * (area * PAIR_SCALE)
    re, im = scaled[0:32], scaled[32:64]
    real = jnp.concatenate([re, im], axis=0)
    imag = jnp.concatenate([im, -re], axis=0)
    rh, ih = hi_part(real), hi_part(imag)
    zero3 = jnp.zeros_like(x)
    zero1 = jnp.zeros_like(x[0:1])
    ones = jnp.ones_like(zero1)
    xn = jnp.sum(x * n, axis=0, keepdims=True)
    prow = split3(rows8(-n, zero3, xn, zero1))
    qrow = split3(rows8(zero3, -x, zero1, ones))
    zeros_w = jnp.zeros((192, x.shape[1]), F32)
    tail = jnp.zeros((64, x.shape[1]), F32)
    cols = [
        jnp.concatenate([rh, real - rh, rh, tail], axis=0),
        jnp.concatenate([ih, imag - ih, ih, tail], axis=0),
        jnp.concatenate([zeros_w] + [prow[b] for _, b in SPLIT_PAIRS], axis=0),
        jnp.concatenate([zeros_w] + [qrow[b] for _, b in SPLIT_PAIRS], axis=0),
    ]
    return cols


def pair_chunk(prod, xi, xj, area):
    wr, wi, pn, q = prod
    d0, d1, d2 = xi[0] - xj[0], xi[1] - xj[1], xi[2] - xj[2]
    r2 = (d0 * d0 + d1 * d1) + (d2 * d2 + area)
    rs = lax.rsqrt(r2)
    turns = r2 * rs
    t = turns - jnp.round(turns)
    v = rs * (1.0 / (2.0 * math.pi))
    y = t * t
    sv = (t * v) * horner(SIN_C, y)
    cv = v * horner(COS_C, y)
    es = sv * cv
    ec = v * v - sv * sv
    yr = ec * wr - es * wi
    yi = ec * wi + es * wr
    a = yi + v * yr
    b = yr - v * yi
    c = rs * ((q * yi - pn * yr) + (3.0 * v) * (pn * a + q * b))
    return a, b, c


def dot(a, b, dims=(((1,), (0,)), ((), ()))):
    return lax.dot_general(a, b, dims, preferred_element_type=F32)


def sum_splits(x):
    return x[0:8] + x[8:16] + x[16:24]


def pair_kernel(
    geo_a, geo_b, adj_a, adj_b, sgeo_a, sgeo_b, fwd_a, fwd_b, own_o, own_x, own_c, wt_o, wt_x, wt_c,
    out_ref,
    left, right, xi_ref, xj_ref, prod, abc, frow, fcol, tsum, ssum,
):
    width = geo_a.shape[1]
    total = 2 * width
    center = jnp.round(jnp.mean(geo_a[0:3], axis=1, keepdims=True))
    for part, (geo, adj) in enumerate(((geo_a, adj_a), (geo_b, adj_b))):
        cols = pl.ds(part * width, width)
        x, m, rows = target_rows(geo[...], center)
        left[cols, :] = target_table(adj[...], rows).T.astype(BF16)
        frow[:, cols] = jnp.concatenate(list(rows) + [jnp.zeros_like(rows[0])], axis=0).astype(BF16)
        xt = jnp.concatenate([x, m, m[0:2]], axis=0).T
        for k in range(3):
            xi_ref[k, cols, :] = jnp.broadcast_to(xt[:, k : k + 1], (width, LANE))
    for part, (geo, fwd) in enumerate(((sgeo_a, fwd_a), (sgeo_b, fwd_b))):
        cols = pl.ds(part * width, width)
        x, n = source_rows(geo[...], center)
        xj_ref[:, cols] = jnp.concatenate([x, geo[6:7] * (TURNS * TURNS)] * 2, axis=0)
        tab = source_table(geo[...], fwd[...], x, n)
        for k in range(4):
            right[k, :, cols] = tab[k].astype(BF16)
        ones = jnp.ones_like(x[0:1])
        rows = split3(rows8(x, n, ones, ones))
        frows = jnp.concatenate(list(rows) + [jnp.zeros_like(rows[0])], axis=0).astype(BF16)
        fcol[:, cols] = frows
    tsum[...] = jnp.zeros_like(tsum)
    ssum[...] = jnp.zeros_like(ssum)

    n_i, n_j = total // TI, total // TJ

    def tile(step, _):
        i0 = pl.multiple_of((step // n_j) * TI, TI)
        j0 = pl.multiple_of(lax.rem(step, n_j) * TJ, TJ)
        lhs = left[pl.ds(i0, TI), :]
        for k in range(4):
            prod[k] = dot(lhs, right[k, :, pl.ds(j0, TJ)])
        for jj in range(TJ // LANE):
            lanes = pl.ds(j0 + jj * LANE, LANE)
            xj = [xj_ref[k : k + 1, lanes] for k in range(4)]
            for ii in range(TI // SUB):
                rows = pl.ds(ii * SUB, SUB)
                xi = [xi_ref[k, pl.ds(i0 + ii * SUB, SUB), :] for k in range(3)]
                pr = [prod[k, rows, jj * LANE : (jj + 1) * LANE] for k in range(4)]
                for k, val in enumerate(pair_chunk(pr, xi, xj[0:3], xj[3])):
                    hi = val.astype(BF16)
                    abc[2 * k, rows, jj * LANE : (jj + 1) * LANE] = hi
                    abc[2 * k + 1, rows, jj * LANE : (jj + 1) * LANE] = (val - hi.astype(F32)).astype(BF16)
        fi = frow[:, pl.ds(i0, TI)]
        fj = fcol[:, pl.ds(j0, TJ)]
        for k in range(3):
            ssum[k, :, pl.ds(j0, TJ)] += dot(fi, abc[2 * k]) + dot(fi, abc[2 * k + 1])
            nt = (((1,), (1,)), ((), ()))
            tsum[k, :, pl.ds(i0, TI)] += dot(fj, abc[2 * k], nt) + dot(fj, abc[2 * k + 1], nt)
        return 0

    lax.fori_loop(0, n_i * n_j, tile, 0)

    tgt, src = [], []
    for part, (geo, sgeo) in enumerate(((geo_a, sgeo_a), (geo_b, sgeo_b))):
        cols = pl.ds(part * width, width)
        x = (geo[0:3] - center) * TURNS
        m = geo[3:6] * (1.0 / WAVENUM)
        sa, sb, sc = [sum_splits(tsum[k, :, cols]) for k in range(3)]
        gx = (2.0 * math.pi) * (x * sc[6:7] - sc[0:3]) + sa[3:6] - m * sb[6:7]
        gn = sb[0:3] - x * sb[6:7]
        tgt.append((gx * TURNS, gn * (1.0 / WAVENUM)))
        x = (sgeo[0:3] - center) * TURNS
        n = sgeo[3:6]
        sa, sb, sc = [sum_splits(ssum[k, :, cols]) for k in range(3)]
        gx = (2.0 * math.pi) * (x * sc[6:7] - sc[0:3]) - n * sa[6:7] + sb[3:6]
        gn = sa[0:3] - x * sa[6:7]
        src.append((gx * TURNS, gn))
    zero2 = jnp.zeros((2, width), F32)
    grads = [
        jnp.concatenate([tgt[0][0] + src[0][0], tgt[0][1] + src[0][1], zero2], axis=0),
        jnp.concatenate([tgt[1][0], tgt[1][1], zero2], axis=0),
        jnp.concatenate([src[1][0], src[1][1], zero2], axis=0),
    ]
    lhs = []
    for g in grads:
        hi = hi_part(g)
        lhs.append(jnp.concatenate([hi, g - hi], axis=0).astype(BF16))
    q_tile = 256
    owners = ((own_o, wt_o), (own_x, wt_x), (own_c, wt_c))

    def add_owner(step, _):
        q0 = pl.multiple_of(step * q_tile, q_tile)
        qs = q0 + lax.broadcasted_iota(jnp.int32, (q_tile, width), 0)
        acc = jnp.zeros((16, q_tile), F32)
        for g, (own, wt) in zip(lhs, owners):
            sel = jnp.zeros((q_tile, width), F32)
            for s in range(own.shape[0]):
                sel = sel + jnp.where(own[s : s + 1, :] == qs, wt[s : s + 1, :], 0.0)
            hi = sel.astype(BF16)
            lo = (sel - hi.astype(F32)).astype(BF16)
            nt = (((1,), (1,)), ((), ()))
            acc = acc + dot(g, hi, nt) + dot(g, lo, nt)
        out_ref[:, pl.ds(q0, q_tile)] = acc[0:8] + acc[8:16]
        return 0

    lax.fori_loop(0, out_ref.shape[1] // q_tile, add_owner, 0)


def pair_call(args, cp_total):
    width = args[0].shape[1]
    total = 2 * width
    return pl.pallas_call(
        pair_kernel,
        out_shape=jax.ShapeDtypeStruct((8, cp_total), F32),
        scratch_shapes=[
            pltpu.VMEM((total, 256), BF16),
            pltpu.VMEM((4, 256, total), BF16),
            pltpu.VMEM((3, total, LANE), F32),
            pltpu.VMEM((8, total), F32),
            pltpu.VMEM((4, TI, TJ), F32),
            pltpu.VMEM((6, TI, TJ), BF16),
            pltpu.VMEM((32, total), BF16),
            pltpu.VMEM((32, total), BF16),
            pltpu.VMEM((3, 32, total), F32),
            pltpu.VMEM((3, 32, total), F32),
        ],
        compiler_params=pltpu.CompilerParams(vmem_limit_bytes=48 * 1024 * 1024),
    )(*args)


def swap(x, axis, bit):
    size = lax.axis_size(axis)
    return lax.ppermute(x, axis, [(k, k ^ bit) for k in range(size)])


def halving(part, axes):
    cp_dev = part.shape[1]
    bits = []
    for axis in axes:
        size = lax.axis_size(axis)
        cp_dev //= size
        bits.append(size.bit_length() - 1)
    n_row, n_loop = bits
    cur = part[0:6].reshape([6] + [2] * (n_row + n_loop) + [cp_dev])
    order = list(range(n_row + n_loop, n_row, -1)) + list(range(n_row, 0, -1))
    cur = cur.transpose(order + [0, n_row + n_loop + 1]).reshape(-1, 6, cp_dev)
    steps = [("loop", 1 << b) for b in range(n_loop)] + [("row", 1 << b) for b in range(n_row)]
    for axis, bit in steps:
        half = cur.shape[0] // 2
        up = jnp.where((lax.axis_index(axis) & bit) > 0, 1, 0)
        keep = lax.dynamic_slice_in_dim(cur, up * half, half, 0)
        send = lax.dynamic_slice_in_dim(cur, (1 - up) * half, half, 0)
        cur = keep + swap(send, axis, bit)
    return cur[0]


def on_device(cp_dev, geometry, adjoint, forward, owner_map, owner_weight):
    cp_total = cp_dev * lax.axis_size("row") * lax.axis_size("loop")
    far = [swap(v, "loop", 2) for v in (adjoint, geometry, owner_map, owner_weight)]
    near = [swap(v, "loop", 1) for v in (forward, geometry, owner_map, owner_weight)]
    part = pair_call(
        (geometry, far[1], adjoint, far[0], geometry, near[1], forward, near[0],
         owner_map, far[2], near[2], owner_weight, far[3], near[3]),
        cp_total,
    )
    return halving(part, ("row", "loop"))


def solution(mesh):
    spec = P(None, ("parts", "row", "loop"))
    return jax.shard_map(
        functools.partial(on_device, 32), mesh=mesh, in_specs=(spec,) * 5, out_specs=spec, check_vma=False
    )
```

time: 210 us -> 49.9 us (0.24)
  waiting for transfers between devices: 76.3 us -> 10 us
  other arithmetic: 63 us -> 0.61 us
  local copies, waits for them, and re-layouts: 35.4 us -> 3.42 us
  Pallas kernels: 0 us -> 21.4 us
  blocking collectives: 14.2 us -> 0 us
  starting transfers between devices: 0.04 us -> 14 us
  between operations: 13.5 us -> 0.09 us
  matrix products: 6.89 us -> 0 us
    reduce_scatter x2 -> x0, waiting for transfers between devices: 76.3 us -> none  [the longest x1 55.5 us: on_device(): lax.psum_scatter(partial_cp, ('row', 'loop'), scatter_dimension=1, tiled=...]
    neg x2 -> x0, other arithmetic: 30.4 us -> none  [the longest x1 30.4 us: coupled_sum(): src_proj = -jnp.sum(offset * source_geo[3:6, None, :], axis=0) * inverse]
    pallas_call x0 -> x1, Pallas kernels: none -> 21.4 us  [pair_call(): pl.pallas_call(pair_kernel, out_shape=jax.ShapeDtypeStruct((8, cp_total),...]
    reduce_sum x2 -> x0, other arithmetic: 18.8 us -> none  [the longest x1 9.47 us: coupled_sum(): offset = target_geo[0:3, :, None] - source_geo[0:3, None, :]]
    reduce_sum x3 -> x0, local copies, waits for them, and re-layouts: 16.2 us -> none  [the longest x1 5.47 us: coupled_sum(): tgt_proj = jnp.sum(offset * target_geo[3:6, :, None], axis=0) * inverse]
    all_gather x2 -> x0, blocking collectives: 14.2 us -> none  [the longest x1 7.83 us: on_device(): lax.all_gather(adjoint, 'loop', axis=1, tiled=True)]
    ppermute x0 -> x12, starting transfers between devices: none -> 14 us  [swap(): return lax.ppermute(x, axis, [(k, k ^ bit) for k in range(size)])]
    scatter-add x1 -> x0, other arithmetic: 12.2 us -> none  [owner_add(): return totals.at[:, owners.reshape(-1)].add(flat)]
  transfers between devices with their start and end apart: 2 -> 12, of which waited for: 2 -> 7; matrix products, arithmetic and copies ran while one was open for 0% -> 0% of each run, Pallas kernels for 0% -> 0%
where the time goes in v1:
time: 49.9 us; the launch traced here: 49.6 us
  Pallas kernels  21.4 us (43%)
  starting transfers between devices  14 us (28%)
  waiting for transfers between devices  10 us (20%)
  local copies, waits for them, and re-layouts  3.42 us (7%)
  other arithmetic  0.61 us (1%)
    pallas_call x1, Pallas kernels, pair_call(): pl.pallas_call(pair_kernel, out_shape=jax.ShapeDtypeStruct((8, cp_total),...  21.4 us
    ppermute x12, starting transfers between devices, swap(): return lax.ppermute(x, axis, [(k, k ^ bit) for k in range(size)])  14 us
    ppermute x12, waiting for transfers between devices, swap(): return lax.ppermute(x, axis, [(k, k ^ bit) for k in range(size)])  10 us
    unnamed x10, local copies, waits for them, and re-layouts  3.2 us
  transfers between devices with their start and end apart: 12, of which 7 were waited for; matrix products, arithmetic and copies ran while one was open for 0% of the time, Pallas kernels for 0%

profile of v1, /device:TPU:0, one launch (start us, length us, event | category | flops | bytes accessed | tf_op | source)
XLA Modules:
  0.0 49.6 jit_solution(11151861112756599448)
XLA Ops:
  0.0 0.0 copy-start.2
  0.0 2.9 %collective-permute-start.1 = (f32[64,512]{1,0:T(8,128)}, f32[64,512]{1,0:T(8,128)S(1)}, u32[]{:S(2)}, u32[]{:S(2)}) collective-permute-start(f32[64,512]{1,0:T(8,128)} %adj_a.1), channel_id=1, source_target_pairs={{0,2},{1,3},{2,0},{3,1},{4,6},{5,7},{6,4},{7,5},{8,10},{9,11},{10,... | collective-permute-start | bytes 393224 | tf_op jit(solution)/shard_map/ppermute | solution.py:272
  2.9 0.0 collective-permute-start.3
  2.9 0.1 collective-permute-start.4
  3.1 0.4 collective-permute-start.5
  3.5 1.7 %collective-permute-start.6 = (f32[4,512]{1,0:T(4,128)}, f32[4,512]{1,0:T(4,128)S(1)}, u32[]{:S(2)}, u32[]{:S(2)}) collective-permute-start(f32[4,512]{1,0:T(4,128)} %wt_o.1), channel_id=1, source_target_pairs={{0,2},{1,3},{2,0},{3,1},{4,6},{5,7},{6,4},{7,5},{8,10},{9,11},{10,... | collective-permute-start | bytes 24584 | tf_op jit(solution)/shard_map/ppermute | solution.py:272
  5.2 1.7 %collective-permute-done.4.own_x = s32[4,512]{1,0:T(4,128)S(1)} collective-permute-done((s32[4,512]{1,0:T(4,128)}, s32[4,512]{1,0:T(4,128)S(1)}, u32[]{:S(2)}, u32[]{:S(2)}) %collective-permute-start.4) | collective-permute-done | bytes 8224 | tf_op jit(solution)/shard_map/ppermute | solution.py:272
  6.9 1.7 %collective-permute-start = (f32[7,512]{1,0:T(8,128)}, f32[7,512]{1,0:T(8,128)S(1)}, u32[]{:S(2)}, u32[]{:S(2)}) collective-permute-start(f32[7,512]{1,0:T(8,128)} %sgeo_a.1), channel_id=1, source_target_pairs={{0,2},{1,3},{2,0},{3,1},{4,6},{5,7},{6,4},{7,5},{8,10},{9,11},{10,... | collective-permute-start | bytes 43016 | tf_op jit(solution)/shard_map/ppermute | solution.py:272
  8.7 0.0 collective-permute-done.5.own_c
  8.7 0.0 collective-permute-start.2
  8.7 0.0 collective-permute-done.6.wt_x
  8.7 0.5 %collective-permute-start.7 = (f32[4,512]{1,0:T(4,128)}, f32[4,512]{1,0:T(4,128)S(1)}, u32[]{:S(2)}, u32[]{:S(2)}) collective-permute-start(f32[4,512]{1,0:T(4,128)} %wt_o.1), channel_id=1, source_target_pairs={{0,1},{1,0},{2,3},{3,2},{4,5},{5,4},{6,7},{7,6},{8,9},{9,8},{10,11... | collective-permute-start | bytes 24584 | tf_op jit(solution)/shard_map/ppermute | solution.py:272
  9.2 1.0 %collective-permute-done.7.wt_c = f32[4,512]{1,0:T(4,128)S(1)} collective-permute-done((f32[4,512]{1,0:T(4,128)}, f32[4,512]{1,0:T(4,128)S(1)}, u32[]{:S(2)}, u32[]{:S(2)}) %collective-permute-start.7) | collective-permute-done | bytes 8224 | tf_op jit(solution)/shard_map/ppermute | solution.py:272
  10.2 0.6 %collective-permute-done.geo_b = f32[7,512]{1,0:T(8,128)S(1)} collective-permute-done((f32[7,512]{1,0:T(8,128)}, f32[7,512]{1,0:T(8,128)S(1)}, u32[]{:S(2)}, u32[]{:S(2)}) %collective-permute-start) | collective-permute-done | bytes 14368 | tf_op jit(solution)/shard_map/ppermute | solution.py:272
  10.9 0.0 collective-permute-done.2.sgeo_b
  10.9 0.0 collective-permute-done.1.adj_b
  10.9 0.0 collective-permute-done.3.fwd_b
  10.9 0.0 copy-done.2
  10.9 0.0 copy-start
  10.9 0.9 %copy-done = f32[64,512]{1,0:T(8,128)S(1)} copy-done((f32[64,512]{1,0:T(8,128)S(1)}, f32[64,512]{1,0:T(8,128)}, u32[]{:S(2)}) %copy-start) | copy-done | bytes 131096
  11.8 0.0 copy-start.1
  11.8 0.9 %copy-done.1 = f32[64,512]{1,0:T(8,128)S(1)} copy-done((f32[64,512]{1,0:T(8,128)S(1)}, f32[64,512]{1,0:T(8,128)}, u32[]{:S(2)}) %copy-start.1) | copy-done | bytes 131096
  12.7 0.0 copy-start.3
  12.7 0.7 %copy-done.3 = s32[4,512]{1,0:T(4,128)S(1)} copy-done((s32[4,512]{1,0:T(4,128)S(1)}, s32[4,512]{1,0:T(4,128)}, u32[]{:S(2)}) %copy-start.3) | copy-done | bytes 8216
  13.4 0.0 copy-start.4
  13.4 0.7 %copy-done.4 = f32[4,512]{1,0:T(4,128)S(1)} copy-done((f32[4,512]{1,0:T(4,128)S(1)}, f32[4,512]{1,0:T(4,128)}, u32[]{:S(2)}) %copy-start.4) | copy-done | bytes 8216
  14.1 21.4 %shard_map.55 = f32[8,512]{1,0:T(8,128)S(1)} custom-call(f32[7,512]{1,0:T(8,128)S(1)} %copy-done.2, f32[7,512]{1,0:T(8,128)S(1)} %collective-permute-done.geo_b, f32[64,512]{1,0:T(8,128)S(1)} %copy-done, f32[64,512]{1,0:T(8,128)S(1)} %collective-permute-done.1.adj_b, f32[7,512]{1,0:T(8,128)S(1)} %copy-done.2, f32[7,512]{1,0:T(8,128)S(1)} %collective-permute-done.2.sgeo_b, ...), custom_call_target="tpu_custom_call" | custom-call | tf_op jit(solution)/shard_map/pallas_call | solution.py:251
  35.5 0.2 reshape.6
  35.7 0.1 collective-permute-start.8
  35.8 1.2 %collective-permute-done.8 = f32[8,6,32]{2,1,0:T(8,128)S(1)} collective-permute-done((f32[8,6,32]{2,1,0:T(8,128)S(1)}, f32[8,6,32]{2,1,0:T(8,128)S(1)}, u32[]{:S(2)}, u32[]{:S(2)}) %collective-permute-start.8) | collective-permute-done | bytes 6176 | tf_op jit(solution)/shard_map/ppermute | solution.py:272
  37.0 1.8 %collective-permute-start.9 = (f32[4,6,32]{2,1,0:T(8,128)S(1)}, f32[4,6,32]{2,1,0:T(8,128)S(1)}, u32[]{:S(2)}, u32[]{:S(2)}) collective-permute-start(f32[4,6,32]{2,1,0:T(8,128)S(1)} %constant_dynamic-slice_fusion.2), channel_id=1, source_target_pairs={{0,2},{1,3},{2,0},{3,1},{4,6},{5,7},{6,4},{7,5},{8,10},{9,11},{10,... | collective-permute-start | bytes 9224 | tf_op jit(solution)/shard_map/ppermute | solution.py:272
  38.8 2.0 %collective-permute-done.9 = f32[4,6,32]{2,1,0:T(8,128)S(1)} collective-permute-done((f32[4,6,32]{2,1,0:T(8,128)S(1)}, f32[4,6,32]{2,1,0:T(8,128)S(1)}, u32[]{:S(2)}, u32[]{:S(2)}) %collective-permute-start.9) | collective-permute-done | bytes 3104 | tf_op jit(solution)/shard_map/ppermute | solution.py:272
  40.8 1.8 %collective-permute-start.10 = (f32[2,6,32]{2,1,0:T(8,128)S(1)}, f32[2,6,32]{2,1,0:T(8,128)S(1)}, u32[]{:S(2)}, u32[]{:S(2)}) collective-permute-start(f32[2,6,32]{2,1,0:T(8,128)S(1)} %constant_dynamic-slice_fusion.1), channel_id=1, source_target_pairs={{0,4},{4,0},{8,12},{12,8},{1,5},{5,1},{9,13},{13,9},{2,6},{6,2},{1... | collective-permute-start | bytes 4616 | tf_op jit(solution)/shard_map/ppermute | solution.py:272
  42.7 1.8 %collective-permute-done.10 = f32[2,6,32]{2,1,0:T(8,128)S(1)} collective-permute-done((f32[2,6,32]{2,1,0:T(8,128)S(1)}, f32[2,6,32]{2,1,0:T(8,128)S(1)}, u32[]{:S(2)}, u32[]{:S(2)}) %collective-permute-start.10) | collective-permute-done | bytes 1568 | tf_op jit(solution)/shard_map/ppermute | solution.py:272
  44.5 2.9 %collective-permute-start.11 = (f32[1,6,32]{2,1,0:T(8,128)S(1)}, f32[1,6,32]{2,1,0:T(8,128)S(1)}, u32[]{:S(2)}, u32[]{:S(2)}) collective-permute-start(f32[1,6,32]{2,1,0:T(8,128)S(1)} %constant_dynamic-slice_fusion), channel_id=1, source_target_pairs={{0,8},{4,12},{8,0},{12,4},{1,9},{5,13},{9,1},{13,5},{2,10},{6,14},... | collective-permute-start | bytes 2312 | tf_op jit(solution)/shard_map/ppermute | solution.py:272
  47.4 1.7 %collective-permute-done.11 = f32[1,6,32]{2,1,0:T(8,128)S(1)} collective-permute-done((f32[1,6,32]{2,1,0:T(8,128)S(1)}, f32[1,6,32]{2,1,0:T(8,128)S(1)}, u32[]{:S(2)}, u32[]{:S(2)}) %collective-permute-start.11) | collective-permute-done | bytes 800 | tf_op jit(solution)/shard_map/ppermute | solution.py:272
  49.0 0.6 %add_bitcast_fusion = f32[6,32]{1,0:T(8,128)} fusion(f32[1,6,32]{2,1,0:T(8,128)S(1)} %collective-permute-done.11, f32[2,6,32]{2,1,0:T(8,128)S(1)} %dynamic-slice_add_fusion.2, s32[]{:T(128)S(6)} %select_n.44), kind=kLoop, calls=%fused_computation.3 | loop fusion | flops 192 | bytes 2308 | tf_op jit(solution)/shard_map/squeeze | solution.py:293
  (8 shorter events, 0.1 us)
Async XLA Ops:
  0.0 10.9 %copy-start.2 = (f32[7,512]{1,0:T(8,128)S(1)}, f32[7,512]{1,0:T(8,128)}, u32[]{:S(2)}) copy-start(f32[7,512]{1,0:T(8,128)} %sgeo_a.1) | copy-start | bytes 43012
  0.0 10.9 %collective-permute-start.1 = (f32[64,512]{1,0:T(8,128)}, f32[64,512]{1,0:T(8,128)S(1)}, u32[]{:S(2)}, u32[]{:S(2)}) collective-permute-start(f32[64,512]{1,0:T(8,128)} %adj_a.1), channel_id=1, source_target_pairs={{0,2},{1,3},{2,0},{3,1},{4,6},{5,7},{6,4},{7,5},{8,10},{9,11},{10,... | collective-permute-start | bytes 393224 | tf_op jit(solution)/shard_map/ppermute | solution.py:272
  2.9 7.9 %collective-permute-start.3 = (f32[64,512]{1,0:T(8,128)}, f32[64,512]{1,0:T(8,128)S(1)}, u32[]{:S(2)}, u32[]{:S(2)}) collective-permute-start(f32[64,512]{1,0:T(8,128)} %fwd_a.1), channel_id=1, source_target_pairs={{0,1},{1,0},{2,3},{3,2},{4,5},{5,4},{6,7},{7,6},{8,9},{9,8},{10,11... | collective-permute-start | bytes 393224 | tf_op jit(solution)/shard_map/ppermute | solution.py:272
  2.9 4.0 %collective-permute-start.4 = (s32[4,512]{1,0:T(4,128)}, s32[4,512]{1,0:T(4,128)S(1)}, u32[]{:S(2)}, u32[]{:S(2)}) collective-permute-start(s32[4,512]{1,0:T(4,128)} %own_o.1), channel_id=1, source_target_pairs={{0,2},{1,3},{2,0},{3,1},{4,6},{5,7},{6,4},{7,5},{8,10},{9,11},{10,... | collective-permute-start | bytes 24584 | tf_op jit(solution)/shard_map/ppermute | solution.py:272
  3.1 5.6 %collective-permute-start.5 = (s32[4,512]{1,0:T(4,128)}, s32[4,512]{1,0:T(4,128)S(1)}, u32[]{:S(2)}, u32[]{:S(2)}) collective-permute-start(s32[4,512]{1,0:T(4,128)} %own_o.1), channel_id=1, source_target_pairs={{0,1},{1,0},{2,3},{3,2},{4,5},{5,4},{6,7},{7,6},{8,9},{9,8},{10,11... | collective-permute-start | bytes 24584 | tf_op jit(solution)/shard_map/ppermute | solution.py:272
  3.5 5.2 %collective-permute-start.6 = (f32[4,512]{1,0:T(4,128)}, f32[4,512]{1,0:T(4,128)S(1)}, u32[]{:S(2)}, u32[]{:S(2)}) collective-permute-start(f32[4,512]{1,0:T(4,128)} %wt_o.1), channel_id=1, source_target_pairs={{0,2},{1,3},{2,0},{3,1},{4,6},{5,7},{6,4},{7,5},{8,10},{9,11},{10,... | collective-permute-start | bytes 24584 | tf_op jit(solution)/shard_map/ppermute | solution.py:272
  6.9 3.9 %collective-permute-start = (f32[7,512]{1,0:T(8,128)}, f32[7,512]{1,0:T(8,128)S(1)}, u32[]{:S(2)}, u32[]{:S(2)}) collective-permute-start(f32[7,512]{1,0:T(8,128)} %sgeo_a.1), channel_id=1, source_target_pairs={{0,2},{1,3},{2,0},{3,1},{4,6},{5,7},{6,4},{7,5},{8,10},{9,11},{10,... | collective-permute-start | bytes 43016 | tf_op jit(solution)/shard_map/ppermute | solution.py:272
  8.7 2.2 %collective-permute-start.2 = (f32[7,512]{1,0:T(8,128)}, f32[7,512]{1,0:T(8,128)S(1)}, u32[]{:S(2)}, u32[]{:S(2)}) collective-permute-start(f32[7,512]{1,0:T(8,128)} %sgeo_a.1), channel_id=1, source_target_pairs={{0,1},{1,0},{2,3},{3,2},{4,5},{5,4},{6,7},{7,6},{8,9},{9,8},{10,11... | collective-permute-start | bytes 43016 | tf_op jit(solution)/shard_map/ppermute | solution.py:272
  8.7 1.5 %collective-permute-start.7 = (f32[4,512]{1,0:T(4,128)}, f32[4,512]{1,0:T(4,128)S(1)}, u32[]{:S(2)}, u32[]{:S(2)}) collective-permute-start(f32[4,512]{1,0:T(4,128)} %wt_o.1), channel_id=1, source_target_pairs={{0,1},{1,0},{2,3},{3,2},{4,5},{5,4},{6,7},{7,6},{8,9},{9,8},{10,11... | collective-permute-start | bytes 24584 | tf_op jit(solution)/shard_map/ppermute | solution.py:272
  10.9 0.9 %copy-start = (f32[64,512]{1,0:T(8,128)S(1)}, f32[64,512]{1,0:T(8,128)}, u32[]{:S(2)}) copy-start(f32[64,512]{1,0:T(8,128)} %adj_a.1) | copy-start | bytes 393220
  11.8 0.9 %copy-start.1 = (f32[64,512]{1,0:T(8,128)S(1)}, f32[64,512]{1,0:T(8,128)}, u32[]{:S(2)}) copy-start(f32[64,512]{1,0:T(8,128)} %fwd_a.1) | copy-start | bytes 393220
  12.7 0.7 %copy-start.3 = (s32[4,512]{1,0:T(4,128)S(1)}, s32[4,512]{1,0:T(4,128)}, u32[]{:S(2)}) copy-start(s32[4,512]{1,0:T(4,128)} %own_o.1) | copy-start | bytes 24580
  13.4 0.7 %copy-start.4 = (f32[4,512]{1,0:T(4,128)S(1)}, f32[4,512]{1,0:T(4,128)}, u32[]{:S(2)}) copy-start(f32[4,512]{1,0:T(4,128)} %wt_o.1) | copy-start | bytes 24580
  35.7 1.3 %collective-permute-start.8 = (f32[8,6,32]{2,1,0:T(8,128)S(1)}, f32[8,6,32]{2,1,0:T(8,128)S(1)}, u32[]{:S(2)}, u32[]{:S(2)}) collective-permute-start(f32[8,6,32]{2,1,0:T(8,128)S(1)} %constant_dynamic-slice_fusion.3), channel_id=1, source_target_pairs={{0,1},{1,0},{2,3},{3,2},{4,5},{5,4},{6,7},{7,6},{8,9},{9,8},{10,11... | collective-permute-start | bytes 18440 | tf_op jit(solution)/shard_map/ppermute | solution.py:272
  37.0 3.8 %collective-permute-start.9 = (f32[4,6,32]{2,1,0:T(8,128)S(1)}, f32[4,6,32]{2,1,0:T(8,128)S(1)}, u32[]{:S(2)}, u32[]{:S(2)}) collective-permute-start(f32[4,6,32]{2,1,0:T(8,128)S(1)} %constant_dynamic-slice_fusion.2), channel_id=1, source_target_pairs={{0,2},{1,3},{2,0},{3,1},{4,6},{5,7},{6,4},{7,5},{8,10},{9,11},{10,... | collective-permute-start | bytes 9224 | tf_op jit(solution)/shard_map/ppermute | solution.py:272
  40.8 3.7 %collective-permute-start.10 = (f32[2,6,32]{2,1,0:T(8,128)S(1)}, f32[2,6,32]{2,1,0:T(8,128)S(1)}, u32[]{:S(2)}, u32[]{:S(2)}) collective-permute-start(f32[2,6,32]{2,1,0:T(8,128)S(1)} %constant_dynamic-slice_fusion.1), channel_id=1, source_target_pairs={{0,4},{4,0},{8,12},{12,8},{1,5},{5,1},{9,13},{13,9},{2,6},{6,2},{1... | collective-permute-start | bytes 4616 | tf_op jit(solution)/shard_map/ppermute | solution.py:272
  44.5 4.5 %collective-permute-start.11 = (f32[1,6,32]{2,1,0:T(8,128)S(1)}, f32[1,6,32]{2,1,0:T(8,128)S(1)}, u32[]{:S(2)}, u32[]{:S(2)}) collective-permute-start(f32[1,6,32]{2,1,0:T(8,128)S(1)} %constant_dynamic-slice_fusion), channel_id=1, source_target_pairs={{0,8},{4,12},{8,0},{12,4},{1,9},{5,13},{9,1},{13,5},{2,10},{6,14},... | collective-permute-start | bytes 2312 | tf_op jit(solution)/shard_map/ppermute | solution.py:272

commit v2 on v1

--- a/solution.py
+++ b/solution.py
@@ -140,130 +140,236 @@
     return x[0:8] + x[8:16] + x[16:24]
 
 
-def pair_kernel(
-    geo_a, geo_b, adj_a, adj_b, sgeo_a, sgeo_b, fwd_a, fwd_b, own_o, own_x, own_c, wt_o, wt_x, wt_c,
-    out_ref,
-    left, right, xi_ref, xj_ref, prod, abc, frow, fcol, tsum, ssum,
-):
-    width = geo_a.shape[1]
-    total = 2 * width
-    center = jnp.round(jnp.mean(geo_a[0:3], axis=1, keepdims=True))
-    for part, (geo, adj) in enumerate(((geo_a, adj_a), (geo_b, adj_b))):
-        cols = pl.ds(part * width, width)
-        x, m, rows = target_rows(geo[...], center)
-        left[cols, :] = target_table(adj[...], rows).T.astype(BF16)
-        frow[:, cols] = jnp.concatenate(list(rows) + [jnp.zeros_like(rows[0])], axis=0).astype(BF16)
-        xt = jnp.concatenate([x, m, m[0:2]], axis=0).T
-        for k in range(3):
-            xi_ref[k, cols, :] = jnp.broadcast_to(xt[:, k : k + 1], (width, LANE))
-    for part, (geo, fwd) in enumerate(((sgeo_a, fwd_a), (sgeo_b, fwd_b))):
-        cols = pl.ds(part * width, width)
-        x, n = source_rows(geo[...], center)
-        xj_ref[:, cols] = jnp.concatenate([x, geo[6:7] * (TURNS * TURNS)] * 2, axis=0)
-        tab = source_table(geo[...], fwd[...], x, n)
-        for k in range(4):
-            right[k, :, cols] = tab[k].astype(BF16)
-        ones = jnp.ones_like(x[0:1])
-        rows = split3(rows8(x, n, ones, ones))
-        frows = jnp.concatenate(list(rows) + [jnp.zeros_like(rows[0])], axis=0).astype(BF16)
-        fcol[:, cols] = frows
-    tsum[...] = jnp.zeros_like(tsum)
-    ssum[...] = jnp.zeros_like(ssum)
-
-    n_i, n_j = total // TI, total // TJ
-
-    def tile(step, _):
-        i0 = pl.multiple_of((step // n_j) * TI, TI)
-        j0 = pl.multiple_of(lax.rem(step, n_j) * TJ, TJ)
+NT = (((1,), (1,)), ((), ()))
+
+
+def build_targets(geo, adj, center, cols, left, xi_ref, frow):
+    x, m, rows = target_rows(geo, center)
+    left[cols, :] = target_table(adj, rows).T.astype(BF16)
+    frow[:, cols] = jnp.concatenate(list(rows) + [jnp.zeros_like(rows[0])], axis=0).astype(BF16)
+    xt = jnp.concatenate([x, m, m[0:2]], axis=0).T
+    for k in range(3):
+        xi_ref[k, cols, :] = jnp.broadcast_to(xt[:, k : k + 1], (x.shape[1], LANE))
+
+
+def build_sources(geo, fwd, center, cols, right, xj_ref, fcol):
+    x, n = source_rows(geo, center)
+    xj_ref[:, cols] = jnp.concatenate([x, geo[6:7] * (TURNS * TURNS)] * 2, axis=0)
+    tab = source_table(geo, fwd, x, n)
+    for k in range(4):
+        right[k, :, cols] = tab[k].astype(BF16)
+    ones = jnp.ones_like(x[0:1])
+    rows = split3(rows8(x, n, ones, ones))
+    fcol[:, cols] = jnp.concatenate(list(rows) + [jnp.zeros_like(rows[0])], axis=0).astype(BF16)
+
+
+def center_of(geo):
+    return jnp.round(jnp.mean(geo[0:3], axis=1, keepdims=True))
+
+
+def run_tiles(count, place, left, right, xi_ref, xj_ref, frow, fcol, prod, abc, tsum, ssum):
+    def start(t):
+        i0, j0 = place(t)
+        return pl.multiple_of(i0, TI), pl.multiple_of(j0, TJ)
+
+    def products(t, slot):
+        i0, j0 = start(t)
         lhs = left[pl.ds(i0, TI), :]
         for k in range(4):
-            prod[k] = dot(lhs, right[k, :, pl.ds(j0, TJ)])
+            prod[slot, k] = dot(lhs, right[k, :, pl.ds(j0, TJ)])
+
+    def values(t, slot):
+        i0, j0 = start(t)
         for jj in range(TJ // LANE):
             lanes = pl.ds(j0 + jj * LANE, LANE)
+            here = slice(jj * LANE, (jj + 1) * LANE)
             xj = [xj_ref[k : k + 1, lanes] for k in range(4)]
             for ii in range(TI // SUB):
                 rows = pl.ds(ii * SUB, SUB)
                 xi = [xi_ref[k, pl.ds(i0 + ii * SUB, SUB), :] for k in range(3)]
-                pr = [prod[k, rows, jj * LANE : (jj + 1) * LANE] for k in range(4)]
+                pr = [prod[slot, k, rows, here] for k in range(4)]
                 for k, val in enumerate(pair_chunk(pr, xi, xj[0:3], xj[3])):
                     hi = val.astype(BF16)
-                    abc[2 * k, rows, jj * LANE : (jj + 1) * LANE] = hi
-                    abc[2 * k + 1, rows, jj * LANE : (jj + 1) * LANE] = (val - hi.astype(F32)).astype(BF16)
+                    abc[slot, 2 * k, rows, here] = hi
+                    abc[slot, 2 * k + 1, rows, here] = (val - hi.astype(F32)).astype(BF16)
+
+    def sums(t, slot):
+        i0, j0 = start(t)
         fi = frow[:, pl.ds(i0, TI)]
         fj = fcol[:, pl.ds(j0, TJ)]
         for k in range(3):
-            ssum[k, :, pl.ds(j0, TJ)] += dot(fi, abc[2 * k]) + dot(fi, abc[2 * k + 1])
-            nt = (((1,), (1,)), ((), ()))
-            tsum[k, :, pl.ds(i0, TI)] += dot(fj, abc[2 * k], nt) + dot(fj, abc[2 * k + 1], nt)
+            ssum[k, :, pl.ds(j0, TJ)] += dot(fi, abc[slot, 2 * k]) + dot(fi, abc[slot, 2 * k + 1])
+            tsum[k, :, pl.ds(i0, TI)] += dot(fj, abc[slot, 2 * k], NT) + dot(fj, abc[slot, 2 * k + 1], NT)
+
+    last = count - 1
+    products(0, 0)
+    abc[1] = jnp.zeros_like(abc[1])
+
+    def double(u, _):
+        t = 2 * u
+        products(t + 1, 1)
+        values(t, 0)
+        sums(jnp.maximum(t - 1, 0), 1)
+        products(jnp.minimum(t + 2, last), 0)
+        values(t + 1, 1)
+        sums(t, 0)
         return 0
 
-    lax.fori_loop(0, n_i * n_j, tile, 0)
-
-    tgt, src = [], []
-    for part, (geo, sgeo) in enumerate(((geo_a, sgeo_a), (geo_b, sgeo_b))):
-        cols = pl.ds(part * width, width)
-        x = (geo[0:3] - center) * TURNS
-        m = geo[3:6] * (1.0 / WAVENUM)
+    lax.fori_loop(0, count // 2, double, 0)
+    sums(last, 1)
+
+
+def own_kernel(geo, adj, fwd, left, right, xi_ref, tsum, ssum, xj_ref, frow, fcol, prod, abc):
+    width = geo.shape[1]
+    center = center_of(geo)
+    cols = pl.ds(0, width)
+    build_targets(geo[...], adj[...], center, cols, left, xi_ref, frow)
+    build_sources(geo[...], fwd[...], center, cols, right, xj_ref, fcol)
+    tsum[...] = jnp.zeros_like(tsum)
+    ssum[...] = jnp.zeros_like(ssum)
+    n_j = width // TJ
+    run_tiles(
+        (width // TI) * n_j, lambda t: ((t // n_j) * TI, lax.rem(t, n_j) * TJ),
+        left, right, xi_ref, xj_ref, frow, fcol, prod, abc, tsum, ssum,
+    )
+
+
+def sum_splits(x):
+    return x[0:8] + x[8:16] + x[16:24]
+
+
+def rest_kernel(
+    geo, far, near, own, wt, left_o, right_o, xi_o, tsum_o, ssum_o,
+    out_ref,
+    left, right, xi_ref, xj_ref, frow, fcol, prod, abc, tsum, ssum,
+):
+    width = geo.shape[1]
+    center = center_of(geo)
+    first, second = pl.ds(0, width), pl.ds(width, width)
+    left[first, :] = left_o[...]
+    right[:, :, first] = right_o[...]
+    xi_ref[:, first, :] = xi_o[...]
+    x, m, rows = target_rows(geo[...], center)
+    frow[:, first] = jnp.concatenate(list(rows) + [jnp.zeros_like(rows[0])], axis=0).astype(BF16)
+    ones = jnp.ones_like(x[0:1])
+    rows = split3(rows8(x, geo[3:6], ones, ones))
+    fcol[:, first] = jnp.concatenate(list(rows) + [jnp.zeros_like(rows[0])], axis=0).astype(BF16)
+    xj_ref[:, first] = jnp.concatenate([x, geo[6:7] * (TURNS * TURNS)] * 2, axis=0)
+    tsum[:, :, first] = tsum_o[...]
+    ssum[:, :, first] = ssum_o[...]
+    tsum[:, :, second] = jnp.zeros_like(tsum_o)
+    ssum[:, :, second] = jnp.zeros_like(ssum_o)
+    build_targets(far[64:71], far[0:64], center, second, left, xi_ref, frow)
+    build_sources(near[64:71], near[0:64], center, second, right, xj_ref, fcol)
+
+    n_i, n_j = width // TI, width // TJ
+    block = n_i * n_j
+
+    def place(t):
+        b = t // block
+        inner = lax.rem(t, block)
+        i0 = jnp.where(b > 0, width, 0) + (inner // n_j) * TI
+        j0 = jnp.where(b == 1, 0, width) + lax.rem(inner, n_j) * TJ
+        return i0, j0
+
+    run_tiles(3 * block, place, left, right, xi_ref, xj_ref, frow, fcol, prod, abc, tsum, ssum)
+
+    def target_grad(g, cols):
+        x = (g[0:3] - center) * TURNS
+        m = g[3:6] * (1.0 / WAVENUM)
         sa, sb, sc = [sum_splits(tsum[k, :, cols]) for k in range(3)]
         gx = (2.0 * math.pi) * (x * sc[6:7] - sc[0:3]) + sa[3:6] - m * sb[6:7]
         gn = sb[0:3] - x * sb[6:7]
-        tgt.append((gx * TURNS, gn * (1.0 / WAVENUM)))
-        x = (sgeo[0:3] - center) * TURNS
-        n = sgeo[3:6]
+        return gx * TURNS, gn * (1.0 / WAVENUM)
+
+    def source_grad(g, cols):
+        x = (g[0:3] - center) * TURNS
+        n = g[3:6]
         sa, sb, sc = [sum_splits(ssum[k, :, cols]) for k in range(3)]
         gx = (2.0 * math.pi) * (x * sc[6:7] - sc[0:3]) - n * sa[6:7] + sb[3:6]
         gn = sa[0:3] - x * sa[6:7]
-        src.append((gx * TURNS, gn))
+        return gx * TURNS, gn
+
+    t_own, s_own = target_grad(geo, first), source_grad(geo, first)
     zero2 = jnp.zeros((2, width), F32)
     grads = [
-        jnp.concatenate([tgt[0][0] + src[0][0], tgt[0][1] + src[0][1], zero2], axis=0),
-        jnp.concatenate([tgt[1][0], tgt[1][1], zero2], axis=0),
-        jnp.concatenate([src[1][0], src[1][1], zero2], axis=0),
+        (t_own[0] + s_own[0], t_own[1] + s_own[1]),
+        target_grad(far[64:71], second),
+        source_grad(near[64:71], second),
     ]
     lhs = []
-    for g in grads:
+    for gx, gn in grads:
+        g = jnp.concatenate([gx, gn, zero2], axis=0)
         hi = hi_part(g)
         lhs.append(jnp.concatenate([hi, g - hi], axis=0).astype(BF16))
     q_tile = 256
-    owners = ((own_o, wt_o), (own_x, wt_x), (own_c, wt_c))
+    owners = (
+        (own[...].astype(F32), wt[...]), (far[76:80], far[72:76]), (near[76:80], near[72:76])
+    )
 
     def add_owner(step, _):
         q0 = pl.multiple_of(step * q_tile, q_tile)
-        qs = q0 + lax.broadcasted_iota(jnp.int32, (q_tile, width), 0)
+        qs = (q0 + lax.broadcasted_iota(jnp.int32, (q_tile, width), 0)).astype(F32)
         acc = jnp.zeros((16, q_tile), F32)
-        for g, (own, wt) in zip(lhs, owners):
+        for g, (who, weight) in zip(lhs, owners):
             sel = jnp.zeros((q_tile, width), F32)
-            for s in range(own.shape[0]):
-                sel = sel + jnp.where(own[s : s + 1, :] == qs, wt[s : s + 1, :], 0.0)
+            for s in range(4):
+                sel = sel + jnp.where(who[s : s + 1, :] == qs, weight[s : s + 1, :], 0.0)
             hi = sel.astype(BF16)
             lo = (sel - hi.astype(F32)).astype(BF16)
-            nt = (((1,), (1,)), ((), ()))
-            acc = acc + dot(g, hi, nt) + dot(g, lo, nt)
+            acc = acc + dot(g, hi, NT) + dot(g, lo, NT)
         out_ref[:, pl.ds(q0, q_tile)] = acc[0:8] + acc[8:16]
         return 0
 
     lax.fori_loop(0, out_ref.shape[1] // q_tile, add_owner, 0)
 
 
-def pair_call(args, cp_total):
+def shape(dims, kind):
+    return jax.ShapeDtypeStruct(dims, kind)
+
+
+def tile_scratch():
+    return [pltpu.VMEM((2, 4, TI, TJ), F32), pltpu.VMEM((2, 6, TI, TJ), BF16)]
+
+
+PARAMS = pltpu.CompilerParams(vmem_limit_bytes=40 * 1024 * 1024)
+
+
+def own_call(geo, adj, fwd):
+    width = geo.shape[1]
+    return pl.pallas_call(
+        own_kernel,
+        out_shape=[
+            shape((width, 256), BF16), shape((4, 256, width), BF16), shape((3, width, LANE), F32),
+            shape((3, 32, width), F32), shape((3, 32, width), F32),
+        ],
+        scratch_shapes=[pltpu.VMEM((8, width), F32), pltpu.VMEM((32, width), BF16), pltpu.VMEM((32, width), BF16)]
+        + tile_scratch(),
+        compiler_params=PARAMS,
+        cost_estimate=pl.CostEstimate(flops=4 * 10**9, bytes_accessed=4 * 10**6, transcendentals=0),
+        name="own",
+    )(geo, adj, fwd)
+
+
+def rest_call(args, cp_total):
     width = args[0].shape[1]
     total = 2 * width
     return pl.pallas_call(
-        pair_kernel,
-        out_shape=jax.ShapeDtypeStruct((8, cp_total), F32),
+        rest_kernel,
+        out_shape=shape((8, cp_total), F32),
         scratch_shapes=[
             pltpu.VMEM((total, 256), BF16),
             pltpu.VMEM((4, 256, total), BF16),
             pltpu.VMEM((3, total, LANE), F32),
             pltpu.VMEM((8, total), F32),
-            pltpu.VMEM((4, TI, TJ), F32),
-            pltpu.VMEM((6, TI, TJ), BF16),
             pltpu.VMEM((32, total), BF16),
             pltpu.VMEM((32, total), BF16),
-            pltpu.VMEM((3, 32, total), F32),
-            pltpu.VMEM((3, 32, total), F32),
-        ],
-        compiler_params=pltpu.CompilerParams(vmem_limit_bytes=48 * 1024 * 1024),
+        ]
+        + tile_scratch()
+        + [pltpu.VMEM((3, 32, total), F32), pltpu.VMEM((3, 32, total), F32)],
+        compiler_params=PARAMS,
+        cost_estimate=pl.CostEstimate(flops=12 * 10**9, bytes_accessed=4 * 10**6, transcendentals=0),
+        name="rest",
     )(*args)
 
 
@@ -295,13 +401,11 @@
 
 def on_device(cp_dev, geometry, adjoint, forward, owner_map, owner_weight):
     cp_total = cp_dev * lax.axis_size("row") * lax.axis_size("loop")
-    far = [swap(v, "loop", 2) for v in (adjoint, geometry, owner_map, owner_weight)]
-    near = [swap(v, "loop", 1) for v in (forward, geometry, owner_map, owner_weight)]
-    part = pair_call(
-        (geometry, far[1], adjoint, far[0], geometry, near[1], forward, near[0],
-         owner_map, far[2], near[2], owner_weight, far[3], near[3]),
-        cp_total,
-    )
+    tail = [geometry, jnp.zeros_like(owner_weight[0:1]), owner_weight, owner_map.astype(F32)]
+    far = swap(jnp.concatenate([adjoint] + tail, axis=0), "loop", 2)
+    near = swap(jnp.concatenate([forward] + tail, axis=0), "loop", 1)
+    tables = own_call(geometry, adjoint, forward)
+    part = rest_call((geometry, far, near, owner_map, owner_weight, *tables), cp_total)
     return halving(part, ("row", "loop"))
 
 

time: 49.9 us -> 40.5 us (0.81)
  starting transfers between devices: 14 us -> 8.4 us
  waiting for transfers between devices: 10 us -> 8.04 us
  Pallas kernels: 21.4 us -> 19.6 us
  local copies, waits for them, and re-layouts: 3.42 us -> 2.64 us
  other arithmetic: 0.61 us -> 1.32 us
    ppermute x12 -> x6, starting transfers between devices: 14 us -> 8.4 us  [swap(): return lax.ppermute(x, axis, [(k, k ^ bit) for k in range(size)])]
    unnamed x10, local copies, waits for them, and re-layouts: 3.2 us -> 0.69 us
    ppermute x12 -> x6, waiting for transfers between devices: 10 us -> 8.04 us  [swap(): return lax.ppermute(x, axis, [(k, k ^ bit) for k in range(size)])]
    pallas_call x1 -> x2, Pallas kernels: 21.4 us -> 19.6 us  [the longest x1 14.7 us: rest_call(): pl.pallas_call(rest_kernel, out_shape=shape((8, cp_total), F32), scratch_...]
    concatenate x0 -> x2, local copies, waits for them, and re-layouts: none -> 1.74 us  [the longest x1 1.68 us: on_device(): far = swap(jnp.concatenate([adjoint] + tail, axis=0), 'loop', 2)]
    convert_element_type x0 -> x1, other arithmetic: none -> 0.71 us  [on_device(): owner_map.astype(F32)]
  transfers between devices with their start and end apart: 12 -> 6, of which waited for: 7 -> 4; matrix products, arithmetic and copies ran while one was open for 0% -> 0% of each run, Pallas kernels for 0% -> 12%
where the time goes in v2:
time: 40.5 us; the launch traced here: 40.1 us
  Pallas kernels  19.6 us (48%)
  starting transfers between devices  8.4 us (21%)
  waiting for transfers between devices  8.04 us (20%)
  local copies, waits for them, and re-layouts  2.64 us (7%)
  other arithmetic  1.32 us (3%)
    pallas_call x1, Pallas kernels, rest_call(): pl.pallas_call(rest_kernel, out_shape=shape((8, cp_total), F32), scratch_...  14.7 us
    ppermute x6, starting transfers between devices, swap(): return lax.ppermute(x, axis, [(k, k ^ bit) for k in range(size)])  8.4 us
    ppermute x6, waiting for transfers between devices, swap(): return lax.ppermute(x, axis, [(k, k ^ bit) for k in range(size)])  8.04 us
    pallas_call x1, Pallas kernels, own_call(): pl.pallas_call(own_kernel, out_shape=[shape((width, 256), BF16), shape((4...  4.94 us
    concatenate x1, local copies, waits for them, and re-layouts, on_device(): far = swap(jnp.concatenate([adjoint] + tail, axis=0), 'loop', 2)  1.68 us
  transfers between devices with their start and end apart: 6, of which 4 were waited for; matrix products, arithmetic and copies ran while one was open for 0% of the time, Pallas kernels for 12%

profile of v2, /device:TPU:0, one launch (start us, length us, event | category | flops | bytes accessed | tf_op | source)
XLA Modules:
  0.0 40.1 jit_solution(13782404862899296718)
XLA Ops:
  0.0 0.0 copy-start.2
  0.0 0.7 %convert_element_type.3 = f32[4,512]{1,0:T(4,128)S(1)} convert(s32[4,512]{1,0:T(4,128)} %own.3) | non-fusion elementwise | flops 2048 | bytes 16384 | tf_op jit(solution)/shard_map/convert_element_type | solution.py:404
  0.7 0.0 copy-done.2
  0.7 0.0 copy-start.1
  0.7 0.0 copy-start.3
  0.7 1.7 %concatenate.6 = f32[80,512]{1,0:T(8,128)S(1)} concatenate(f32[64,512]{1,0:T(8,128)} %adj.1, f32[7,512]{1,0:T(8,128)S(1)} %copy-done.2, f32[1,512]{1,0:T(1,128)S(1)} %broadcast_in_dim.3, f32[4,512]{1,0:T(4,128)} %wt.1, f32[4,512]{1,0:T(4,128)S(1)} %convert_element_type.3), dimensions={0} | concatenate | bytes 327680 | tf_op jit(solution)/shard_map/concatenate | solution.py:405
  2.4 0.0 copy-start
  2.4 3.0 %collective-permute-start = (f32[80,512]{1,0:T(8,128)S(1)}, f32[80,512]{1,0:T(8,128)S(1)}, u32[]{:S(2)}, u32[]{:S(2)}) collective-permute-start(f32[80,512]{1,0:T(8,128)S(1)} %concatenate.6), channel_id=1, source_target_pairs={{0,2},{1,3},{2,0},{3,1},{4,6},{5,7},{6,4},{7,5},{8,10},{9,11},{10,... | collective-permute-start | bytes 491528 | tf_op jit(solution)/shard_map/ppermute | solution.py:378
  5.4 0.0 copy-done.1
  5.4 0.0 copy-done.3
  5.4 0.1 concatenate.7
  5.5 0.1 collective-permute-start.1
  5.6 0.0 copy-done
  5.6 4.9 %own.2 = (bf16[512,256]{1,0:T(8,128)(2,1)S(1)}, bf16[4,256,512]{2,1,0:T(8,128)(2,1)S(1)}, f32[3,512,128]{2,1,0:T(8,128)S(1)}, f32[3,32,512]{2,1,0:T(8,128)S(1)}, f32[3,32,512]{2,1,0:T(8,128)S(1)}) custom-call(f32[7,512]{1,0:T(8,128)S(1)} %copy-done.2, f32[64,512]{1,0:T(8,128)S(1)} %copy-done, f32[64,512]{1,0:T(8,128)S(1)} %copy-done.1), custom_call_target="tpu_custom_call" | custom-call | flops 4000000000 | bytes 4000000 | tf_op jit(solution)/shard_map/own/pallas_call | solution.py:340
  10.5 0.0 copy-start.4
  10.5 0.0 collective-permute-done.far
  10.6 0.0 collective-permute-done.1.near
  10.6 0.7 %copy-done.4 = s32[4,512]{1,0:T(4,128)S(1)} copy-done((s32[4,512]{1,0:T(4,128)S(1)}, s32[4,512]{1,0:T(4,128)}, u32[]{:S(2)}) %copy-start.4) | copy-done | bytes 8216
  11.2 14.7 %rest.1 = f32[8,512]{1,0:T(8,128)S(1)} custom-call(f32[7,512]{1,0:T(8,128)S(1)} %copy-done.2, f32[80,512]{1,0:T(8,128)S(1)} %collective-permute-done.far, f32[80,512]{1,0:T(8,128)S(1)} %collective-permute-done.1.near, s32[4,512]{1,0:T(4,128)S(1)} %copy-done.4, f32[4,512]{1,0:T(4,128)S(1)} %copy-done.3, bf16[512,256]{1,0:T(8,128)(2,1)S(1)} %get-tuple-element.10.left_o, ...), custom_call_target="tpu_custom_call" | custom-call | flops 12000000000 | bytes 4000000 | tf_op jit(solution)/shard_map/rest/pallas_call | solution.py:357
  25.9 0.2 reshape.6
  26.1 0.6 %collective-permute-start.2 = (f32[8,6,32]{2,1,0:T(8,128)S(1)}, f32[8,6,32]{2,1,0:T(8,128)S(1)}, u32[]{:S(2)}, u32[]{:S(2)}) collective-permute-start(f32[8,6,32]{2,1,0:T(8,128)S(1)} %constant_dynamic-slice_fusion.3), channel_id=1, source_target_pairs={{0,1},{1,0},{2,3},{3,2},{4,5},{5,4},{6,7},{7,6},{8,9},{9,8},{10,11... | collective-permute-start | bytes 18440 | tf_op jit(solution)/shard_map/ppermute | solution.py:378
  26.7 0.9 %collective-permute-done.2 = f32[8,6,32]{2,1,0:T(8,128)S(1)} collective-permute-done((f32[8,6,32]{2,1,0:T(8,128)S(1)}, f32[8,6,32]{2,1,0:T(8,128)S(1)}, u32[]{:S(2)}, u32[]{:S(2)}) %collective-permute-start.2) | collective-permute-done | bytes 6176 | tf_op jit(solution)/shard_map/ppermute | solution.py:378
  27.6 0.6 %collective-permute-start.3 = (f32[4,6,32]{2,1,0:T(8,128)S(1)}, f32[4,6,32]{2,1,0:T(8,128)S(1)}, u32[]{:S(2)}, u32[]{:S(2)}) collective-permute-start(f32[4,6,32]{2,1,0:T(8,128)S(1)} %constant_dynamic-slice_fusion.2), channel_id=1, source_target_pairs={{0,2},{1,3},{2,0},{3,1},{4,6},{5,7},{6,4},{7,5},{8,10},{9,11},{10,... | collective-permute-start | bytes 9224 | tf_op jit(solution)/shard_map/ppermute | solution.py:378
  28.2 3.2 %collective-permute-done.3 = f32[4,6,32]{2,1,0:T(8,128)S(1)} collective-permute-done((f32[4,6,32]{2,1,0:T(8,128)S(1)}, f32[4,6,32]{2,1,0:T(8,128)S(1)}, u32[]{:S(2)}, u32[]{:S(2)}) %collective-permute-start.3) | collective-permute-done | bytes 3104 | tf_op jit(solution)/shard_map/ppermute | solution.py:378
  31.4 1.6 %collective-permute-start.4 = (f32[2,6,32]{2,1,0:T(8,128)S(1)}, f32[2,6,32]{2,1,0:T(8,128)S(1)}, u32[]{:S(2)}, u32[]{:S(2)}) collective-permute-start(f32[2,6,32]{2,1,0:T(8,128)S(1)} %constant_dynamic-slice_fusion.1), channel_id=1, source_target_pairs={{0,4},{4,0},{8,12},{12,8},{1,5},{5,1},{9,13},{13,9},{2,6},{6,2},{1... | collective-permute-start | bytes 4616 | tf_op jit(solution)/shard_map/ppermute | solution.py:378
  33.0 2.1 %collective-permute-done.4 = f32[2,6,32]{2,1,0:T(8,128)S(1)} collective-permute-done((f32[2,6,32]{2,1,0:T(8,128)S(1)}, f32[2,6,32]{2,1,0:T(8,128)S(1)}, u32[]{:S(2)}, u32[]{:S(2)}) %collective-permute-start.4) | collective-permute-done | bytes 1568 | tf_op jit(solution)/shard_map/ppermute | solution.py:378
  35.0 2.6 %collective-permute-start.5 = (f32[1,6,32]{2,1,0:T(8,128)S(1)}, f32[1,6,32]{2,1,0:T(8,128)S(1)}, u32[]{:S(2)}, u32[]{:S(2)}) collective-permute-start(f32[1,6,32]{2,1,0:T(8,128)S(1)} %constant_dynamic-slice_fusion), channel_id=1, source_target_pairs={{0,8},{4,12},{8,0},{12,4},{1,9},{5,13},{9,1},{13,5},{2,10},{6,14},... | collective-permute-start | bytes 2312 | tf_op jit(solution)/shard_map/ppermute | solution.py:378
  37.6 1.9 %collective-permute-done.5 = f32[1,6,32]{2,1,0:T(8,128)S(1)} collective-permute-done((f32[1,6,32]{2,1,0:T(8,128)S(1)}, f32[1,6,32]{2,1,0:T(8,128)S(1)}, u32[]{:S(2)}, u32[]{:S(2)}) %collective-permute-start.5) | collective-permute-done | bytes 800 | tf_op jit(solution)/shard_map/ppermute | solution.py:378
  39.5 0.6 %add_bitcast_fusion = f32[6,32]{1,0:T(8,128)} fusion(f32[1,6,32]{2,1,0:T(8,128)S(1)} %collective-permute-done.5, f32[2,6,32]{2,1,0:T(8,128)S(1)} %dynamic-slice_add_fusion.2, s32[]{:T(128)S(6)} %select_n.44), kind=kLoop, calls=%fused_computation.3 | loop fusion | flops 192 | bytes 2308 | tf_op jit(solution)/shard_map/squeeze | solution.py:399
  (9 shorter events, 0.1 us)
Async XLA Ops:
  0.0 0.7 %copy-start.2 = (f32[7,512]{1,0:T(8,128)S(1)}, f32[7,512]{1,0:T(8,128)}, u32[]{:S(2)}) copy-start(f32[7,512]{1,0:T(8,128)} %geo.3) | copy-start | bytes 43012
  0.7 4.7 %copy-start.1 = (f32[64,512]{1,0:T(8,128)S(1)}, f32[64,512]{1,0:T(8,128)}, u32[]{:S(2)}) copy-start(f32[64,512]{1,0:T(8,128)} %fwd.1) | copy-start | bytes 393220
  0.7 4.7 %copy-start.3 = (f32[4,512]{1,0:T(4,128)S(1)}, f32[4,512]{1,0:T(4,128)}, u32[]{:S(2)}) copy-start(f32[4,512]{1,0:T(4,128)} %wt.1) | copy-start | bytes 24580
  2.4 3.1 %copy-start = (f32[64,512]{1,0:T(8,128)S(1)}, f32[64,512]{1,0:T(8,128)}, u32[]{:S(2)}) copy-start(f32[64,512]{1,0:T(8,128)} %adj.1) | copy-start | bytes 393220
  2.4 8.1 %collective-permute-start = (f32[80,512]{1,0:T(8,128)S(1)}, f32[80,512]{1,0:T(8,128)S(1)}, u32[]{:S(2)}, u32[]{:S(2)}) collective-permute-start(f32[80,512]{1,0:T(8,128)S(1)} %concatenate.6), channel_id=1, source_target_pairs={{0,2},{1,3},{2,0},{3,1},{4,6},{5,7},{6,4},{7,5},{8,10},{9,11},{10,... | collective-permute-start | bytes 491528 | tf_op jit(solution)/shard_map/ppermute | solution.py:378
  5.5 5.1 %collective-permute-start.1 = (f32[80,512]{1,0:T(8,128)S(1)}, f32[80,512]{1,0:T(8,128)S(1)}, u32[]{:S(2)}, u32[]{:S(2)}) collective-permute-start(f32[80,512]{1,0:T(8,128)S(1)} %concatenate.7), channel_id=1, source_target_pairs={{0,1},{1,0},{2,3},{3,2},{4,5},{5,4},{6,7},{7,6},{8,9},{9,8},{10,11... | collective-permute-start | bytes 491528 | tf_op jit(solution)/shard_map/ppermute | solution.py:378
  10.5 0.7 %copy-start.4 = (s32[4,512]{1,0:T(4,128)S(1)}, s32[4,512]{1,0:T(4,128)}, u32[]{:S(2)}) copy-start(s32[4,512]{1,0:T(4,128)} %own.3) | copy-start | bytes 24580
  26.1 1.4 %collective-permute-start.2 = (f32[8,6,32]{2,1,0:T(8,128)S(1)}, f32[8,6,32]{2,1,0:T(8,128)S(1)}, u32[]{:S(2)}, u32[]{:S(2)}) collective-permute-start(f32[8,6,32]{2,1,0:T(8,128)S(1)} %constant_dynamic-slice_fusion.3), channel_id=1, source_target_pairs={{0,1},{1,0},{2,3},{3,2},{4,5},{5,4},{6,7},{7,6},{8,9},{9,8},{10,11... | collective-permute-start | bytes 18440 | tf_op jit(solution)/shard_map/ppermute | solution.py:378
  27.6 3.8 %collective-permute-start.3 = (f32[4,6,32]{2,1,0:T(8,128)S(1)}, f32[4,6,32]{2,1,0:T(8,128)S(1)}, u32[]{:S(2)}, u32[]{:S(2)}) collective-permute-start(f32[4,6,32]{2,1,0:T(8,128)S(1)} %constant_dynamic-slice_fusion.2), channel_id=1, source_target_pairs={{0,2},{1,3},{2,0},{3,1},{4,6},{5,7},{6,4},{7,5},{8,10},{9,11},{10,... | collective-permute-start | bytes 9224 | tf_op jit(solution)/shard_map/ppermute | solution.py:378
  31.4 3.7 %collective-permute-start.4 = (f32[2,6,32]{2,1,0:T(8,128)S(1)}, f32[2,6,32]{2,1,0:T(8,128)S(1)}, u32[]{:S(2)}, u32[]{:S(2)}) collective-permute-start(f32[2,6,32]{2,1,0:T(8,128)S(1)} %constant_dynamic-slice_fusion.1), channel_id=1, source_target_pairs={{0,4},{4,0},{8,12},{12,8},{1,5},{5,1},{9,13},{13,9},{2,6},{6,2},{1... | collective-permute-start | bytes 4616 | tf_op jit(solution)/shard_map/ppermute | solution.py:378
  35.0 4.5 %collective-permute-start.5 = (f32[1,6,32]{2,1,0:T(8,128)S(1)}, f32[1,6,32]{2,1,0:T(8,128)S(1)}, u32[]{:S(2)}, u32[]{:S(2)}) collective-permute-start(f32[1,6,32]{2,1,0:T(8,128)S(1)} %constant_dynamic-slice_fusion), channel_id=1, source_target_pairs={{0,8},{4,12},{8,0},{12,4},{1,9},{5,13},{9,1},{13,5},{2,10},{6,14},... | collective-permute-start | bytes 2312 | tf_op jit(solution)/shard_map/ppermute | solution.py:378

commit v3 on v2

v3 whole, which is shorter than its diff:
```python
import functools
import math

import jax
import jax.numpy as jnp
from jax import lax
from jax.experimental import pallas as pl
from jax.experimental.pallas import tpu as pltpu
from jax.sharding import PartitionSpec as P

WAVENUM = 2.0 * math.pi * 6000.0 / 1500.0
TURNS = WAVENUM / (2.0 * math.pi)
PAIR_SCALE = WAVENUM**3 / (4.0 * math.pi * TURNS)
F32 = jnp.float32
BF16 = jnp.bfloat16
TI = 256
TJ = 256
SUB = 16
LANE = 128

SIN_C = None
COS_C = None


def _fit(fn, odd, terms):
    import numpy as np

    nodes = 0.5 * np.cos(np.pi * (np.arange(400) + 0.5) / 400)
    cols = np.stack([nodes ** (2 * n + odd) for n in range(terms)], axis=1)
    coef = np.linalg.lstsq(cols, fn(nodes), rcond=None)[0]
    return [float(np.float32(c)) for c in coef]


def _tables():
    import numpy as np

    s = _fit(lambda t: math.sqrt(2.0) * np.sin(np.pi * t), 1, 4)
    c = _fit(lambda t: math.sqrt(2.0) * np.cos(np.pi * t), 0, 5)
    return s, c


SIN_C, COS_C = _tables()


def horner(coef, y):
    acc = coef[-1] * y + coef[-2]
    for c in coef[-3::-1]:
        acc = acc * y + c
    return acc


def hi_part(x):
    return x.astype(BF16).astype(F32)


def split3(x):
    one = hi_part(x)
    rest = x - one
    two = hi_part(rest)
    return one, two, rest - two


SPLIT_PAIRS = ((0, 0), (0, 1), (1, 0), (0, 2), (2, 0), (1, 1), (1, 2), (2, 1))


def rows8(x, n, a, b):
    return jnp.concatenate([x, n, a, b], axis=0)


def target_rows(geo, center):
    x = (geo[0:3] - center) * TURNS
    m = geo[3:6] * (1.0 / WAVENUM)
    ones = jnp.ones_like(x[0:1])
    xm = jnp.sum(x * m, axis=0, keepdims=True)
    return x, m, split3(rows8(x, m, ones, xm))


def target_table(adj, rows):
    hi = hi_part(adj)
    lo = adj - hi
    return jnp.concatenate([hi, hi, lo] + [rows[a] for a, _ in SPLIT_PAIRS], axis=0)


def source_rows(geo, center):
    x = (geo[0:3] - center) * TURNS
    n = geo[3:6]
    return x, n


def source_table(geo, fwd, x, n):
    area = geo[6:7]
    scaled = fwd * (area * PAIR_SCALE)
    re, im = scaled[0:32], scaled[32:64]
    real = jnp.concatenate([re, im], axis=0)
    imag = jnp.concatenate([im, -re], axis=0)
    rh, ih = hi_part(real), hi_part(imag)
    zero3 = jnp.zeros_like(x)
    zero1 = jnp.zeros_like(x[0:1])
    ones = jnp.ones_like(zero1)
    xn = jnp.sum(x * n, axis=0, keepdims=True)
    prow = split3(rows8(-n, zero3, xn, zero1))
    qrow = split3(rows8(zero3, -x, zero1, ones))
    zeros_w = jnp.zeros((192, x.shape[1]), F32)
    tail = jnp.zeros((64, x.shape[1]), F32)
    cols = [
        jnp.concatenate([rh, real - rh, rh, tail], axis=0),
        jnp.concatenate([ih, imag - ih, ih, tail], axis=0),
        jnp.concatenate([zeros_w] + [prow[b] for _, b in SPLIT_PAIRS], axis=0),
        jnp.concatenate([zeros_w] + [qrow[b] for _, b in SPLIT_PAIRS], axis=0),
    ]
    return cols


def pair_chunk(prod, xi, xj, area):
    wr, wi, pn, q = prod
    d0, d1, d2 = xi[0] - xj[0], xi[1] - xj[1], xi[2] - xj[2]
    r2 = (d0 * d0 + d1 * d1) + (d2 * d2 + area)
    rs = lax.rsqrt(r2)
    turns = r2 * rs
    t = turns - jnp.round(turns)
    v = rs * (1.0 / (2.0 * math.pi))
    y = t * t
    sv = (t * v) * horner(SIN_C, y)
    cv = v * horner(COS_C, y)
    es = sv * cv
    ec = v * v - sv * sv
    yr = ec * wr - es * wi
    yi = ec * wi + es * wr
    a = yi + v * yr
    b = yr - v * yi
    c = rs * ((q * yi - pn * yr) + (3.0 * v) * (pn * a + q * b))
    return a, b, c


def dot(a, b, dims=(((1,), (0,)), ((), ()))):
    return lax.dot_general(a, b, dims, preferred_element_type=F32)


def sum_splits(x):
    return x[0:8] + x[8:16] + x[16:24]


NT = (((1,), (1,)), ((), ()))


def sum_rows(x, n):
    width = x.shape[1]
    zero = jnp.zeros((1, width), F32)
    x1, x2, x3 = split3(x)
    n1 = hi_part(n)
    xr = jnp.concatenate([x1, jnp.ones_like(zero), x2, zero, x3, zero], axis=0)
    nr = jnp.concatenate([n1, zero, n - n1, zero], axis=0)
    z12, z20 = jnp.zeros((12, width), F32), jnp.zeros((20, width), F32)
    rows = ([xr, z20], [z12, nr, z12], [z20, xr])
    return [jnp.concatenate(r, axis=0).astype(BF16) for r in rows]


def read_sums(acc):
    return acc[0:4] + acc[4:8] + acc[8:12], acc[12:15] + acc[16:19], acc[20:24] + acc[24:28] + acc[28:32]


def build_targets(geo, adj, center, cols, left, xi_ref, frow):
    x, m, rows = target_rows(geo, center)
    left[cols, :] = target_table(adj, rows).T.astype(BF16)
    sums = sum_rows(x, m)
    for k in range(3):
        frow[k, :, cols] = sums[k]
    xt = jnp.concatenate([x, m, m[0:2]], axis=0).T
    for k in range(3):
        xi_ref[k, cols, :] = jnp.broadcast_to(xt[:, k : k + 1], (x.shape[1], LANE))


def build_sources(geo, fwd, center, cols, right, xj_ref, fcol):
    x, n = source_rows(geo, center)
    xj_ref[:, cols] = jnp.concatenate([x, geo[6:7] * (TURNS * TURNS)] * 2, axis=0)
    tab = source_table(geo, fwd, x, n)
    for k in range(4):
        right[k, :, cols] = tab[k].astype(BF16)
    sums = sum_rows(x, n)
    for k, part in enumerate((sums[1], sums[0], sums[2])):
        fcol[k, :, cols] = part


def center_of(geo):
    return jnp.round(jnp.mean(geo[0:3], axis=1, keepdims=True))


def run_tiles(count, place, left, right, xi_ref, xj_ref, frow, fcol, prod, abc, tsum, ssum):
    def start(t):
        i0, j0 = place(t)
        return pl.multiple_of(i0, TI), pl.multiple_of(j0, TJ)

    def products(t, slot):
        i0, j0 = start(t)

        def piece(k):
            prod[slot, k] = dot(left[pl.ds(i0, TI), :], right[k, :, pl.ds(j0, TJ)])

        return [functools.partial(piece, k) for k in range(4)]

    def values(t, slot):
        i0, j0 = start(t)

        def piece(jj, ii):
            lanes = pl.ds(j0 + jj * LANE, LANE)
            here = slice(jj * LANE, (jj + 1) * LANE)
            xj = [xj_ref[k : k + 1, lanes] for k in range(4)]
            rows = pl.ds(ii * SUB, SUB)
            xi = [xi_ref[k, pl.ds(i0 + ii * SUB, SUB), :] for k in range(3)]
            pr = [prod[slot, k, rows, here] for k in range(4)]
            for k, val in enumerate(pair_chunk(pr, xi, xj[0:3], xj[3])):
                hi = val.astype(BF16)
                abc[slot, 2 * k, rows, here] = hi
                abc[slot, 2 * k + 1, rows, here] = (val - hi.astype(F32)).astype(BF16)

        return [functools.partial(piece, jj, ii) for jj in range(TJ // LANE) for ii in range(TI // SUB)]

    def sums(t, slot):
        i0, j0 = start(t)
        kept = [None, None]

        def piece(k):
            fi = frow[k, :, pl.ds(i0, TI)]
            hi, lo = abc[slot, 2 * k], abc[slot, 2 * k + 1]
            add = dot(jnp.concatenate([fi, fi], axis=1), jnp.concatenate([hi, lo], axis=0))
            kept[0] = add if k == 0 else kept[0] + add
            if k == 2:
                ssum[:, pl.ds(j0, TJ)] += kept[0]

        def other(k):
            fj = fcol[k, :, pl.ds(j0, TJ)]
            hi, lo = abc[slot, 2 * k], abc[slot, 2 * k + 1]
            add = dot(jnp.concatenate([fj, fj], axis=1), jnp.concatenate([hi, lo], axis=1), NT)
            kept[1] = add if k == 0 else kept[1] + add
            if k == 2:
                tsum[:, pl.ds(i0, TI)] += kept[1]

        return [functools.partial(f, k) for f in (piece, other) for k in range(3)]

    def interleave(vector, matrix):
        gap = len(vector) // len(matrix)
        for n, todo in enumerate(vector):
            if n % gap == 0 and n // gap < len(matrix):
                matrix[n // gap]()
            todo()

    last = count - 1
    for todo in products(0, 0):
        todo()
    abc[1] = jnp.zeros_like(abc[1])

    def double(u, _):
        t = 2 * u
        interleave(values(t, 0), products(t + 1, 1) + sums(jnp.maximum(t - 1, 0), 1))
        interleave(values(t + 1, 1), products(jnp.minimum(t + 2, last), 0) + sums(t, 0))
        return 0

    lax.fori_loop(0, count // 2, double, 0)
    for todo in sums(last, 1):
        todo()


def pack_kernel(geo, adj, fwd, own, wt, tpack, spack, geo_v, own_v, wt_v, sems):
    copies = [
        pltpu.make_async_copy(src, dst, sems.at[k])
        for k, (src, dst) in enumerate(
            ((adj, tpack.at[0:64]), (fwd, spack.at[0:64]), (geo, geo_v), (own, own_v), (wt, wt_v))
        )
    ]
    for c in copies:
        c.start()
    for c in copies[2:]:
        c.wait()
    geo_rows = jnp.concatenate([geo_v[...], jnp.zeros_like(geo_v[0:1])], axis=0)
    own_rows = jnp.concatenate([wt_v[...], own_v[...].astype(F32)], axis=0)
    for pack in (tpack, spack):
        pack[64:72] = geo_rows
        pack[72:80] = own_rows
    for c in copies[:2]:
        c.wait()


def own_kernel(geo_ref, adj, fwd, left, right, xi_ref, tsum, ssum, xj_ref, frow, fcol, prod, abc):
    width = geo_ref.shape[1]
    geo = geo_ref[...]
    center = center_of(geo)
    cols = pl.ds(0, width)
    build_targets(geo, adj[...], center, cols, left, xi_ref, frow)
    build_sources(geo, fwd[...], center, cols, right, xj_ref, fcol)
    tsum[...] = jnp.zeros_like(tsum)
    ssum[...] = jnp.zeros_like(ssum)
    n_j = width // TJ
    run_tiles(
        (width // TI) * n_j, lambda t: ((t // n_j) * TI, lax.rem(t, n_j) * TJ),
        left, right, xi_ref, xj_ref, frow, fcol, prod, abc, tsum, ssum,
    )


def reverse_bits(x, bits):
    out = jnp.zeros_like(x)
    for b in range(bits):
        out = out | (((x >> b) & 1) << (bits - 1 - b))
    return out


def rest_kernel(
    tpack, far, near, left_o, right_o, xi_o, tsum_o, ssum_o,
    out_ref,
    left, right, xi_ref, xj_ref, frow, fcol, prod, abc, tsum, ssum,
):
    width = tpack.shape[1]
    geo = tpack[64:71]
    center = center_of(geo)
    first, second = pl.ds(0, width), pl.ds(width, width)
    left[first, :] = left_o[...]
    right[:, :, first] = right_o[...]
    xi_ref[:, first, :] = xi_o[...]
    x, n = source_rows(geo, center)
    tsums, ssums = sum_rows(x, n * (1.0 / WAVENUM)), sum_rows(x, n)
    for k in range(3):
        frow[k, :, first] = tsums[k]
        fcol[k, :, first] = ssums[(1, 0, 2)[k]]
    xj_ref[:, first] = jnp.concatenate([x, geo[6:7] * (TURNS * TURNS)] * 2, axis=0)
    tsum[:, first] = tsum_o[...]
    ssum[:, first] = ssum_o[...]
    tsum[:, second] = jnp.zeros_like(tsum_o)
    ssum[:, second] = jnp.zeros_like(ssum_o)
    build_targets(far[64:71], far[0:64], center, second, left, xi_ref, frow)
    build_sources(near[64:71], near[0:64], center, second, right, xj_ref, fcol)

    n_i, n_j = width // TI, width // TJ
    block = n_i * n_j

    def place(t):
        b = t // block
        inner = lax.rem(t, block)
        i0 = jnp.where(b > 0, width, 0) + (inner // n_j) * TI
        j0 = jnp.where(b == 1, 0, width) + lax.rem(inner, n_j) * TJ
        return i0, j0

    run_tiles(3 * block, place, left, right, xi_ref, xj_ref, frow, fcol, prod, abc, tsum, ssum)

    def target_grad(g, cols):
        x = (g[0:3] - center) * TURNS
        m = g[3:6] * (1.0 / WAVENUM)
        sb, an, sc = read_sums(tsum[:, cols])
        gx = (2.0 * math.pi) * (x * sc[3:4] - sc[0:3]) + an - m * sb[3:4]
        gn = sb[0:3] - x * sb[3:4]
        return gx * TURNS, gn * (1.0 / WAVENUM)

    def source_grad(g, cols):
        x = (g[0:3] - center) * TURNS
        n = g[3:6]
        sa, bm, sc = read_sums(ssum[:, cols])
        gx = (2.0 * math.pi) * (x * sc[3:4] - sc[0:3]) - n * sa[3:4] + bm
        gn = sa[0:3] - x * sa[3:4]
        return gx * TURNS, gn

    t_own, s_own = target_grad(geo, first), source_grad(geo, first)
    zero2 = jnp.zeros((2, width), F32)
    grads = [
        (t_own[0] + s_own[0], t_own[1] + s_own[1]),
        target_grad(far[64:71], second),
        source_grad(near[64:71], second),
    ]
    slots, _, cp_dev = out_ref.shape
    low_iota = lax.broadcasted_iota(jnp.int32, (cp_dev, width), 0)
    terms = []
    for (gx, gn), pack in zip(grads, (tpack, far, near)):
        g = jnp.concatenate([gx, gn, zero2], axis=0)
        own, wt = pack[76:80].astype(jnp.int32), pack[72:76]
        place_of = reverse_bits(own // cp_dev, slots.bit_length() - 1)
        low = lax.rem(own, cp_dev)
        for s in range(4):
            gw = g * wt[s : s + 1]
            hi = hi_part(gw)
            here = jnp.where(low[s : s + 1] == low_iota, 1.0, 0.0).astype(BF16)
            terms.append((place_of[s : s + 1], hi, gw - hi, here))
    onehot = jnp.concatenate([t[3] for t in terms], axis=1)

    def add_owner(step, _):
        s0 = step * 16
        cols = []
        for where_to, hi, lo, _ in terms:
            rows = []
            for r in range(16):
                mask = where_to == s0 + r
                rows += [jnp.where(mask, hi, 0.0), jnp.where(mask, lo, 0.0)]
            cols.append(jnp.concatenate(rows, axis=0).astype(BF16))
        acc = dot(jnp.concatenate(cols, axis=1), onehot, NT).reshape(16, 16, cp_dev)
        out_ref[pl.ds(s0, 16)] = acc[:, 0:8] + acc[:, 8:16]
        return 0

    if slots == 16:
        add_owner(0, 0)
    else:
        lax.fori_loop(0, slots // 16, add_owner, 0)


def shape(dims, kind):
    return jax.ShapeDtypeStruct(dims, kind)


def tile_scratch():
    return [pltpu.VMEM((2, 4, TI, TJ), F32), pltpu.VMEM((2, 6, TI, TJ), BF16)]


PARAMS = pltpu.CompilerParams(vmem_limit_bytes=20 * 1024 * 1024)


def pack_call(geo, adj, fwd, own, wt):
    width = geo.shape[1]
    return pl.pallas_call(
        pack_kernel,
        in_specs=[pl.BlockSpec(memory_space=pl.ANY)] * 5,
        out_shape=[shape((80, width), F32)] * 2,
        scratch_shapes=[
            pltpu.VMEM((7, width), F32), pltpu.VMEM((4, width), jnp.int32), pltpu.VMEM((4, width), F32),
            pltpu.SemaphoreType.DMA((5,)),
        ],
        name="pack",
    )(geo, adj, fwd, own, wt)


def own_call(geo, adj, fwd):
    width = geo.shape[1]
    return pl.pallas_call(
        own_kernel,
        out_shape=[
            shape((width, 256), BF16), shape((4, 256, width), BF16), shape((3, width, LANE), F32),
            shape((32, width), F32), shape((32, width), F32),
        ],
        scratch_shapes=[
            pltpu.VMEM((8, width), F32), pltpu.VMEM((3, 32, width), BF16), pltpu.VMEM((3, 32, width), BF16)
        ]
        + tile_scratch(),
        compiler_params=PARAMS,
        cost_estimate=pl.CostEstimate(flops=4 * 10**9, bytes_accessed=4 * 10**6, transcendentals=0),
        name="own",
    )(geo, adj, fwd)


def rest_call(args, slots, cp_dev):
    width = args[0].shape[1]
    total = 2 * width
    return pl.pallas_call(
        rest_kernel,
        out_shape=shape((slots, 8, cp_dev), F32),
        scratch_shapes=[
            pltpu.VMEM((total, 256), BF16),
            pltpu.VMEM((4, 256, total), BF16),
            pltpu.VMEM((3, total, LANE), F32),
            pltpu.VMEM((8, total), F32),
            pltpu.VMEM((3, 32, total), BF16),
            pltpu.VMEM((3, 32, total), BF16),
        ]
        + tile_scratch()
        + [pltpu.VMEM((32, total), F32), pltpu.VMEM((32, total), F32)],
        compiler_params=PARAMS,
        cost_estimate=pl.CostEstimate(flops=12 * 10**9, bytes_accessed=4 * 10**6, transcendentals=0),
        name="rest",
    )(*args)


def swap(x, axis, bit):
    size = lax.axis_size(axis)
    return lax.ppermute(x, axis, [(k, k ^ bit) for k in range(size)])


def halving(cur):
    n_loop = lax.axis_size("loop").bit_length() - 1
    n_row = lax.axis_size("row").bit_length() - 1
    steps = [("loop", 1 << b) for b in range(n_loop)] + [("row", 1 << b) for b in range(n_row)]
    for axis, bit in steps:
        half = cur.shape[0] // 2
        up = jnp.where((lax.axis_index(axis) & bit) > 0, 1, 0)
        keep = lax.dynamic_slice_in_dim(cur, up * half, half, 0)
        send = lax.dynamic_slice_in_dim(cur, (1 - up) * half, half, 0)
        cur = keep + swap(send, axis, bit)
    return cur[0, 0:6]


def on_device(cp_dev, geometry, adjoint, forward, owner_map, owner_weight):
    slots = lax.axis_size("row") * lax.axis_size("loop")
    tpack, spack = pack_call(geometry, adjoint, forward, owner_map, owner_weight)
    far = swap(tpack, "loop", 2)
    near = swap(spack, "loop", 1)
    tables = own_call(geometry, adjoint, forward)
    return halving(rest_call((tpack, far, near, *tables), slots, cp_dev))


def solution(mesh):
    spec = P(None, ("parts", "row", "loop"))
    return jax.shard_map(
        functools.partial(on_device, 32), mesh=mesh, in_specs=(spec,) * 5, out_specs=spec, check_vma=False
    )
```

time: 40.5 us -> 37.5 us (0.926)
  local copies, waits for them, and re-layouts: 2.64 us -> 0.64 us
  other arithmetic: 1.32 us -> 0.02 us
  waiting for transfers between devices: 8.04 us -> 7.49 us
  starting transfers between devices: 8.4 us -> 8.94 us
  Pallas kernels: 19.6 us -> 20.1 us
    concatenate x2 -> x0, local copies, waits for them, and re-layouts: 1.74 us -> none  [the longest x1 1.68 us: on_device(): far = swap(jnp.concatenate([adjoint] + tail, axis=0), 'loop', 2)]
    convert_element_type x1 -> x0, other arithmetic: 0.71 us -> none  [on_device(): owner_map.astype(F32)]
    unnamed x10 -> x8, local copies, waits for them, and re-layouts: 0.69 us -> 0.01 us
    pallas_call x1 -> x2, Pallas kernels: 14.7 us -> 15.3 us  [the longest x1 13.6 us: rest_call(): pl.pallas_call(rest_kernel, out_shape=shape((slots, 8, cp_dev), F32), scr...]
    squeeze x0 -> x1, local copies, waits for them, and re-layouts: none -> 0.6 us  [halving(): return cur[0, 0:6]]
    squeeze x1 -> x0, other arithmetic: 0.59 us -> none  [halving(): return cur[0]]
    ppermute x6, waiting for transfers between devices: 8.04 us -> 7.49 us  [swap(): return lax.ppermute(x, axis, [(k, k ^ bit) for k in range(size)])]
    ppermute x6, starting transfers between devices: 8.4 us -> 8.94 us  [swap(): return lax.ppermute(x, axis, [(k, k ^ bit) for k in range(size)])]
  transfers between devices with their start and end apart: 6 -> 6, of which waited for: 4 -> 4; matrix products, arithmetic and copies ran while one was open for 0% -> 0% of each run, Pallas kernels for 12% -> 13%
where the time goes in v3:
time: 37.5 us; the launch traced here: 37.3 us
  Pallas kernels  20.1 us (54%)
  starting transfers between devices  8.94 us (24%)
  waiting for transfers between devices  7.49 us (20%)
  local copies, waits for them, and re-layouts  0.64 us (2%)
    pallas_call x1, Pallas kernels, rest_call(): pl.pallas_call(rest_kernel, out_shape=shape((slots, 8, cp_dev), F32), scr...  13.6 us
    ppermute x6, starting transfers between devices, swap(): return lax.ppermute(x, axis, [(k, k ^ bit) for k in range(size)])  8.94 us
    ppermute x6, waiting for transfers between devices, swap(): return lax.ppermute(x, axis, [(k, k ^ bit) for k in range(size)])  7.49 us
    pallas_call x1, Pallas kernels, own_call(): pl.pallas_call(own_kernel, out_shape=[shape((width, 256), BF16), shape((4...  4.79 us
    pallas_call x1, Pallas kernels, pack_call(): pl.pallas_call(pack_kernel, in_specs=[pl.BlockSpec(memory_space=pl.ANY)]...  1.78 us
  transfers between devices with their start and end apart: 6, of which 4 were waited for; matrix products, arithmetic and copies ran while one was open for 0% of the time, Pallas kernels for 13%

profile of v3, /device:TPU:0, one launch (start us, length us, event | category | flops | bytes accessed | tf_op | source)
XLA Modules:
  0.0 37.3 jit_solution(6386892773914108122)
XLA Ops:
  0.0 0.0 copy-start.2
  0.0 0.0 copy-start
  0.0 0.0 copy-start.1
  0.0 1.8 %pack.1 = (f32[80,512]{1,0:T(8,128)}, f32[80,512]{1,0:T(8,128)}) custom-call(f32[7,512]{1,0:T(8,128)} %geo_ref.1, f32[64,512]{1,0:T(8,128)} %adj.3, f32[64,512]{1,0:T(8,128)} %fwd.3, s32[4,512]{1,0:T(4,128)} %own.2, f32[4,512]{1,0:T(4,128)} %wt.1), custom_call_target="tpu_custom_call" | custom-call | tf_op jit(solution)/shard_map/pack/pallas_call | solution.py:413
  1.8 3.0 %collective-permute-start = (f32[80,512]{1,0:T(8,128)}, f32[80,512]{1,0:T(8,128)S(1)}, u32[]{:S(2)}, u32[]{:S(2)}) collective-permute-start(f32[80,512]{1,0:T(8,128)} %get-tuple-element.12.tpack), channel_id=1, source_target_pairs={{0,2},{1,3},{2,0},{3,1},{4,6},{5,7},{6,4},{7,5},{8,10},{9,11},{10,... | collective-permute-start | bytes 491528 | tf_op jit(solution)/shard_map/ppermute | solution.py:467
  4.8 0.0 copy-start.3
  4.8 0.0 collective-permute-start.1
  4.8 0.0 copy-done.2
  4.8 0.0 copy-done
  4.8 0.0 copy-done.1
  4.8 4.8 %own.3 = (bf16[512,256]{1,0:T(8,128)(2,1)S(1)}, bf16[4,256,512]{2,1,0:T(8,128)(2,1)S(1)}, f32[3,512,128]{2,1,0:T(8,128)S(1)}, f32[32,512]{1,0:T(8,128)S(1)}, f32[32,512]{1,0:T(8,128)S(1)}) custom-call(f32[7,512]{1,0:T(8,128)S(1)} %copy-done.2, f32[64,512]{1,0:T(8,128)S(1)} %copy-done, f32[64,512]{1,0:T(8,128)S(1)} %copy-done.1), custom_call_target="tpu_custom_call" | custom-call | flops 4000000000 | bytes 4000000 | tf_op jit(solution)/shard_map/own/pallas_call | solution.py:427
  9.6 0.0 collective-permute-done.far
  9.6 0.0 collective-permute-done.1.near
  9.6 0.0 copy-done.3
  9.7 13.6 %rest.1 = f32[16,8,32]{2,1,0:T(8,128)S(1)} custom-call(f32[80,512]{1,0:T(8,128)S(1)} %copy-done.3, f32[80,512]{1,0:T(8,128)S(1)} %collective-permute-done.far, f32[80,512]{1,0:T(8,128)S(1)} %collective-permute-done.1.near, bf16[512,256]{1,0:T(8,128)(2,1)S(1)} %get-tuple-element.14.left_o, bf16[4,256,512]{2,1,0:T(8,128)(2,1)S(1)} %get-tuple-element.15.right_o, ...), custom_call_target="tpu_custom_call" | custom-call | flops 12000000000 | bytes 4000000 | tf_op jit(solution)/shard_map/rest/pallas_call | solution.py:446
  23.2 0.6 %collective-permute-start.2 = (f32[8,8,32]{2,1,0:T(8,128)S(1)}, f32[8,8,32]{2,1,0:T(8,128)S(1)}, u32[]{:S(2)}, u32[]{:S(2)}) collective-permute-start(f32[8,8,32]{2,1,0:T(8,128)S(1)} %constant_dynamic-slice_fusion.3), channel_id=1, source_target_pairs={{0,1},{1,0},{2,3},{3,2},{4,5},{5,4},{6,7},{7,6},{8,9},{9,8},{10,11... | collective-permute-start | bytes 24584 | tf_op jit(solution)/shard_map/ppermute | solution.py:467
  23.8 0.9 %collective-permute-done.2 = f32[8,8,32]{2,1,0:T(8,128)S(1)} collective-permute-done((f32[8,8,32]{2,1,0:T(8,128)S(1)}, f32[8,8,32]{2,1,0:T(8,128)S(1)}, u32[]{:S(2)}, u32[]{:S(2)}) %collective-permute-start.2) | collective-permute-done | bytes 8224 | tf_op jit(solution)/shard_map/ppermute | solution.py:467
  24.7 1.2 %collective-permute-start.3 = (f32[4,8,32]{2,1,0:T(8,128)S(1)}, f32[4,8,32]{2,1,0:T(8,128)S(1)}, u32[]{:S(2)}, u32[]{:S(2)}) collective-permute-start(f32[4,8,32]{2,1,0:T(8,128)S(1)} %constant_dynamic-slice_fusion.2), channel_id=1, source_target_pairs={{0,2},{1,3},{2,0},{3,1},{4,6},{5,7},{6,4},{7,5},{8,10},{9,11},{10,... | collective-permute-start | bytes 12296 | tf_op jit(solution)/shard_map/ppermute | solution.py:467
  25.9 2.6 %collective-permute-done.3 = f32[4,8,32]{2,1,0:T(8,128)S(1)} collective-permute-done((f32[4,8,32]{2,1,0:T(8,128)S(1)}, f32[4,8,32]{2,1,0:T(8,128)S(1)}, u32[]{:S(2)}, u32[]{:S(2)}) %collective-permute-start.3) | collective-permute-done | bytes 4128 | tf_op jit(solution)/shard_map/ppermute | solution.py:467
  28.5 1.6 %collective-permute-start.4 = (f32[2,8,32]{2,1,0:T(8,128)S(1)}, f32[2,8,32]{2,1,0:T(8,128)S(1)}, u32[]{:S(2)}, u32[]{:S(2)}) collective-permute-start(f32[2,8,32]{2,1,0:T(8,128)S(1)} %constant_dynamic-slice_fusion.1), channel_id=1, source_target_pairs={{0,4},{4,0},{8,12},{12,8},{1,5},{5,1},{9,13},{13,9},{2,6},{6,2},{1... | collective-permute-start | bytes 6152 | tf_op jit(solution)/shard_map/ppermute | solution.py:467
  30.1 2.1 %collective-permute-done.4 = f32[2,8,32]{2,1,0:T(8,128)S(1)} collective-permute-done((f32[2,8,32]{2,1,0:T(8,128)S(1)}, f32[2,8,32]{2,1,0:T(8,128)S(1)}, u32[]{:S(2)}, u32[]{:S(2)}) %collective-permute-start.4) | collective-permute-done | bytes 2080 | tf_op jit(solution)/shard_map/ppermute | solution.py:467
  32.2 2.6 %collective-permute-start.5 = (f32[1,8,32]{2,1,0:T(8,128)S(1)}, f32[1,8,32]{2,1,0:T(8,128)S(1)}, u32[]{:S(2)}, u32[]{:S(2)}) collective-permute-start(f32[1,8,32]{2,1,0:T(8,128)S(1)} %constant_dynamic-slice_fusion), channel_id=1, source_target_pairs={{0,8},{4,12},{8,0},{12,4},{1,9},{5,13},{9,1},{13,5},{2,10},{6,14},... | collective-permute-start | bytes 3080 | tf_op jit(solution)/shard_map/ppermute | solution.py:467
  34.8 1.9 %collective-permute-done.5 = f32[1,8,32]{2,1,0:T(8,128)S(1)} collective-permute-done((f32[1,8,32]{2,1,0:T(8,128)S(1)}, f32[1,8,32]{2,1,0:T(8,128)S(1)}, u32[]{:S(2)}, u32[]{:S(2)}) %collective-permute-start.5) | collective-permute-done | bytes 1056 | tf_op jit(solution)/shard_map/ppermute | solution.py:467
  36.7 0.6 %slice_bitcast_fusion = f32[6,32]{1,0:T(8,128)} fusion(f32[1,8,32]{2,1,0:T(8,128)S(1)} %dynamic-slice_add_fusion.3), kind=kLoop, calls=%fused_computation.3 | loop fusion | bytes 1536 | tf_op jit(solution)/shard_map/squeeze | solution.py:480
  (8 shorter events, 0.0 us)
Async XLA Ops:
  0.0 4.8 %copy-start.2 = (f32[7,512]{1,0:T(8,128)S(1)}, f32[7,512]{1,0:T(8,128)}, u32[]{:S(2)}) copy-start(f32[7,512]{1,0:T(8,128)} %geo_ref.1) | copy-start | bytes 43012
  0.0 4.8 %copy-start = (f32[64,512]{1,0:T(8,128)S(1)}, f32[64,512]{1,0:T(8,128)}, u32[]{:S(2)}) copy-start(f32[64,512]{1,0:T(8,128)} %adj.3) | copy-start | bytes 393220
  0.0 4.8 %copy-start.1 = (f32[64,512]{1,0:T(8,128)S(1)}, f32[64,512]{1,0:T(8,128)}, u32[]{:S(2)}) copy-start(f32[64,512]{1,0:T(8,128)} %fwd.3) | copy-start | bytes 393220
  1.8 7.8 %collective-permute-start = (f32[80,512]{1,0:T(8,128)}, f32[80,512]{1,0:T(8,128)S(1)}, u32[]{:S(2)}, u32[]{:S(2)}) collective-permute-start(f32[80,512]{1,0:T(8,128)} %get-tuple-element.12.tpack), channel_id=1, source_target_pairs={{0,2},{1,3},{2,0},{3,1},{4,6},{5,7},{6,4},{7,5},{8,10},{9,11},{10,... | collective-permute-start | bytes 491528 | tf_op jit(solution)/shard_map/ppermute | solution.py:467
  4.8 4.8 %copy-start.3 = (f32[80,512]{1,0:T(8,128)S(1)}, f32[80,512]{1,0:T(8,128)}, u32[]{:S(2)}) copy-start(f32[80,512]{1,0:T(8,128)} %get-tuple-element.12.tpack) | copy-start | bytes 491524
  4.8 4.8 %collective-permute-start.1 = (f32[80,512]{1,0:T(8,128)}, f32[80,512]{1,0:T(8,128)S(1)}, u32[]{:S(2)}, u32[]{:S(2)}) collective-permute-start(f32[80,512]{1,0:T(8,128)} %get-tuple-element.13), channel_id=1, source_target_pairs={{0,1},{1,0},{2,3},{3,2},{4,5},{5,4},{6,7},{7,6},{8,9},{9,8},{10,11... | collective-permute-start | bytes 491528 | tf_op jit(solution)/shard_map/ppermute | solution.py:467
  23.2 1.4 %collective-permute-start.2 = (f32[8,8,32]{2,1,0:T(8,128)S(1)}, f32[8,8,32]{2,1,0:T(8,128)S(1)}, u32[]{:S(2)}, u32[]{:S(2)}) collective-permute-start(f32[8,8,32]{2,1,0:T(8,128)S(1)} %constant_dynamic-slice_fusion.3), channel_id=1, source_target_pairs={{0,1},{1,0},{2,3},{3,2},{4,5},{5,4},{6,7},{7,6},{8,9},{9,8},{10,11... | collective-permute-start | bytes 24584 | tf_op jit(solution)/shard_map/ppermute | solution.py:467
  24.7 3.8 %collective-permute-start.3 = (f32[4,8,32]{2,1,0:T(8,128)S(1)}, f32[4,8,32]{2,1,0:T(8,128)S(1)}, u32[]{:S(2)}, u32[]{:S(2)}) collective-permute-start(f32[4,8,32]{2,1,0:T(8,128)S(1)} %constant_dynamic-slice_fusion.2), channel_id=1, source_target_pairs={{0,2},{1,3},{2,0},{3,1},{4,6},{5,7},{6,4},{7,5},{8,10},{9,11},{10,... | collective-permute-start | bytes 12296 | tf_op jit(solution)/shard_map/ppermute | solution.py:467
  28.5 3.7 %collective-permute-start.4 = (f32[2,8,32]{2,1,0:T(8,128)S(1)}, f32[2,8,32]{2,1,0:T(8,128)S(1)}, u32[]{:S(2)}, u32[]{:S(2)}) collective-permute-start(f32[2,8,32]{2,1,0:T(8,128)S(1)} %constant_dynamic-slice_fusion.1), channel_id=1, source_target_pairs={{0,4},{4,0},{8,12},{12,8},{1,5},{5,1},{9,13},{13,9},{2,6},{6,2},{1... | collective-permute-start | bytes 6152 | tf_op jit(solution)/shard_map/ppermute | solution.py:467
  32.2 4.5 %collective-permute-start.5 = (f32[1,8,32]{2,1,0:T(8,128)S(1)}, f32[1,8,32]{2,1,0:T(8,128)S(1)}, u32[]{:S(2)}, u32[]{:S(2)}) collective-permute-start(f32[1,8,32]{2,1,0:T(8,128)S(1)} %constant_dynamic-slice_fusion), channel_id=1, source_target_pairs={{0,8},{4,12},{8,0},{12,4},{1,9},{5,13},{9,1},{13,5},{2,10},{6,14},... | collective-permute-start | bytes 3080 | tf_op jit(solution)/shard_map/ppermute | solution.py:467

commit v4 on v3

--- a/solution.py
+++ b/solution.py
@@ -17,6 +17,7 @@
 TJ = 256
 SUB = 16
 LANE = 128
+WIDE = 256
 
 SIN_C = None
 COS_C = None
@@ -78,7 +79,7 @@
 def target_table(adj, rows):
     hi = hi_part(adj)
     lo = adj - hi
-    return jnp.concatenate([hi, hi, lo] + [rows[a] for a, _ in SPLIT_PAIRS], axis=0)
+    return jnp.concatenate([rows[a] for a, _ in SPLIT_PAIRS] + [hi, hi, lo], axis=0)
 
 
 def source_rows(geo, center):
@@ -100,13 +101,12 @@
     xn = jnp.sum(x * n, axis=0, keepdims=True)
     prow = split3(rows8(-n, zero3, xn, zero1))
     qrow = split3(rows8(zero3, -x, zero1, ones))
-    zeros_w = jnp.zeros((192, x.shape[1]), F32)
-    tail = jnp.zeros((64, x.shape[1]), F32)
+    zeros = jnp.zeros((64, x.shape[1]), F32)
     cols = [
-        jnp.concatenate([rh, real - rh, rh, tail], axis=0),
-        jnp.concatenate([ih, imag - ih, ih, tail], axis=0),
-        jnp.concatenate([zeros_w] + [prow[b] for _, b in SPLIT_PAIRS], axis=0),
-        jnp.concatenate([zeros_w] + [qrow[b] for _, b in SPLIT_PAIRS], axis=0),
+        jnp.concatenate([zeros, rh, real - rh, rh], axis=0),
+        jnp.concatenate([zeros, ih, imag - ih, ih], axis=0),
+        jnp.concatenate([prow[b] for _, b in SPLIT_PAIRS] + [zeros], axis=0),
+        jnp.concatenate([qrow[b] for _, b in SPLIT_PAIRS] + [zeros], axis=0),
     ]
     return cols
 
@@ -170,12 +170,13 @@
         xi_ref[k, cols, :] = jnp.broadcast_to(xt[:, k : k + 1], (x.shape[1], LANE))
 
 
-def build_sources(geo, fwd, center, cols, right, xj_ref, fcol):
+def build_sources(geo, fwd, center, cols, right, rightn, xj_ref, fcol):
     x, n = source_rows(geo, center)
     xj_ref[:, cols] = jnp.concatenate([x, geo[6:7] * (TURNS * TURNS)] * 2, axis=0)
     tab = source_table(geo, fwd, x, n)
-    for k in range(4):
+    for k in range(2):
         right[k, :, cols] = tab[k].astype(BF16)
+        rightn[k, :, cols] = tab[k + 2].astype(BF16)
     sums = sum_rows(x, n)
     for k, part in enumerate((sums[1], sums[0], sums[2])):
         fcol[k, :, cols] = part
@@ -185,7 +186,7 @@
     return jnp.round(jnp.mean(geo[0:3], axis=1, keepdims=True))
 
 
-def run_tiles(count, place, left, right, xi_ref, xj_ref, frow, fcol, prod, abc, tsum, ssum):
+def run_tiles(count, place, left, right, rightn, xi_ref, xj_ref, frow, fcol, prod, abc, tsum, ssum):
     def start(t):
         i0, j0 = place(t)
         return pl.multiple_of(i0, TI), pl.multiple_of(j0, TJ)
@@ -194,7 +195,10 @@
         i0, j0 = start(t)
 
         def piece(k):
-            prod[slot, k] = dot(left[pl.ds(i0, TI), :], right[k, :, pl.ds(j0, TJ)])
+            if k < 2:
+                prod[slot, k] = dot(left[pl.ds(i0, TI), :], right[k, :, pl.ds(j0, TJ)])
+            else:
+                prod[slot, k] = dot(left[pl.ds(i0, TI), 0:128], rightn[k - 2, :, pl.ds(j0, TJ)])
 
         return [functools.partial(piece, k) for k in range(4)]
 
@@ -202,43 +206,52 @@
         i0, j0 = start(t)
 
         def piece(jj, ii):
-            lanes = pl.ds(j0 + jj * LANE, LANE)
-            here = slice(jj * LANE, (jj + 1) * LANE)
+            lanes = pl.ds(j0 + jj * WIDE, WIDE)
+            here = slice(jj * WIDE, (jj + 1) * WIDE)
             xj = [xj_ref[k : k + 1, lanes] for k in range(4)]
             rows = pl.ds(ii * SUB, SUB)
             xi = [xi_ref[k, pl.ds(i0 + ii * SUB, SUB), :] for k in range(3)]
+            xi = [jnp.concatenate([v, v], axis=1) for v in xi]
             pr = [prod[slot, k, rows, here] for k in range(4)]
-            for k, val in enumerate(pair_chunk(pr, xi, xj[0:3], xj[3])):
+            a, b, c = pair_chunk(pr, xi, xj[0:3], xj[3])
+            for k, val in ((0, a), (2, c)):
                 hi = val.astype(BF16)
-                abc[slot, 2 * k, rows, here] = hi
-                abc[slot, 2 * k + 1, rows, here] = (val - hi.astype(F32)).astype(BF16)
-
-        return [functools.partial(piece, jj, ii) for jj in range(TJ // LANE) for ii in range(TI // SUB)]
+                abc[slot, k, rows, here] = hi
+                abc[slot, k + 1, rows, here] = (val - hi.astype(F32)).astype(BF16)
+            abc[slot, 4, rows, here] = b.astype(BF16)
+
+        return [functools.partial(piece, jj, ii) for jj in range(TJ // WIDE) for ii in range(TI // SUB)]
 
     def sums(t, slot):
         i0, j0 = start(t)
         kept = [None, None]
 
-        def piece(k):
+        def piece(n, k, parts):
             fi = frow[k, :, pl.ds(i0, TI)]
-            hi, lo = abc[slot, 2 * k], abc[slot, 2 * k + 1]
-            add = dot(jnp.concatenate([fi, fi], axis=1), jnp.concatenate([hi, lo], axis=0))
-            kept[0] = add if k == 0 else kept[0] + add
-            if k == 2:
+            add = dot(
+                jnp.concatenate([fi] * len(parts), axis=1),
+                jnp.concatenate([abc[slot, p] for p in parts], axis=0),
+            )
+            kept[0] = add if n == 0 else kept[0] + add
+            if n == 2:
                 ssum[:, pl.ds(j0, TJ)] += kept[0]
 
-        def other(k):
+        def other(n, k, parts):
             fj = fcol[k, :, pl.ds(j0, TJ)]
-            hi, lo = abc[slot, 2 * k], abc[slot, 2 * k + 1]
-            add = dot(jnp.concatenate([fj, fj], axis=1), jnp.concatenate([hi, lo], axis=1), NT)
-            kept[1] = add if k == 0 else kept[1] + add
-            if k == 2:
+            add = dot(
+                jnp.concatenate([fj] * len(parts), axis=1),
+                jnp.concatenate([abc[slot, p] for p in parts], axis=1),
+                NT,
+            )
+            kept[1] = add if n == 0 else kept[1] + add
+            if n == 2:
                 tsum[:, pl.ds(i0, TI)] += kept[1]
 
-        return [functools.partial(f, k) for f in (piece, other) for k in range(3)]
+        groups = ((0, (0, 1)), (2, (2, 3)), (1, (4,)))
+        return [functools.partial(f, n, *g) for f in (piece, other) for n, g in enumerate(groups)]
 
     def interleave(vector, matrix):
-        gap = len(vector) // len(matrix)
+        gap = max(1, len(vector) // len(matrix))
         for n, todo in enumerate(vector):
             if n % gap == 0 and n // gap < len(matrix):
                 matrix[n // gap]()
@@ -280,19 +293,19 @@
         c.wait()
 
 
-def own_kernel(geo_ref, adj, fwd, left, right, xi_ref, tsum, ssum, xj_ref, frow, fcol, prod, abc):
+def own_kernel(geo_ref, adj, fwd, left, right, rightn, xi_ref, tsum, ssum, xj_ref, frow, fcol, prod, abc):
     width = geo_ref.shape[1]
     geo = geo_ref[...]
     center = center_of(geo)
     cols = pl.ds(0, width)
     build_targets(geo, adj[...], center, cols, left, xi_ref, frow)
-    build_sources(geo, fwd[...], center, cols, right, xj_ref, fcol)
+    build_sources(geo, fwd[...], center, cols, right, rightn, xj_ref, fcol)
     tsum[...] = jnp.zeros_like(tsum)
     ssum[...] = jnp.zeros_like(ssum)
     n_j = width // TJ
     run_tiles(
         (width // TI) * n_j, lambda t: ((t // n_j) * TI, lax.rem(t, n_j) * TJ),
-        left, right, xi_ref, xj_ref, frow, fcol, prod, abc, tsum, ssum,
+        left, right, rightn, xi_ref, xj_ref, frow, fcol, prod, abc, tsum, ssum,
     )
 
 
@@ -304,9 +317,9 @@
 
 
 def rest_kernel(
-    tpack, far, near, left_o, right_o, xi_o, tsum_o, ssum_o,
+    tpack, far, near, left_o, right_o, rightn_o, xi_o, tsum_o, ssum_o,
     out_ref,
-    left, right, xi_ref, xj_ref, frow, fcol, prod, abc, tsum, ssum,
+    left, right, rightn, xi_ref, xj_ref, frow, fcol, prod, abc, tsum, ssum,
 ):
     width = tpack.shape[1]
     geo = tpack[64:71]
@@ -314,6 +327,7 @@
     first, second = pl.ds(0, width), pl.ds(width, width)
     left[first, :] = left_o[...]
     right[:, :, first] = right_o[...]
+    rightn[:, :, first] = rightn_o[...]
     xi_ref[:, first, :] = xi_o[...]
     x, n = source_rows(geo, center)
     tsums, ssums = sum_rows(x, n * (1.0 / WAVENUM)), sum_rows(x, n)
@@ -326,7 +340,7 @@
     tsum[:, second] = jnp.zeros_like(tsum_o)
     ssum[:, second] = jnp.zeros_like(ssum_o)
     build_targets(far[64:71], far[0:64], center, second, left, xi_ref, frow)
-    build_sources(near[64:71], near[0:64], center, second, right, xj_ref, fcol)
+    build_sources(near[64:71], near[0:64], center, second, right, rightn, xj_ref, fcol)
 
     n_i, n_j = width // TI, width // TJ
     block = n_i * n_j
@@ -338,7 +352,7 @@
         j0 = jnp.where(b == 1, 0, width) + lax.rem(inner, n_j) * TJ
         return i0, j0
 
-    run_tiles(3 * block, place, left, right, xi_ref, xj_ref, frow, fcol, prod, abc, tsum, ssum)
+    run_tiles(3 * block, place, left, right, rightn, xi_ref, xj_ref, frow, fcol, prod, abc, tsum, ssum)
 
     def target_grad(g, cols):
         x = (g[0:3] - center) * TURNS
@@ -375,26 +389,20 @@
             gw = g * wt[s : s + 1]
             hi = hi_part(gw)
             here = jnp.where(low[s : s + 1] == low_iota, 1.0, 0.0).astype(BF16)
-            terms.append((place_of[s : s + 1], hi, gw - hi, here))
-    onehot = jnp.concatenate([t[3] for t in terms], axis=1)
-
-    def add_owner(step, _):
-        s0 = step * 16
-        cols = []
-        for where_to, hi, lo, _ in terms:
-            rows = []
-            for r in range(16):
-                mask = where_to == s0 + r
-                rows += [jnp.where(mask, hi, 0.0), jnp.where(mask, lo, 0.0)]
-            cols.append(jnp.concatenate(rows, axis=0).astype(BF16))
-        acc = dot(jnp.concatenate(cols, axis=1), onehot, NT).reshape(16, 16, cp_dev)
-        out_ref[pl.ds(s0, 16)] = acc[:, 0:8] + acc[:, 8:16]
-        return 0
-
-    if slots == 16:
-        add_owner(0, 0)
-    else:
-        lax.fori_loop(0, slots // 16, add_owner, 0)
+            both = jnp.concatenate([hi, gw - hi], axis=0).astype(BF16)
+            where_to = jnp.broadcast_to(place_of[s : s + 1].astype(F32), both.shape).astype(BF16)
+            terms.append((where_to, both, here))
+    onehot = jnp.concatenate([t[2] for t in terms], axis=1)
+    where_to = jnp.concatenate([t[0] for t in terms], axis=1)
+    both = jnp.concatenate([t[1] for t in terms], axis=1)
+
+    def add_owner(s0):
+        rows = [jnp.where(where_to == (s0 + r), both, jnp.zeros_like(both)) for r in range(16)]
+        acc = dot(jnp.concatenate(rows, axis=0), onehot, NT).reshape(16, 16, cp_dev)
+        out_ref[s0 : s0 + 16] = acc[:, 0:8] + acc[:, 8:16]
+
+    for s0 in range(0, slots, 16):
+        add_owner(s0)
 
 
 def shape(dims, kind):
@@ -402,7 +410,7 @@
 
 
 def tile_scratch():
-    return [pltpu.VMEM((2, 4, TI, TJ), F32), pltpu.VMEM((2, 6, TI, TJ), BF16)]
+    return [pltpu.VMEM((2, 4, TI, TJ), F32), pltpu.VMEM((2, 5, TI, TJ), BF16)]
 
 
 PARAMS = pltpu.CompilerParams(vmem_limit_bytes=20 * 1024 * 1024)
@@ -427,7 +435,8 @@
     return pl.pallas_call(
         own_kernel,
         out_shape=[
-            shape((width, 256), BF16), shape((4, 256, width), BF16), shape((3, width, LANE), F32),
+            shape((width, 256), BF16), shape((2, 256, width), BF16), shape((2, 128, width), BF16),
+            shape((3, width, LANE), F32),
             shape((32, width), F32), shape((32, width), F32),
         ],
         scratch_shapes=[
@@ -448,7 +457,8 @@
         out_shape=shape((slots, 8, cp_dev), F32),
         scratch_shapes=[
             pltpu.VMEM((total, 256), BF16),
-            pltpu.VMEM((4, 256, total), BF16),
+            pltpu.VMEM((2, 256, total), BF16),
+            pltpu.VMEM((2, 128, total), BF16),
             pltpu.VMEM((3, total, LANE), F32),
             pltpu.VMEM((8, total), F32),
             pltpu.VMEM((3, 32, total), BF16),

time: 37.5 us -> 35.8 us (0.955)
  Pallas kernels: 20.1 us -> 18.4 us
  waiting for transfers between devices: 7.49 us -> 6.76 us
  starting transfers between devices: 8.94 us -> 9.66 us
    pallas_call x1, Pallas kernels: 13.6 us -> 12.4 us  [rest_call(): pl.pallas_call(rest_kernel, out_shape=shape((slots, 8, cp_dev), F32), scr...]
    ppermute x6, waiting for transfers between devices: 7.49 us -> 6.76 us  [swap(): return lax.ppermute(x, axis, [(k, k ^ bit) for k in range(size)])]
    ppermute x6, starting transfers between devices: 8.94 us -> 9.66 us  [swap(): return lax.ppermute(x, axis, [(k, k ^ bit) for k in range(size)])]
    pallas_call x1, Pallas kernels: 4.79 us -> 4.3 us  [own_call(): pl.pallas_call(own_kernel, out_shape=[shape((width, 256), BF16), shape((2...]
  transfers between devices with their start and end apart: 6 -> 6, of which waited for: 4 -> 5; matrix products, arithmetic and copies ran while one was open for 0% -> 0% of each run, Pallas kernels for 13% -> 12%
where the time goes in v4:
time: 35.8 us; the launch traced here: 35.6 us
  Pallas kernels  18.4 us (51%)
  starting transfers between devices  9.66 us (27%)
  waiting for transfers between devices  6.76 us (19%)
  local copies, waits for them, and re-layouts  0.64 us (2%)
    pallas_call x1, Pallas kernels, rest_call(): pl.pallas_call(rest_kernel, out_shape=shape((slots, 8, cp_dev), F32), scr...  12.4 us
    ppermute x6, starting transfers between devices, swap(): return lax.ppermute(x, axis, [(k, k ^ bit) for k in range(size)])  9.66 us
    ppermute x6, waiting for transfers between devices, swap(): return lax.ppermute(x, axis, [(k, k ^ bit) for k in range(size)])  6.76 us
    pallas_call x1, Pallas kernels, own_call(): pl.pallas_call(own_kernel, out_shape=[shape((width, 256), BF16), shape((2...  4.3 us
    pallas_call x1, Pallas kernels, pack_call(): pl.pallas_call(pack_kernel, in_specs=[pl.BlockSpec(memory_space=pl.ANY)]...  1.78 us
  transfers between devices with their start and end apart: 6, of which 5 were waited for; matrix products, arithmetic and copies ran while one was open for 0% of the time, Pallas kernels for 12%

profile of v4, /device:TPU:0, one launch (start us, length us, event | category | flops | bytes accessed | tf_op | source)
XLA Modules:
  0.0 35.6 jit_solution(15553784558222365385)
XLA Ops:
  0.0 0.0 copy-start.2
  0.0 0.0 copy-start
  0.0 0.0 copy-start.1
  0.0 1.8 %pack.1 = (f32[80,512]{1,0:T(8,128)}, f32[80,512]{1,0:T(8,128)}) custom-call(f32[7,512]{1,0:T(8,128)} %geo_ref.1, f32[64,512]{1,0:T(8,128)} %adj.3, f32[64,512]{1,0:T(8,128)} %fwd.3, s32[4,512]{1,0:T(4,128)} %own.2, f32[4,512]{1,0:T(4,128)} %wt.1), custom_call_target="tpu_custom_call" | custom-call | tf_op jit(solution)/shard_map/pack/pallas_call | solution.py:421
  1.8 3.0 %collective-permute-start = (f32[80,512]{1,0:T(8,128)}, f32[80,512]{1,0:T(8,128)S(1)}, u32[]{:S(2)}, u32[]{:S(2)}) collective-permute-start(f32[80,512]{1,0:T(8,128)} %get-tuple-element.13.tpack), channel_id=1, source_target_pairs={{0,2},{1,3},{2,0},{3,1},{4,6},{5,7},{6,4},{7,5},{8,10},{9,11},{10,... | collective-permute-start | bytes 491528 | tf_op jit(solution)/shard_map/ppermute | solution.py:477
  4.8 0.0 copy-start.3
  4.8 0.0 collective-permute-start.1
  4.8 0.0 copy-done.2
  4.8 0.0 copy-done
  4.8 0.0 copy-done.1
  4.8 4.3 %own.3 = (bf16[512,256]{1,0:T(8,128)(2,1)S(1)}, bf16[2,256,512]{2,1,0:T(8,128)(2,1)S(1)}, bf16[2,128,512]{2,1,0:T(8,128)(2,1)S(1)}, f32[3,512,128]{2,1,0:T(8,128...) custom-call(f32[7,512]{1,0:T(8,128)S(1)} %copy-done.2, f32[64,512]{1,0:T(8,128)S(1)} %copy-done, f32[64,512]{1,0:T(8,128)S(1)} %copy-done.1), custom_call_target="tpu_custom_call" | custom-call | flops 4000000000 | bytes 4000000 | tf_op jit(solution)/shard_map/own/pallas_call | solution.py:435
  9.2 0.1 collective-permute-done.far
  9.2 0.0 collective-permute-done.1.near
  9.2 0.0 copy-done.3
  9.2 12.4 %rest.1 = f32[16,8,32]{2,1,0:T(8,128)S(1)} custom-call(f32[80,512]{1,0:T(8,128)S(1)} %copy-done.3, f32[80,512]{1,0:T(8,128)S(1)} %collective-permute-done.far, f32[80,512]{1,0:T(8,128)S(1)} %collective-permute-done.1.near, bf16[512,256]{1,0:T(8,128)(2,1)S(1)} %get-tuple-element.15.left_o, bf16[2,256,512]{2,1,0:T(8,128)(2,1)S(1)} %get-tuple-element.16.right_o, ...), custom_call_target="tpu_custom_call" | custom-call | flops 12000000000 | bytes 4000000 | tf_op jit(solution)/shard_map/rest/pallas_call | solution.py:455
  21.6 0.5 %collective-permute-start.2 = (f32[8,8,32]{2,1,0:T(8,128)S(1)}, f32[8,8,32]{2,1,0:T(8,128)S(1)}, u32[]{:S(2)}, u32[]{:S(2)}) collective-permute-start(f32[8,8,32]{2,1,0:T(8,128)S(1)} %constant_dynamic-slice_fusion.3), channel_id=1, source_target_pairs={{0,1},{1,0},{2,3},{3,2},{4,5},{5,4},{6,7},{7,6},{8,9},{9,8},{10,11... | collective-permute-start | bytes 24584 | tf_op jit(solution)/shard_map/ppermute | solution.py:477
  22.1 0.9 %collective-permute-done.2 = f32[8,8,32]{2,1,0:T(8,128)S(1)} collective-permute-done((f32[8,8,32]{2,1,0:T(8,128)S(1)}, f32[8,8,32]{2,1,0:T(8,128)S(1)}, u32[]{:S(2)}, u32[]{:S(2)}) %collective-permute-start.2) | collective-permute-done | bytes 8224 | tf_op jit(solution)/shard_map/ppermute | solution.py:477
  23.0 1.7 %collective-permute-start.3 = (f32[4,8,32]{2,1,0:T(8,128)S(1)}, f32[4,8,32]{2,1,0:T(8,128)S(1)}, u32[]{:S(2)}, u32[]{:S(2)}) collective-permute-start(f32[4,8,32]{2,1,0:T(8,128)S(1)} %constant_dynamic-slice_fusion.2), channel_id=1, source_target_pairs={{0,2},{1,3},{2,0},{3,1},{4,6},{5,7},{6,4},{7,5},{8,10},{9,11},{10,... | collective-permute-start | bytes 12296 | tf_op jit(solution)/shard_map/ppermute | solution.py:477
  24.7 2.1 %collective-permute-done.3 = f32[4,8,32]{2,1,0:T(8,128)S(1)} collective-permute-done((f32[4,8,32]{2,1,0:T(8,128)S(1)}, f32[4,8,32]{2,1,0:T(8,128)S(1)}, u32[]{:S(2)}, u32[]{:S(2)}) %collective-permute-start.3) | collective-permute-done | bytes 4128 | tf_op jit(solution)/shard_map/ppermute | solution.py:477
  26.8 1.7 %collective-permute-start.4 = (f32[2,8,32]{2,1,0:T(8,128)S(1)}, f32[2,8,32]{2,1,0:T(8,128)S(1)}, u32[]{:S(2)}, u32[]{:S(2)}) collective-permute-start(f32[2,8,32]{2,1,0:T(8,128)S(1)} %constant_dynamic-slice_fusion.1), channel_id=1, source_target_pairs={{0,4},{4,0},{8,12},{12,8},{1,5},{5,1},{9,13},{13,9},{2,6},{6,2},{1... | collective-permute-start | bytes 6152 | tf_op jit(solution)/shard_map/ppermute | solution.py:477
  28.5 1.9 %collective-permute-done.4 = f32[2,8,32]{2,1,0:T(8,128)S(1)} collective-permute-done((f32[2,8,32]{2,1,0:T(8,128)S(1)}, f32[2,8,32]{2,1,0:T(8,128)S(1)}, u32[]{:S(2)}, u32[]{:S(2)}) %collective-permute-start.4) | collective-permute-done | bytes 2080 | tf_op jit(solution)/shard_map/ppermute | solution.py:477
  30.5 2.7 %collective-permute-start.5 = (f32[1,8,32]{2,1,0:T(8,128)S(1)}, f32[1,8,32]{2,1,0:T(8,128)S(1)}, u32[]{:S(2)}, u32[]{:S(2)}) collective-permute-start(f32[1,8,32]{2,1,0:T(8,128)S(1)} %constant_dynamic-slice_fusion), channel_id=1, source_target_pairs={{0,8},{4,12},{8,0},{12,4},{1,9},{5,13},{9,1},{13,5},{2,10},{6,14},... | collective-permute-start | bytes 3080 | tf_op jit(solution)/shard_map/ppermute | solution.py:477
  33.2 1.8 %collective-permute-done.5 = f32[1,8,32]{2,1,0:T(8,128)S(1)} collective-permute-done((f32[1,8,32]{2,1,0:T(8,128)S(1)}, f32[1,8,32]{2,1,0:T(8,128)S(1)}, u32[]{:S(2)}, u32[]{:S(2)}) %collective-permute-start.5) | collective-permute-done | bytes 1056 | tf_op jit(solution)/shard_map/ppermute | solution.py:477
  35.0 0.6 %slice_bitcast_fusion = f32[6,32]{1,0:T(8,128)} fusion(f32[1,8,32]{2,1,0:T(8,128)S(1)} %dynamic-slice_add_fusion.3), kind=kLoop, calls=%fused_computation.3 | loop fusion | bytes 1536 | tf_op jit(solution)/shard_map/squeeze | solution.py:490
  (8 shorter events, 0.0 us)
Async XLA Ops:
  0.0 4.8 %copy-start.2 = (f32[7,512]{1,0:T(8,128)S(1)}, f32[7,512]{1,0:T(8,128)}, u32[]{:S(2)}) copy-start(f32[7,512]{1,0:T(8,128)} %geo_ref.1) | copy-start | bytes 43012
  0.0 4.8 %copy-start = (f32[64,512]{1,0:T(8,128)S(1)}, f32[64,512]{1,0:T(8,128)}, u32[]{:S(2)}) copy-start(f32[64,512]{1,0:T(8,128)} %adj.3) | copy-start | bytes 393220
  0.0 4.8 %copy-start.1 = (f32[64,512]{1,0:T(8,128)S(1)}, f32[64,512]{1,0:T(8,128)}, u32[]{:S(2)}) copy-start(f32[64,512]{1,0:T(8,128)} %fwd.3) | copy-start | bytes 393220
  1.8 7.4 %collective-permute-start = (f32[80,512]{1,0:T(8,128)}, f32[80,512]{1,0:T(8,128)S(1)}, u32[]{:S(2)}, u32[]{:S(2)}) collective-permute-start(f32[80,512]{1,0:T(8,128)} %get-tuple-element.13.tpack), channel_id=1, source_target_pairs={{0,2},{1,3},{2,0},{3,1},{4,6},{5,7},{6,4},{7,5},{8,10},{9,11},{10,... | collective-permute-start | bytes 491528 | tf_op jit(solution)/shard_map/ppermute | solution.py:477
  4.8 4.4 %copy-start.3 = (f32[80,512]{1,0:T(8,128)S(1)}, f32[80,512]{1,0:T(8,128)}, u32[]{:S(2)}) copy-start(f32[80,512]{1,0:T(8,128)} %get-tuple-element.13.tpack) | copy-start | bytes 491524
  4.8 4.4 %collective-permute-start.1 = (f32[80,512]{1,0:T(8,128)}, f32[80,512]{1,0:T(8,128)S(1)}, u32[]{:S(2)}, u32[]{:S(2)}) collective-permute-start(f32[80,512]{1,0:T(8,128)} %get-tuple-element.14), channel_id=1, source_target_pairs={{0,1},{1,0},{2,3},{3,2},{4,5},{5,4},{6,7},{7,6},{8,9},{9,8},{10,11... | collective-permute-start | bytes 491528 | tf_op jit(solution)/shard_map/ppermute | solution.py:477
  21.6 1.4 %collective-permute-start.2 = (f32[8,8,32]{2,1,0:T(8,128)S(1)}, f32[8,8,32]{2,1,0:T(8,128)S(1)}, u32[]{:S(2)}, u32[]{:S(2)}) collective-permute-start(f32[8,8,32]{2,1,0:T(8,128)S(1)} %constant_dynamic-slice_fusion.3), channel_id=1, source_target_pairs={{0,1},{1,0},{2,3},{3,2},{4,5},{5,4},{6,7},{7,6},{8,9},{9,8},{10,11... | collective-permute-start | bytes 24584 | tf_op jit(solution)/shard_map/ppermute | solution.py:477
  23.0 3.8 %collective-permute-start.3 = (f32[4,8,32]{2,1,0:T(8,128)S(1)}, f32[4,8,32]{2,1,0:T(8,128)S(1)}, u32[]{:S(2)}, u32[]{:S(2)}) collective-permute-start(f32[4,8,32]{2,1,0:T(8,128)S(1)} %constant_dynamic-slice_fusion.2), channel_id=1, source_target_pairs={{0,2},{1,3},{2,0},{3,1},{4,6},{5,7},{6,4},{7,5},{8,10},{9,11},{10,... | collective-permute-start | bytes 12296 | tf_op jit(solution)/shard_map/ppermute | solution.py:477
  26.8 3.7 %collective-permute-start.4 = (f32[2,8,32]{2,1,0:T(8,128)S(1)}, f32[2,8,32]{2,1,0:T(8,128)S(1)}, u32[]{:S(2)}, u32[]{:S(2)}) collective-permute-start(f32[2,8,32]{2,1,0:T(8,128)S(1)} %constant_dynamic-slice_fusion.1), channel_id=1, source_target_pairs={{0,4},{4,0},{8,12},{12,8},{1,5},{5,1},{9,13},{13,9},{2,6},{6,2},{1... | collective-permute-start | bytes 6152 | tf_op jit(solution)/shard_map/ppermute | solution.py:477
  30.5 4.5 %collective-permute-start.5 = (f32[1,8,32]{2,1,0:T(8,128)S(1)}, f32[1,8,32]{2,1,0:T(8,128)S(1)}, u32[]{:S(2)}, u32[]{:S(2)}) collective-permute-start(f32[1,8,32]{2,1,0:T(8,128)S(1)} %constant_dynamic-slice_fusion), channel_id=1, source_target_pairs={{0,8},{4,12},{8,0},{12,4},{1,9},{5,13},{9,1},{13,5},{2,10},{6,14},... | collective-permute-start | bytes 3080 | tf_op jit(solution)/shard_map/ppermute | solution.py:477

commit v5 on v4

--- a/solution.py
+++ b/solution.py
@@ -16,6 +16,7 @@
 TI = 256
 TJ = 256
 SUB = 16
+STEP = 8
 LANE = 128
 WIDE = 256
 
@@ -210,10 +211,13 @@
             here = slice(jj * WIDE, (jj + 1) * WIDE)
             xj = [xj_ref[k : k + 1, lanes] for k in range(4)]
             rows = pl.ds(ii * SUB, SUB)
-            xi = [xi_ref[k, pl.ds(i0 + ii * SUB, SUB), :] for k in range(3)]
-            xi = [jnp.concatenate([v, v], axis=1) for v in xi]
-            pr = [prod[slot, k, rows, here] for k in range(4)]
-            a, b, c = pair_chunk(pr, xi, xj[0:3], xj[3])
+            halves = []
+            for r in range(0, SUB, STEP):
+                xi = [xi_ref[k, pl.ds(i0 + ii * SUB + r, STEP), :] for k in range(3)]
+                xi = [jnp.concatenate([v, v], axis=1) for v in xi]
+                pr = [prod[slot, k, pl.ds(ii * SUB + r, STEP), here] for k in range(4)]
+                halves.append(pair_chunk(pr, xi, xj[0:3], xj[3]))
+            a, b, c = [jnp.concatenate(parts, axis=0) for parts in zip(*halves)]
             for k, val in ((0, a), (2, c)):
                 hi = val.astype(BF16)
                 abc[slot, k, rows, here] = hi
@@ -225,6 +229,7 @@
     def sums(t, slot):
         i0, j0 = start(t)
         kept = [None, None]
+        groups = ((0, (0,)), (0, (1,)), (2, (2,)), (2, (3,)), (1, (4,)))
 
         def piece(n, k, parts):
             fi = frow[k, :, pl.ds(i0, TI)]
@@ -233,7 +238,7 @@
                 jnp.concatenate([abc[slot, p] for p in parts], axis=0),
             )
             kept[0] = add if n == 0 else kept[0] + add
-            if n == 2:
+            if n == len(groups) - 1:
                 ssum[:, pl.ds(j0, TJ)] += kept[0]
 
         def other(n, k, parts):
@@ -244,17 +249,17 @@
                 NT,
             )
             kept[1] = add if n == 0 else kept[1] + add
-            if n == 2:
+            if n == len(groups) - 1:
                 tsum[:, pl.ds(i0, TI)] += kept[1]
 
-        groups = ((0, (0, 1)), (2, (2, 3)), (1, (4,)))
-        return [functools.partial(f, n, *g) for f in (piece, other) for n, g in enumerate(groups)]
+        return [functools.partial(f, n, *g) for n, g in enumerate(groups) for f in (piece, other)]
 
     def interleave(vector, matrix):
-        gap = max(1, len(vector) // len(matrix))
+        done = 0
         for n, todo in enumerate(vector):
-            if n % gap == 0 and n // gap < len(matrix):
-                matrix[n // gap]()
+            while done < len(matrix) and done * len(vector) <= n * len(matrix):
+                matrix[done]()
+                done += 1
             todo()
 
     last = count - 1
@@ -264,8 +269,18 @@
 
     def double(u, _):
         t = 2 * u
-        interleave(values(t, 0), products(t + 1, 1) + sums(jnp.maximum(t - 1, 0), 1))
-        interleave(values(t + 1, 1), products(jnp.minimum(t + 2, last), 0) + sums(t, 0))
+        def half(h, _):
+            @pl.when(h == 0)
+            def _():
+                interleave(values(t, 0), products(t + 1, 1) + sums(jnp.maximum(t - 1, 0), 1))
+
+            @pl.when(h == 1)
+            def _():
+                interleave(values(t + 1, 1), products(jnp.minimum(t + 2, last), 0) + sums(t, 0))
+
+            return 0
+
+        lax.fori_loop(0, 2, half, 0)
         return 0
 
     lax.fori_loop(0, count // 2, double, 0)

time: 35.8 us -> 33.9 us (0.947)
  Pallas kernels: 18.4 us -> 15.8 us
  waiting for transfers between devices: 6.76 us -> 7.59 us
    pallas_call x1, Pallas kernels: 12.4 us -> 10.6 us  [rest_call(): pl.pallas_call(rest_kernel, out_shape=shape((slots, 8, cp_dev), F32), scr...]
    pallas_call x1, Pallas kernels: 4.3 us -> 3.44 us  [own_call(): pl.pallas_call(own_kernel, out_shape=[shape((width, 256), BF16), shape((2...]
    ppermute x6, waiting for transfers between devices: 6.76 us -> 7.59 us  [swap(): return lax.ppermute(x, axis, [(k, k ^ bit) for k in range(size)])]
  transfers between devices with their start and end apart: 6 -> 6, of which waited for: 5 -> 5; matrix products, arithmetic and copies ran while one was open for 0% -> 0% of each run, Pallas kernels for 12% -> 10%
where the time goes in v5:
time: 33.9 us; the launch traced here: 33.7 us
  Pallas kernels  15.8 us (47%)
  starting transfers between devices  9.56 us (28%)
  waiting for transfers between devices  7.59 us (22%)
  local copies, waits for them, and re-layouts  0.64 us (2%)
    pallas_call x1, Pallas kernels, rest_call(): pl.pallas_call(rest_kernel, out_shape=shape((slots, 8, cp_dev), F32), scr...  10.6 us
    ppermute x6, starting transfers between devices, swap(): return lax.ppermute(x, axis, [(k, k ^ bit) for k in range(size)])  9.56 us
    ppermute x6, waiting for transfers between devices, swap(): return lax.ppermute(x, axis, [(k, k ^ bit) for k in range(size)])  7.59 us
    pallas_call x1, Pallas kernels, own_call(): pl.pallas_call(own_kernel, out_shape=[shape((width, 256), BF16), shape((2...  3.44 us
    pallas_call x1, Pallas kernels, pack_call(): pl.pallas_call(pack_kernel, in_specs=[pl.BlockSpec(memory_space=pl.ANY)]...  1.78 us
  transfers between devices with their start and end apart: 6, of which 5 were waited for; matrix products, arithmetic and copies ran while one was open for 0% of the time, Pallas kernels for 10%

profile of v5, /device:TPU:0, one launch (start us, length us, event | category | flops | bytes accessed | tf_op | source)
XLA Modules:
  0.0 33.7 jit_solution(16642561271635340798)
XLA Ops:
  0.0 0.0 copy-start.2
  0.0 0.0 copy-start
  0.0 0.0 copy-start.1
  0.0 1.8 %pack.1 = (f32[80,512]{1,0:T(8,128)}, f32[80,512]{1,0:T(8,128)}) custom-call(f32[7,512]{1,0:T(8,128)} %geo_ref.1, f32[64,512]{1,0:T(8,128)} %adj.3, f32[64,512]{1,0:T(8,128)} %fwd.3, s32[4,512]{1,0:T(4,128)} %own.2, f32[4,512]{1,0:T(4,128)} %wt.1), custom_call_target="tpu_custom_call" | custom-call | tf_op jit(solution)/shard_map/pack/pallas_call | solution.py:436
  1.8 3.0 %collective-permute-start = (f32[80,512]{1,0:T(8,128)}, f32[80,512]{1,0:T(8,128)S(1)}, u32[]{:S(2)}, u32[]{:S(2)}) collective-permute-start(f32[80,512]{1,0:T(8,128)} %get-tuple-element.13.tpack), channel_id=1, source_target_pairs={{0,2},{1,3},{2,0},{3,1},{4,6},{5,7},{6,4},{7,5},{8,10},{9,11},{10,... | collective-permute-start | bytes 491528 | tf_op jit(solution)/shard_map/ppermute | solution.py:492
  4.8 0.0 copy-start.3
  4.8 0.0 collective-permute-start.1
  4.8 0.0 copy-done.2
  4.8 0.0 copy-done
  4.8 0.0 copy-done.1
  4.8 3.4 %own.3 = (bf16[512,256]{1,0:T(8,128)(2,1)S(1)}, bf16[2,256,512]{2,1,0:T(8,128)(2,1)S(1)}, bf16[2,128,512]{2,1,0:T(8,128)(2,1)S(1)}, f32[3,512,128]{2,1,0:T(8,128...) custom-call(f32[7,512]{1,0:T(8,128)S(1)} %copy-done.2, f32[64,512]{1,0:T(8,128)S(1)} %copy-done, f32[64,512]{1,0:T(8,128)S(1)} %copy-done.1), custom_call_target="tpu_custom_call" | custom-call | flops 4000000000 | bytes 4000000 | tf_op jit(solution)/shard_map/own/pallas_call | solution.py:450
  8.3 0.9 %collective-permute-done.far = f32[80,512]{1,0:T(8,128)S(1)} collective-permute-done((f32[80,512]{1,0:T(8,128)}, f32[80,512]{1,0:T(8,128)S(1)}, u32[]{:S(2)}, u32[]{:S(2)}) %collective-permute-start) | collective-permute-done | bytes 163872 | tf_op jit(solution)/shard_map/ppermute | solution.py:492
  9.2 0.0 collective-permute-done.1.near
  9.2 0.0 copy-done.3
  9.2 10.6 %rest.1 = f32[16,8,32]{2,1,0:T(8,128)S(1)} custom-call(f32[80,512]{1,0:T(8,128)S(1)} %copy-done.3, f32[80,512]{1,0:T(8,128)S(1)} %collective-permute-done.far, f32[80,512]{1,0:T(8,128)S(1)} %collective-permute-done.1.near, bf16[512,256]{1,0:T(8,128)(2,1)S(1)} %get-tuple-element.15.left_o, bf16[2,256,512]{2,1,0:T(8,128)(2,1)S(1)} %get-tuple-element.16.right_o, ...), custom_call_target="tpu_custom_call" | custom-call | flops 12000000000 | bytes 4000000 | tf_op jit(solution)/shard_map/rest/pallas_call | solution.py:470
  19.8 0.1 collective-permute-start.2
  19.9 1.2 %collective-permute-done.2 = f32[8,8,32]{2,1,0:T(8,128)S(1)} collective-permute-done((f32[8,8,32]{2,1,0:T(8,128)S(1)}, f32[8,8,32]{2,1,0:T(8,128)S(1)}, u32[]{:S(2)}, u32[]{:S(2)}) %collective-permute-start.2) | collective-permute-done | bytes 8224 | tf_op jit(solution)/shard_map/ppermute | solution.py:492
  21.1 1.8 %collective-permute-start.3 = (f32[4,8,32]{2,1,0:T(8,128)S(1)}, f32[4,8,32]{2,1,0:T(8,128)S(1)}, u32[]{:S(2)}, u32[]{:S(2)}) collective-permute-start(f32[4,8,32]{2,1,0:T(8,128)S(1)} %constant_dynamic-slice_fusion.2), channel_id=1, source_target_pairs={{0,2},{1,3},{2,0},{3,1},{4,6},{5,7},{6,4},{7,5},{8,10},{9,11},{10,... | collective-permute-start | bytes 12296 | tf_op jit(solution)/shard_map/ppermute | solution.py:492
  22.9 2.0 %collective-permute-done.3 = f32[4,8,32]{2,1,0:T(8,128)S(1)} collective-permute-done((f32[4,8,32]{2,1,0:T(8,128)S(1)}, f32[4,8,32]{2,1,0:T(8,128)S(1)}, u32[]{:S(2)}, u32[]{:S(2)}) %collective-permute-start.3) | collective-permute-done | bytes 4128 | tf_op jit(solution)/shard_map/ppermute | solution.py:492
  24.9 1.8 %collective-permute-start.4 = (f32[2,8,32]{2,1,0:T(8,128)S(1)}, f32[2,8,32]{2,1,0:T(8,128)S(1)}, u32[]{:S(2)}, u32[]{:S(2)}) collective-permute-start(f32[2,8,32]{2,1,0:T(8,128)S(1)} %constant_dynamic-slice_fusion.1), channel_id=1, source_target_pairs={{0,4},{4,0},{8,12},{12,8},{1,5},{5,1},{9,13},{13,9},{2,6},{6,2},{1... | collective-permute-start | bytes 6152 | tf_op jit(solution)/shard_map/ppermute | solution.py:492
  26.8 1.8 %collective-permute-done.4 = f32[2,8,32]{2,1,0:T(8,128)S(1)} collective-permute-done((f32[2,8,32]{2,1,0:T(8,128)S(1)}, f32[2,8,32]{2,1,0:T(8,128)S(1)}, u32[]{:S(2)}, u32[]{:S(2)}) %collective-permute-start.4) | collective-permute-done | bytes 2080 | tf_op jit(solution)/shard_map/ppermute | solution.py:492
  28.6 2.8 %collective-permute-start.5 = (f32[1,8,32]{2,1,0:T(8,128)S(1)}, f32[1,8,32]{2,1,0:T(8,128)S(1)}, u32[]{:S(2)}, u32[]{:S(2)}) collective-permute-start(f32[1,8,32]{2,1,0:T(8,128)S(1)} %constant_dynamic-slice_fusion), channel_id=1, source_target_pairs={{0,8},{4,12},{8,0},{12,4},{1,9},{5,13},{9,1},{13,5},{2,10},{6,14},... | collective-permute-start | bytes 3080 | tf_op jit(solution)/shard_map/ppermute | solution.py:492
  31.5 1.7 %collective-permute-done.5 = f32[1,8,32]{2,1,0:T(8,128)S(1)} collective-permute-done((f32[1,8,32]{2,1,0:T(8,128)S(1)}, f32[1,8,32]{2,1,0:T(8,128)S(1)}, u32[]{:S(2)}, u32[]{:S(2)}) %collective-permute-start.5) | collective-permute-done | bytes 1056 | tf_op jit(solution)/shard_map/ppermute | solution.py:492
  33.1 0.6 %slice_bitcast_fusion = f32[6,32]{1,0:T(8,128)} fusion(f32[1,8,32]{2,1,0:T(8,128)S(1)} %dynamic-slice_add_fusion.3), kind=kLoop, calls=%fused_computation.3 | loop fusion | bytes 1536 | tf_op jit(solution)/shard_map/squeeze | solution.py:505
  (8 shorter events, 0.0 us)
Async XLA Ops:
  0.0 4.8 %copy-start.2 = (f32[7,512]{1,0:T(8,128)S(1)}, f32[7,512]{1,0:T(8,128)}, u32[]{:S(2)}) copy-start(f32[7,512]{1,0:T(8,128)} %geo_ref.1) | copy-start | bytes 43012
  0.0 4.8 %copy-start = (f32[64,512]{1,0:T(8,128)S(1)}, f32[64,512]{1,0:T(8,128)}, u32[]{:S(2)}) copy-start(f32[64,512]{1,0:T(8,128)} %adj.3) | copy-start | bytes 393220
  0.0 4.8 %copy-start.1 = (f32[64,512]{1,0:T(8,128)S(1)}, f32[64,512]{1,0:T(8,128)}, u32[]{:S(2)}) copy-start(f32[64,512]{1,0:T(8,128)} %fwd.3) | copy-start | bytes 393220
  1.8 7.4 %collective-permute-start = (f32[80,512]{1,0:T(8,128)}, f32[80,512]{1,0:T(8,128)S(1)}, u32[]{:S(2)}, u32[]{:S(2)}) collective-permute-start(f32[80,512]{1,0:T(8,128)} %get-tuple-element.13.tpack), channel_id=1, source_target_pairs={{0,2},{1,3},{2,0},{3,1},{4,6},{5,7},{6,4},{7,5},{8,10},{9,11},{10,... | collective-permute-start | bytes 491528 | tf_op jit(solution)/shard_map/ppermute | solution.py:492
  4.8 4.4 %copy-start.3 = (f32[80,512]{1,0:T(8,128)S(1)}, f32[80,512]{1,0:T(8,128)}, u32[]{:S(2)}) copy-start(f32[80,512]{1,0:T(8,128)} %get-tuple-element.13.tpack) | copy-start | bytes 491524
  4.8 4.4 %collective-permute-start.1 = (f32[80,512]{1,0:T(8,128)}, f32[80,512]{1,0:T(8,128)S(1)}, u32[]{:S(2)}, u32[]{:S(2)}) collective-permute-start(f32[80,512]{1,0:T(8,128)} %get-tuple-element.14), channel_id=1, source_target_pairs={{0,1},{1,0},{2,3},{3,2},{4,5},{5,4},{6,7},{7,6},{8,9},{9,8},{10,11... | collective-permute-start | bytes 491528 | tf_op jit(solution)/shard_map/ppermute | solution.py:492
  19.8 1.3 %collective-permute-start.2 = (f32[8,8,32]{2,1,0:T(8,128)S(1)}, f32[8,8,32]{2,1,0:T(8,128)S(1)}, u32[]{:S(2)}, u32[]{:S(2)}) collective-permute-start(f32[8,8,32]{2,1,0:T(8,128)S(1)} %constant_dynamic-slice_fusion.3), channel_id=1, source_target_pairs={{0,1},{1,0},{2,3},{3,2},{4,5},{5,4},{6,7},{7,6},{8,9},{9,8},{10,11... | collective-permute-start | bytes 24584 | tf_op jit(solution)/shard_map/ppermute | solution.py:492
  21.1 3.8 %collective-permute-start.3 = (f32[4,8,32]{2,1,0:T(8,128)S(1)}, f32[4,8,32]{2,1,0:T(8,128)S(1)}, u32[]{:S(2)}, u32[]{:S(2)}) collective-permute-start(f32[4,8,32]{2,1,0:T(8,128)S(1)} %constant_dynamic-slice_fusion.2), channel_id=1, source_target_pairs={{0,2},{1,3},{2,0},{3,1},{4,6},{5,7},{6,4},{7,5},{8,10},{9,11},{10,... | collective-permute-start | bytes 12296 | tf_op jit(solution)/shard_map/ppermute | solution.py:492
  24.9 3.7 %collective-permute-start.4 = (f32[2,8,32]{2,1,0:T(8,128)S(1)}, f32[2,8,32]{2,1,0:T(8,128)S(1)}, u32[]{:S(2)}, u32[]{:S(2)}) collective-permute-start(f32[2,8,32]{2,1,0:T(8,128)S(1)} %constant_dynamic-slice_fusion.1), channel_id=1, source_target_pairs={{0,4},{4,0},{8,12},{12,8},{1,5},{5,1},{9,13},{13,9},{2,6},{6,2},{1... | collective-permute-start | bytes 6152 | tf_op jit(solution)/shard_map/ppermute | solution.py:492
  28.6 4.5 %collective-permute-start.5 = (f32[1,8,32]{2,1,0:T(8,128)S(1)}, f32[1,8,32]{2,1,0:T(8,128)S(1)}, u32[]{:S(2)}, u32[]{:S(2)}) collective-permute-start(f32[1,8,32]{2,1,0:T(8,128)S(1)} %constant_dynamic-slice_fusion), channel_id=1, source_target_pairs={{0,8},{4,12},{8,0},{12,4},{1,9},{5,13},{9,1},{13,5},{2,10},{6,14},... | collective-permute-start | bytes 3080 | tf_op jit(solution)/shard_map/ppermute | solution.py:492

commit v6 on v5

--- a/solution.py
+++ b/solution.py
@@ -166,9 +166,12 @@
     sums = sum_rows(x, m)
     for k in range(3):
         frow[k, :, cols] = sums[k]
-    xt = jnp.concatenate([x, m, m[0:2]], axis=0).T
+    row = lax.broadcasted_iota(jnp.int32, (128, 3 * LANE), 0)
+    axis = lax.broadcasted_iota(jnp.int32, (128, 3 * LANE), 1) // LANE
+    pick = (row == axis) | (row == axis + 16) | (row == axis + 32)
+    spread = dot(left[cols, 0:128], jnp.where(pick, 1.0, 0.0).astype(BF16))
     for k in range(3):
-        xi_ref[k, cols, :] = jnp.broadcast_to(xt[:, k : k + 1], (x.shape[1], LANE))
+        xi_ref[k, cols, :] = spread[:, k * LANE : (k + 1) * LANE]
 
 
 def build_sources(geo, fwd, center, cols, right, rightn, xj_ref, fcol):
@@ -308,18 +311,27 @@
         c.wait()
 
 
-def own_kernel(geo_ref, adj, fwd, left, right, rightn, xi_ref, tsum, ssum, xj_ref, frow, fcol, prod, abc):
+def tile_place(n_j):
+    return lambda t: ((t // n_j) * TI, lax.rem(t, n_j) * TJ)
+
+
+def own_kernel(
+    geo_ref, adj, fwd, near,
+    right, rightn, xj_ref, fcol, tsum, ssum,
+    left, xi_ref, frow, prod, abc,
+):
     width = geo_ref.shape[1]
     geo = geo_ref[...]
     center = center_of(geo)
-    cols = pl.ds(0, width)
-    build_targets(geo, adj[...], center, cols, left, xi_ref, frow)
-    build_sources(geo, fwd[...], center, cols, right, rightn, xj_ref, fcol)
+    first, second = pl.ds(0, width), pl.ds(width, width)
+    build_targets(geo, adj[...], center, first, left, xi_ref, frow)
+    build_sources(geo, fwd[...], center, first, right, rightn, xj_ref, fcol)
+    build_sources(near[64:71], near[0:64], center, second, right, rightn, xj_ref, fcol)
     tsum[...] = jnp.zeros_like(tsum)
     ssum[...] = jnp.zeros_like(ssum)
-    n_j = width // TJ
+    n_j = 2 * width // TJ
     run_tiles(
-        (width // TI) * n_j, lambda t: ((t // n_j) * TI, lax.rem(t, n_j) * TJ),
+        (width // TI) * n_j, tile_place(n_j),
         left, right, rightn, xi_ref, xj_ref, frow, fcol, prod, abc, tsum, ssum,
     )
 
@@ -332,47 +344,27 @@
 
 
 def rest_kernel(
-    tpack, far, near, left_o, right_o, rightn_o, xi_o, tsum_o, ssum_o,
+    tpack, far, near, right, rightn, xj_ref, fcol, tsum_o, ssum_o,
     out_ref,
-    left, right, rightn, xi_ref, xj_ref, frow, fcol, prod, abc, tsum, ssum,
+    left, xi_ref, frow, prod, abc, tsum, ssum,
 ):
     width = tpack.shape[1]
-    geo = tpack[64:71]
+    geo, geo_s = tpack[64:71], near[64:71]
     center = center_of(geo)
     first, second = pl.ds(0, width), pl.ds(width, width)
-    left[first, :] = left_o[...]
-    right[:, :, first] = right_o[...]
-    rightn[:, :, first] = rightn_o[...]
-    xi_ref[:, first, :] = xi_o[...]
-    x, n = source_rows(geo, center)
-    tsums, ssums = sum_rows(x, n * (1.0 / WAVENUM)), sum_rows(x, n)
-    for k in range(3):
-        frow[k, :, first] = tsums[k]
-        fcol[k, :, first] = ssums[(1, 0, 2)[k]]
-    xj_ref[:, first] = jnp.concatenate([x, geo[6:7] * (TURNS * TURNS)] * 2, axis=0)
-    tsum[:, first] = tsum_o[...]
-    ssum[:, first] = ssum_o[...]
-    tsum[:, second] = jnp.zeros_like(tsum_o)
-    ssum[:, second] = jnp.zeros_like(ssum_o)
-    build_targets(far[64:71], far[0:64], center, second, left, xi_ref, frow)
-    build_sources(near[64:71], near[0:64], center, second, right, rightn, xj_ref, fcol)
-
-    n_i, n_j = width // TI, width // TJ
-    block = n_i * n_j
-
-    def place(t):
-        b = t // block
-        inner = lax.rem(t, block)
-        i0 = jnp.where(b > 0, width, 0) + (inner // n_j) * TI
-        j0 = jnp.where(b == 1, 0, width) + lax.rem(inner, n_j) * TJ
-        return i0, j0
-
-    run_tiles(3 * block, place, left, right, rightn, xi_ref, xj_ref, frow, fcol, prod, abc, tsum, ssum)
-
-    def target_grad(g, cols):
+    tsum[...] = jnp.zeros_like(tsum)
+    ssum[...] = ssum_o[...]
+    build_targets(far[64:71], far[0:64], center, first, left, xi_ref, frow)
+    n_j = 2 * width // TJ
+    run_tiles(
+        (width // TI) * n_j, tile_place(n_j),
+        left, right, rightn, xi_ref, xj_ref, frow, fcol, prod, abc, tsum, ssum,
+    )
+
+    def target_grad(g, acc):
         x = (g[0:3] - center) * TURNS
         m = g[3:6] * (1.0 / WAVENUM)
-        sb, an, sc = read_sums(tsum[:, cols])
+        sb, an, sc = read_sums(acc)
         gx = (2.0 * math.pi) * (x * sc[3:4] - sc[0:3]) + an - m * sb[3:4]
         gn = sb[0:3] - x * sb[3:4]
         return gx * TURNS, gn * (1.0 / WAVENUM)
@@ -385,23 +377,24 @@
         gn = sa[0:3] - x * sa[3:4]
         return gx * TURNS, gn
 
-    t_own, s_own = target_grad(geo, first), source_grad(geo, first)
+    t_own, s_own = target_grad(geo, tsum_o[...]), source_grad(geo, first)
     zero2 = jnp.zeros((2, width), F32)
     grads = [
         (t_own[0] + s_own[0], t_own[1] + s_own[1]),
-        target_grad(far[64:71], second),
-        source_grad(near[64:71], second),
+        target_grad(far[64:71], tsum[...]),
+        source_grad(geo_s, second),
     ]
     slots, _, cp_dev = out_ref.shape
-    low_iota = lax.broadcasted_iota(jnp.int32, (cp_dev, width), 0)
+    low_iota = lax.broadcasted_iota(jnp.int32, (2 * cp_dev, width), 0)
     terms = []
-    for (gx, gn), pack in zip(grads, (tpack, far, near)):
+    for (gx, gn), rows in zip(grads, (tpack[72:80], far[72:80], near[72:80])):
+        own_of, wt_of = rows[4:8].astype(jnp.int32), rows[0:4]
         g = jnp.concatenate([gx, gn, zero2], axis=0)
-        own, wt = pack[76:80].astype(jnp.int32), pack[72:76]
-        place_of = reverse_bits(own // cp_dev, slots.bit_length() - 1)
-        low = lax.rem(own, cp_dev)
+        place_of = reverse_bits(own_of // cp_dev, slots.bit_length() - 1)
+        low = lax.rem(own_of, cp_dev) + (place_of & 1) * cp_dev
+        place_of = place_of >> 1
         for s in range(4):
-            gw = g * wt[s : s + 1]
+            gw = g * wt_of[s : s + 1]
             hi = hi_part(gw)
             here = jnp.where(low[s : s + 1] == low_iota, 1.0, 0.0).astype(BF16)
             both = jnp.concatenate([hi, gw - hi], axis=0).astype(BF16)
@@ -412,9 +405,12 @@
     both = jnp.concatenate([t[1] for t in terms], axis=1)
 
     def add_owner(s0):
-        rows = [jnp.where(where_to == (s0 + r), both, jnp.zeros_like(both)) for r in range(16)]
-        acc = dot(jnp.concatenate(rows, axis=0), onehot, NT).reshape(16, 16, cp_dev)
-        out_ref[s0 : s0 + 16] = acc[:, 0:8] + acc[:, 8:16]
+        rows = [jnp.where(where_to == (s0 // 2 + r), both, jnp.zeros_like(both)) for r in range(8)]
+        acc = dot(jnp.concatenate(rows, axis=0), onehot, NT).reshape(8, 16, 2 * cp_dev)
+        acc = acc[:, 0:8] + acc[:, 8:16]
+        for r in range(8):
+            out_ref[s0 + 2 * r] = acc[r, :, 0:cp_dev]
+            out_ref[s0 + 2 * r + 1] = acc[r, :, cp_dev:]
 
     for s0 in range(0, slots, 16):
         add_owner(s0)
@@ -445,44 +441,36 @@
     )(geo, adj, fwd, own, wt)
 
 
-def own_call(geo, adj, fwd):
-    width = geo.shape[1]
+def target_scratch(width):
+    return [
+        pltpu.VMEM((width, 256), BF16), pltpu.VMEM((3, width, LANE), F32), pltpu.VMEM((3, 32, width), BF16)
+    ] + tile_scratch()
+
+
+def own_call(args):
+    width = args[0].shape[1]
+    total = 2 * width
     return pl.pallas_call(
         own_kernel,
         out_shape=[
-            shape((width, 256), BF16), shape((2, 256, width), BF16), shape((2, 128, width), BF16),
-            shape((3, width, LANE), F32),
-            shape((32, width), F32), shape((32, width), F32),
+            shape((2, 256, total), BF16), shape((2, 128, total), BF16), shape((8, total), F32),
+            shape((3, 32, total), BF16), shape((32, width), F32), shape((32, total), F32),
         ],
-        scratch_shapes=[
-            pltpu.VMEM((8, width), F32), pltpu.VMEM((3, 32, width), BF16), pltpu.VMEM((3, 32, width), BF16)
-        ]
-        + tile_scratch(),
+        scratch_shapes=target_scratch(width),
         compiler_params=PARAMS,
-        cost_estimate=pl.CostEstimate(flops=4 * 10**9, bytes_accessed=4 * 10**6, transcendentals=0),
+        cost_estimate=pl.CostEstimate(flops=8 * 10**9, bytes_accessed=4 * 10**6, transcendentals=0),
         name="own",
-    )(geo, adj, fwd)
+    )(*args)
 
 
 def rest_call(args, slots, cp_dev):
     width = args[0].shape[1]
-    total = 2 * width
     return pl.pallas_call(
         rest_kernel,
         out_shape=shape((slots, 8, cp_dev), F32),
-        scratch_shapes=[
-            pltpu.VMEM((total, 256), BF16),
-            pltpu.VMEM((2, 256, total), BF16),
-            pltpu.VMEM((2, 128, total), BF16),
-            pltpu.VMEM((3, total, LANE), F32),
-            pltpu.VMEM((8, total), F32),
-            pltpu.VMEM((3, 32, total), BF16),
-            pltpu.VMEM((3, 32, total), BF16),
-        ]
-        + tile_scratch()
-        + [pltpu.VMEM((32, total), F32), pltpu.VMEM((32, total), F32)],
+        scratch_shapes=target_scratch(width) + [pltpu.VMEM((32, width), F32), pltpu.VMEM((32, 2 * width), F32)],
         compiler_params=PARAMS,
-        cost_estimate=pl.CostEstimate(flops=12 * 10**9, bytes_accessed=4 * 10**6, transcendentals=0),
+        cost_estimate=pl.CostEstimate(flops=8 * 10**9, bytes_accessed=4 * 10**6, transcendentals=0),
         name="rest",
     )(*args)
 
@@ -508,9 +496,9 @@
 def on_device(cp_dev, geometry, adjoint, forward, owner_map, owner_weight):
     slots = lax.axis_size("row") * lax.axis_size("loop")
     tpack, spack = pack_call(geometry, adjoint, forward, owner_map, owner_weight)
+    near = swap(spack, "loop", 1)
     far = swap(tpack, "loop", 2)
-    near = swap(spack, "loop", 1)
-    tables = own_call(geometry, adjoint, forward)
+    tables = own_call((geometry, adjoint, forward, near))
     return halving(rest_call((tpack, far, near, *tables), slots, cp_dev))
 
 

time: 33.9 us -> 33.1 us (0.976)
  starting transfers between devices: 9.56 us -> 9.11 us
  waiting for transfers between devices: 7.59 us -> 7.22 us
    pallas_call x1, Pallas kernels: 3.44 us -> 6.64 us  [own_call(): pl.pallas_call(own_kernel, out_shape=[shape((2, 256, total), BF16), shape...]
    pallas_call x1, Pallas kernels: 10.6 us -> 7.46 us  [rest_call(): pl.pallas_call(rest_kernel, out_shape=shape((slots, 8, cp_dev), F32), scr...]
    ppermute x6, starting transfers between devices: 9.56 us -> 9.11 us  [swap(): return lax.ppermute(x, axis, [(k, k ^ bit) for k in range(size)])]
    ppermute x6, waiting for transfers between devices: 7.59 us -> 7.22 us  [swap(): return lax.ppermute(x, axis, [(k, k ^ bit) for k in range(size)])]
  transfers between devices with their start and end apart: 6 -> 6, of which waited for: 5 -> 4; matrix products, arithmetic and copies ran while one was open for 0% -> 0% of each run, Pallas kernels for 10% -> 20%
where the time goes in v6:
time: 33.1 us; the launch traced here: 32.9 us
  Pallas kernels  15.9 us (48%)
  starting transfers between devices  9.11 us (28%)
  waiting for transfers between devices  7.22 us (22%)
  local copies, waits for them, and re-layouts  0.64 us (2%)
    ppermute x6, starting transfers between devices, swap(): return lax.ppermute(x, axis, [(k, k ^ bit) for k in range(size)])  9.11 us
    pallas_call x1, Pallas kernels, rest_call(): pl.pallas_call(rest_kernel, out_shape=shape((slots, 8, cp_dev), F32), scr...  7.46 us
    ppermute x6, waiting for transfers between devices, swap(): return lax.ppermute(x, axis, [(k, k ^ bit) for k in range(size)])  7.22 us
    pallas_call x1, Pallas kernels, own_call(): pl.pallas_call(own_kernel, out_shape=[shape((2, 256, total), BF16), shape...  6.64 us
    pallas_call x1, Pallas kernels, pack_call(): pl.pallas_call(pack_kernel, in_specs=[pl.BlockSpec(memory_space=pl.ANY)]...  1.78 us
  transfers between devices with their start and end apart: 6, of which 4 were waited for; matrix products, arithmetic and copies ran while one was open for 0% of the time, Pallas kernels for 20%

profile of v6, /device:TPU:0, one launch (start us, length us, event | category | flops | bytes accessed | tf_op | source)
XLA Modules:
  0.0 32.9 jit_solution(16365640667967250101)
XLA Ops:
  0.0 0.0 copy-start
  0.0 0.0 copy-start.1
  0.0 1.8 %pack.1 = (f32[80,512]{1,0:T(8,128)}, f32[80,512]{1,0:T(8,128)}) custom-call(f32[7,512]{1,0:T(8,128)} %geo_ref.1, f32[64,512]{1,0:T(8,128)} %adj.3, f32[64,512]{1,0:T(8,128)} %fwd.3, s32[4,512]{1,0:T(4,128)} %own.2, f32[4,512]{1,0:T(4,128)} %wt.1), custom_call_target="tpu_custom_call" | custom-call | tf_op jit(solution)/shard_map/pack/pallas_call | solution.py:432
  1.8 0.0 copy-start.2
  1.8 0.5 %collective-permute-start.1 = (f32[80,512]{1,0:T(8,128)}, f32[80,512]{1,0:T(8,128)S(1)}, u32[]{:S(2)}, u32[]{:S(2)}) collective-permute-start(f32[80,512]{1,0:T(8,128)} %get-tuple-element.14), channel_id=1, source_target_pairs={{0,1},{1,0},{2,3},{3,2},{4,5},{5,4},{6,7},{7,6},{8,9},{9,8},{10,11... | collective-permute-start | bytes 491528 | tf_op jit(solution)/shard_map/ppermute | solution.py:480
  2.3 2.6 %collective-permute-start = (f32[80,512]{1,0:T(8,128)}, f32[80,512]{1,0:T(8,128)S(1)}, u32[]{:S(2)}, u32[]{:S(2)}) collective-permute-start(f32[80,512]{1,0:T(8,128)} %get-tuple-element.13.tpack), channel_id=1, source_target_pairs={{0,2},{1,3},{2,0},{3,1},{4,6},{5,7},{6,4},{7,5},{8,10},{9,11},{10,... | collective-permute-start | bytes 491528 | tf_op jit(solution)/shard_map/ppermute | solution.py:480
  4.9 0.0 copy-start.3
  4.9 0.0 collective-permute-done.1.near
  4.9 0.0 copy-done
  4.9 0.0 copy-done.1
  4.9 0.0 copy-done.2
  4.9 6.6 %own.3 = (bf16[2,256,1024]{2,1,0:T(8,128)(2,1)S(1)}, bf16[2,128,1024]{2,1,0:T(8,128)(2,1)S(1)}, f32[8,1024]{1,0:T(8,128)S(1)}, bf16[3,32,1024]{2,1,0:T(8,128)(2,...) custom-call(f32[7,512]{1,0:T(8,128)S(1)} %copy-done.2, f32[64,512]{1,0:T(8,128)S(1)} %copy-done, ...), custom_call_target="tpu_custom_call" | custom-call | flops 8000000000 | bytes 4000000 | tf_op jit(solution)/shard_map/own/pallas_call | solution.py:453
  11.6 0.0 collective-permute-done.far
  11.6 0.0 copy-done.3
  11.6 7.5 %rest.1 = f32[16,8,32]{2,1,0:T(8,128)S(1)} custom-call(f32[80,512]{1,0:T(8,128)S(1)} %copy-done.3, f32[80,512]{1,0:T(8,128)S(1)} %collective-permute-done.far, f32[80,512]{1,0:T(8,128)S(1)} %collective-permute-done.1.near, bf16[2,256,1024]{2,1,0:T(8,128)(2,1)S(1)} %get-tuple-element.15.right, bf16[2,128,1024]{2,1,0:T(8,128)(2,1)S(1)} %get-tuple-element.16.rightn, ...), custom_call_target="tpu_custom_call" | custom-call | flops 8000000000 | bytes 4000000 | tf_op jit(solution)/shard_map/rest/pallas_call | solution.py:468
  19.1 0.2 collective-permute-start.2
  19.3 1.0 %collective-permute-done.2 = f32[8,8,32]{2,1,0:T(8,128)S(1)} collective-permute-done((f32[8,8,32]{2,1,0:T(8,128)S(1)}, f32[8,8,32]{2,1,0:T(8,128)S(1)}, u32[]{:S(2)}, u32[]{:S(2)}) %collective-permute-start.2) | collective-permute-done | bytes 8224 | tf_op jit(solution)/shard_map/ppermute | solution.py:480
  20.3 1.6 %collective-permute-start.3 = (f32[4,8,32]{2,1,0:T(8,128)S(1)}, f32[4,8,32]{2,1,0:T(8,128)S(1)}, u32[]{:S(2)}, u32[]{:S(2)}) collective-permute-start(f32[4,8,32]{2,1,0:T(8,128)S(1)} %constant_dynamic-slice_fusion.2), channel_id=1, source_target_pairs={{0,2},{1,3},{2,0},{3,1},{4,6},{5,7},{6,4},{7,5},{8,10},{9,11},{10,... | collective-permute-start | bytes 12296 | tf_op jit(solution)/shard_map/ppermute | solution.py:480
  21.9 2.2 %collective-permute-done.3 = f32[4,8,32]{2,1,0:T(8,128)S(1)} collective-permute-done((f32[4,8,32]{2,1,0:T(8,128)S(1)}, f32[4,8,32]{2,1,0:T(8,128)S(1)}, u32[]{:S(2)}, u32[]{:S(2)}) %collective-permute-start.3) | collective-permute-done | bytes 4128 | tf_op jit(solution)/shard_map/ppermute | solution.py:480
  24.1 1.6 %collective-permute-start.4 = (f32[2,8,32]{2,1,0:T(8,128)S(1)}, f32[2,8,32]{2,1,0:T(8,128)S(1)}, u32[]{:S(2)}, u32[]{:S(2)}) collective-permute-start(f32[2,8,32]{2,1,0:T(8,128)S(1)} %constant_dynamic-slice_fusion.1), channel_id=1, source_target_pairs={{0,4},{4,0},{8,12},{12,8},{1,5},{5,1},{9,13},{13,9},{2,6},{6,2},{1... | collective-permute-start | bytes 6152 | tf_op jit(solution)/shard_map/ppermute | solution.py:480
  25.8 2.0 %collective-permute-done.4 = f32[2,8,32]{2,1,0:T(8,128)S(1)} collective-permute-done((f32[2,8,32]{2,1,0:T(8,128)S(1)}, f32[2,8,32]{2,1,0:T(8,128)S(1)}, u32[]{:S(2)}, u32[]{:S(2)}) %collective-permute-start.4) | collective-permute-done | bytes 2080 | tf_op jit(solution)/shard_map/ppermute | solution.py:480
  27.8 2.6 %collective-permute-start.5 = (f32[1,8,32]{2,1,0:T(8,128)S(1)}, f32[1,8,32]{2,1,0:T(8,128)S(1)}, u32[]{:S(2)}, u32[]{:S(2)}) collective-permute-start(f32[1,8,32]{2,1,0:T(8,128)S(1)} %constant_dynamic-slice_fusion), channel_id=1, source_target_pairs={{0,8},{4,12},{8,0},{12,4},{1,9},{5,13},{9,1},{13,5},{2,10},{6,14},... | collective-permute-start | bytes 3080 | tf_op jit(solution)/shard_map/ppermute | solution.py:480
  30.4 1.9 %collective-permute-done.5 = f32[1,8,32]{2,1,0:T(8,128)S(1)} collective-permute-done((f32[1,8,32]{2,1,0:T(8,128)S(1)}, f32[1,8,32]{2,1,0:T(8,128)S(1)}, u32[]{:S(2)}, u32[]{:S(2)}) %collective-permute-start.5) | collective-permute-done | bytes 1056 | tf_op jit(solution)/shard_map/ppermute | solution.py:480
  32.3 0.6 %slice_bitcast_fusion = f32[6,32]{1,0:T(8,128)} fusion(f32[1,8,32]{2,1,0:T(8,128)S(1)} %dynamic-slice_add_fusion.3), kind=kLoop, calls=%fused_computation.3 | loop fusion | bytes 1536 | tf_op jit(solution)/shard_map/squeeze | solution.py:493
  (8 shorter events, 0.0 us)
Async XLA Ops:
  0.0 4.9 %copy-start = (f32[64,512]{1,0:T(8,128)S(1)}, f32[64,512]{1,0:T(8,128)}, u32[]{:S(2)}) copy-start(f32[64,512]{1,0:T(8,128)} %adj.3) | copy-start | bytes 393220
  0.0 4.9 %copy-start.1 = (f32[64,512]{1,0:T(8,128)S(1)}, f32[64,512]{1,0:T(8,128)}, u32[]{:S(2)}) copy-start(f32[64,512]{1,0:T(8,128)} %fwd.3) | copy-start | bytes 393220
  1.8 3.1 %copy-start.2 = (f32[7,512]{1,0:T(8,128)S(1)}, f32[7,512]{1,0:T(8,128)}, u32[]{:S(2)}) copy-start(f32[7,512]{1,0:T(8,128)} %geo_ref.1) | copy-start | bytes 43012
  1.8 3.1 %collective-permute-start.1 = (f32[80,512]{1,0:T(8,128)}, f32[80,512]{1,0:T(8,128)S(1)}, u32[]{:S(2)}, u32[]{:S(2)}) collective-permute-start(f32[80,512]{1,0:T(8,128)} %get-tuple-element.14), channel_id=1, source_target_pairs={{0,1},{1,0},{2,3},{3,2},{4,5},{5,4},{6,7},{7,6},{8,9},{9,8},{10,11... | collective-permute-start | bytes 491528 | tf_op jit(solution)/shard_map/ppermute | solution.py:480
  2.3 9.3 %collective-permute-start = (f32[80,512]{1,0:T(8,128)}, f32[80,512]{1,0:T(8,128)S(1)}, u32[]{:S(2)}, u32[]{:S(2)}) collective-permute-start(f32[80,512]{1,0:T(8,128)} %get-tuple-element.13.tpack), channel_id=1, source_target_pairs={{0,2},{1,3},{2,0},{3,1},{4,6},{5,7},{6,4},{7,5},{8,10},{9,11},{10,... | collective-permute-start | bytes 491528 | tf_op jit(solution)/shard_map/ppermute | solution.py:480
  4.9 6.7 %copy-start.3 = (f32[80,512]{1,0:T(8,128)S(1)}, f32[80,512]{1,0:T(8,128)}, u32[]{:S(2)}) copy-start(f32[80,512]{1,0:T(8,128)} %get-tuple-element.13.tpack) | copy-start | bytes 491524
  19.1 1.3 %collective-permute-start.2 = (f32[8,8,32]{2,1,0:T(8,128)S(1)}, f32[8,8,32]{2,1,0:T(8,128)S(1)}, u32[]{:S(2)}, u32[]{:S(2)}) collective-permute-start(f32[8,8,32]{2,1,0:T(8,128)S(1)} %constant_dynamic-slice_fusion.3), channel_id=1, source_target_pairs={{0,1},{1,0},{2,3},{3,2},{4,5},{5,4},{6,7},{7,6},{8,9},{9,8},{10,11... | collective-permute-start | bytes 24584 | tf_op jit(solution)/shard_map/ppermute | solution.py:480
  20.3 3.8 %collective-permute-start.3 = (f32[4,8,32]{2,1,0:T(8,128)S(1)}, f32[4,8,32]{2,1,0:T(8,128)S(1)}, u32[]{:S(2)}, u32[]{:S(2)}) collective-permute-start(f32[4,8,32]{2,1,0:T(8,128)S(1)} %constant_dynamic-slice_fusion.2), channel_id=1, source_target_pairs={{0,2},{1,3},{2,0},{3,1},{4,6},{5,7},{6,4},{7,5},{8,10},{9,11},{10,... | collective-permute-start | bytes 12296 | tf_op jit(solution)/shard_map/ppermute | solution.py:480
  24.1 3.7 %collective-permute-start.4 = (f32[2,8,32]{2,1,0:T(8,128)S(1)}, f32[2,8,32]{2,1,0:T(8,128)S(1)}, u32[]{:S(2)}, u32[]{:S(2)}) collective-permute-start(f32[2,8,32]{2,1,0:T(8,128)S(1)} %constant_dynamic-slice_fusion.1), channel_id=1, source_target_pairs={{0,4},{4,0},{8,12},{12,8},{1,5},{5,1},{9,13},{13,9},{2,6},{6,2},{1... | collective-permute-start | bytes 6152 | tf_op jit(solution)/shard_map/ppermute | solution.py:480
  27.8 4.5 %collective-permute-start.5 = (f32[1,8,32]{2,1,0:T(8,128)S(1)}, f32[1,8,32]{2,1,0:T(8,128)S(1)}, u32[]{:S(2)}, u32[]{:S(2)}) collective-permute-start(f32[1,8,32]{2,1,0:T(8,128)S(1)} %constant_dynamic-slice_fusion), channel_id=1, source_target_pairs={{0,8},{4,12},{8,0},{12,4},{1,9},{5,13},{9,1},{13,5},{2,10},{6,14},... | collective-permute-start | bytes 3080 | tf_op jit(solution)/shard_map/ppermute | solution.py:480

commit v7 on v6

--- a/solution.py
+++ b/solution.py
@@ -20,9 +20,6 @@
 LANE = 128
 WIDE = 256
 
-SIN_C = None
-COS_C = None
-
 
 def _fit(fn, odd, terms):
     import numpy as np
@@ -33,15 +30,13 @@
     return [float(np.float32(c)) for c in coef]
 
 
-def _tables():
+def _sine():
     import numpy as np
 
-    s = _fit(lambda t: math.sqrt(2.0) * np.sin(np.pi * t), 1, 4)
-    c = _fit(lambda t: math.sqrt(2.0) * np.cos(np.pi * t), 0, 5)
-    return s, c
-
-
-SIN_C, COS_C = _tables()
+    return _fit(lambda t: math.sqrt(2.0) * np.sin(np.pi * t), 1, 5)
+
+
+SIN_C = _sine()
 
 
 def horner(coef, y):
@@ -122,9 +117,10 @@
     v = rs * (1.0 / (2.0 * math.pi))
     y = t * t
     sv = (t * v) * horner(SIN_C, y)
-    cv = v * horner(COS_C, y)
-    es = sv * cv
-    ec = v * v - sv * sv
+    v2 = v * v
+    ec = v2 - sv * sv
+    cv2 = jnp.maximum(v2 + ec, 1e-30)
+    es = (sv * cv2) * lax.rsqrt(cv2)
     yr = ec * wr - es * wi
     yi = ec * wi + es * wr
     a = yi + v * yr

time: 33.1 us -> 32.7 us (0.988)
  Pallas kernels: 15.9 us -> 15.4 us
where the time goes in v7:
time: 32.7 us; the launch traced here: 32.5 us
  Pallas kernels  15.4 us (47%)
  starting transfers between devices  9.09 us (28%)
  waiting for transfers between devices  7.23 us (22%)
  local copies, waits for them, and re-layouts  0.64 us (2%)
    ppermute x6, starting transfers between devices, swap(): return lax.ppermute(x, axis, [(k, k ^ bit) for k in range(size)])  9.09 us
    ppermute x6, waiting for transfers between devices, swap(): return lax.ppermute(x, axis, [(k, k ^ bit) for k in range(size)])  7.23 us
    pallas_call x1, Pallas kernels, rest_call(): pl.pallas_call(rest_kernel, out_shape=shape((slots, 8, cp_dev), F32), scr...  7.23 us
    pallas_call x1, Pallas kernels, own_call(): pl.pallas_call(own_kernel, out_shape=[shape((2, 256, total), BF16), shape...  6.4 us
    pallas_call x1, Pallas kernels, pack_call(): pl.pallas_call(pack_kernel, in_specs=[pl.BlockSpec(memory_space=pl.ANY)]...  1.78 us
  transfers between devices with their start and end apart: 6, of which 4 were waited for; matrix products, arithmetic and copies ran while one was open for 0% of the time, Pallas kernels for 20%

profile of v7, /device:TPU:0, one launch (start us, length us, event | category | flops | bytes accessed | tf_op | source)
XLA Modules:
  0.0 32.5 jit_solution(2811706139252375197)
XLA Ops:
  0.0 0.0 copy-start
  0.0 0.0 copy-start.1
  0.0 1.8 %pack.1 = (f32[80,512]{1,0:T(8,128)}, f32[80,512]{1,0:T(8,128)}) custom-call(f32[7,512]{1,0:T(8,128)} %geo_ref.1, f32[64,512]{1,0:T(8,128)} %adj.3, f32[64,512]{1,0:T(8,128)} %fwd.3, s32[4,512]{1,0:T(4,128)} %own.2, f32[4,512]{1,0:T(4,128)} %wt.1), custom_call_target="tpu_custom_call" | custom-call | tf_op jit(solution)/shard_map/pack/pallas_call | solution.py:428
  1.8 0.0 copy-start.2
  1.8 0.5 %collective-permute-start.1 = (f32[80,512]{1,0:T(8,128)}, f32[80,512]{1,0:T(8,128)S(1)}, u32[]{:S(2)}, u32[]{:S(2)}) collective-permute-start(f32[80,512]{1,0:T(8,128)} %get-tuple-element.14), channel_id=1, source_target_pairs={{0,1},{1,0},{2,3},{3,2},{4,5},{5,4},{6,7},{7,6},{8,9},{9,8},{10,11... | collective-permute-start | bytes 491528 | tf_op jit(solution)/shard_map/ppermute | solution.py:476
  2.3 2.6 %collective-permute-start = (f32[80,512]{1,0:T(8,128)}, f32[80,512]{1,0:T(8,128)S(1)}, u32[]{:S(2)}, u32[]{:S(2)}) collective-permute-start(f32[80,512]{1,0:T(8,128)} %get-tuple-element.13.tpack), channel_id=1, source_target_pairs={{0,2},{1,3},{2,0},{3,1},{4,6},{5,7},{6,4},{7,5},{8,10},{9,11},{10,... | collective-permute-start | bytes 491528 | tf_op jit(solution)/shard_map/ppermute | solution.py:476
  4.9 0.0 copy-start.3
  4.9 0.0 collective-permute-done.1.near
  4.9 0.0 copy-done
  4.9 0.0 copy-done.1
  4.9 0.0 copy-done.2
  4.9 6.4 %own.3 = (bf16[2,256,1024]{2,1,0:T(8,128)(2,1)S(1)}, bf16[2,128,1024]{2,1,0:T(8,128)(2,1)S(1)}, f32[8,1024]{1,0:T(8,128)S(1)}, bf16[3,32,1024]{2,1,0:T(8,128)(2,...) custom-call(f32[7,512]{1,0:T(8,128)S(1)} %copy-done.2, f32[64,512]{1,0:T(8,128)S(1)} %copy-done, ...), custom_call_target="tpu_custom_call" | custom-call | flops 8000000000 | bytes 4000000 | tf_op jit(solution)/shard_map/own/pallas_call | solution.py:449
  11.3 0.0 collective-permute-done.far
  11.3 0.0 copy-done.3
  11.4 7.2 %rest.1 = f32[16,8,32]{2,1,0:T(8,128)S(1)} custom-call(f32[80,512]{1,0:T(8,128)S(1)} %copy-done.3, f32[80,512]{1,0:T(8,128)S(1)} %collective-permute-done.far, f32[80,512]{1,0:T(8,128)S(1)} %collective-permute-done.1.near, bf16[2,256,1024]{2,1,0:T(8,128)(2,1)S(1)} %get-tuple-element.15.right, bf16[2,128,1024]{2,1,0:T(8,128)(2,1)S(1)} %get-tuple-element.16.rightn, ...), custom_call_target="tpu_custom_call" | custom-call | flops 8000000000 | bytes 4000000 | tf_op jit(solution)/shard_map/rest/pallas_call | solution.py:464
  18.6 0.2 collective-permute-start.2
  18.8 1.0 %collective-permute-done.2 = f32[8,8,32]{2,1,0:T(8,128)S(1)} collective-permute-done((f32[8,8,32]{2,1,0:T(8,128)S(1)}, f32[8,8,32]{2,1,0:T(8,128)S(1)}, u32[]{:S(2)}, u32[]{:S(2)}) %collective-permute-start.2) | collective-permute-done | bytes 8224 | tf_op jit(solution)/shard_map/ppermute | solution.py:476
  19.9 1.6 %collective-permute-start.3 = (f32[4,8,32]{2,1,0:T(8,128)S(1)}, f32[4,8,32]{2,1,0:T(8,128)S(1)}, u32[]{:S(2)}, u32[]{:S(2)}) collective-permute-start(f32[4,8,32]{2,1,0:T(8,128)S(1)} %constant_dynamic-slice_fusion.2), channel_id=1, source_target_pairs={{0,2},{1,3},{2,0},{3,1},{4,6},{5,7},{6,4},{7,5},{8,10},{9,11},{10,... | collective-permute-start | bytes 12296 | tf_op jit(solution)/shard_map/ppermute | solution.py:476
  21.5 2.2 %collective-permute-done.3 = f32[4,8,32]{2,1,0:T(8,128)S(1)} collective-permute-done((f32[4,8,32]{2,1,0:T(8,128)S(1)}, f32[4,8,32]{2,1,0:T(8,128)S(1)}, u32[]{:S(2)}, u32[]{:S(2)}) %collective-permute-start.3) | collective-permute-done | bytes 4128 | tf_op jit(solution)/shard_map/ppermute | solution.py:476
  23.7 1.6 %collective-permute-start.4 = (f32[2,8,32]{2,1,0:T(8,128)S(1)}, f32[2,8,32]{2,1,0:T(8,128)S(1)}, u32[]{:S(2)}, u32[]{:S(2)}) collective-permute-start(f32[2,8,32]{2,1,0:T(8,128)S(1)} %constant_dynamic-slice_fusion.1), channel_id=1, source_target_pairs={{0,4},{4,0},{8,12},{12,8},{1,5},{5,1},{9,13},{13,9},{2,6},{6,2},{1... | collective-permute-start | bytes 6152 | tf_op jit(solution)/shard_map/ppermute | solution.py:476
  25.3 2.0 %collective-permute-done.4 = f32[2,8,32]{2,1,0:T(8,128)S(1)} collective-permute-done((f32[2,8,32]{2,1,0:T(8,128)S(1)}, f32[2,8,32]{2,1,0:T(8,128)S(1)}, u32[]{:S(2)}, u32[]{:S(2)}) %collective-permute-start.4) | collective-permute-done | bytes 2080 | tf_op jit(solution)/shard_map/ppermute | solution.py:476
  27.3 2.6 %collective-permute-start.5 = (f32[1,8,32]{2,1,0:T(8,128)S(1)}, f32[1,8,32]{2,1,0:T(8,128)S(1)}, u32[]{:S(2)}, u32[]{:S(2)}) collective-permute-start(f32[1,8,32]{2,1,0:T(8,128)S(1)} %constant_dynamic-slice_fusion), channel_id=1, source_target_pairs={{0,8},{4,12},{8,0},{12,4},{1,9},{5,13},{9,1},{13,5},{2,10},{6,14},... | collective-permute-start | bytes 3080 | tf_op jit(solution)/shard_map/ppermute | solution.py:476
  30.0 1.9 %collective-permute-done.5 = f32[1,8,32]{2,1,0:T(8,128)S(1)} collective-permute-done((f32[1,8,32]{2,1,0:T(8,128)S(1)}, f32[1,8,32]{2,1,0:T(8,128)S(1)}, u32[]{:S(2)}, u32[]{:S(2)}) %collective-permute-start.5) | collective-permute-done | bytes 1056 | tf_op jit(solution)/shard_map/ppermute | solution.py:476
  31.9 0.6 %slice_bitcast_fusion = f32[6,32]{1,0:T(8,128)} fusion(f32[1,8,32]{2,1,0:T(8,128)S(1)} %dynamic-slice_add_fusion.3), kind=kLoop, calls=%fused_computation.3 | loop fusion | bytes 1536 | tf_op jit(solution)/shard_map/squeeze | solution.py:489
  (8 shorter events, 0.0 us)
Async XLA Ops:
  0.0 4.9 %copy-start = (f32[64,512]{1,0:T(8,128)S(1)}, f32[64,512]{1,0:T(8,128)}, u32[]{:S(2)}) copy-start(f32[64,512]{1,0:T(8,128)} %adj.3) | copy-start | bytes 393220
  0.0 4.9 %copy-start.1 = (f32[64,512]{1,0:T(8,128)S(1)}, f32[64,512]{1,0:T(8,128)}, u32[]{:S(2)}) copy-start(f32[64,512]{1,0:T(8,128)} %fwd.3) | copy-start | bytes 393220
  1.8 3.1 %copy-start.2 = (f32[7,512]{1,0:T(8,128)S(1)}, f32[7,512]{1,0:T(8,128)}, u32[]{:S(2)}) copy-start(f32[7,512]{1,0:T(8,128)} %geo_ref.1) | copy-start | bytes 43012
  1.8 3.1 %collective-permute-start.1 = (f32[80,512]{1,0:T(8,128)}, f32[80,512]{1,0:T(8,128)S(1)}, u32[]{:S(2)}, u32[]{:S(2)}) collective-permute-start(f32[80,512]{1,0:T(8,128)} %get-tuple-element.14), channel_id=1, source_target_pairs={{0,1},{1,0},{2,3},{3,2},{4,5},{5,4},{6,7},{7,6},{8,9},{9,8},{10,11... | collective-permute-start | bytes 491528 | tf_op jit(solution)/shard_map/ppermute | solution.py:476
  2.3 9.0 %collective-permute-start = (f32[80,512]{1,0:T(8,128)}, f32[80,512]{1,0:T(8,128)S(1)}, u32[]{:S(2)}, u32[]{:S(2)}) collective-permute-start(f32[80,512]{1,0:T(8,128)} %get-tuple-element.13.tpack), channel_id=1, source_target_pairs={{0,2},{1,3},{2,0},{3,1},{4,6},{5,7},{6,4},{7,5},{8,10},{9,11},{10,... | collective-permute-start | bytes 491528 | tf_op jit(solution)/shard_map/ppermute | solution.py:476
  4.9 6.5 %copy-start.3 = (f32[80,512]{1,0:T(8,128)S(1)}, f32[80,512]{1,0:T(8,128)}, u32[]{:S(2)}) copy-start(f32[80,512]{1,0:T(8,128)} %get-tuple-element.13.tpack) | copy-start | bytes 491524
  18.6 1.3 %collective-permute-start.2 = (f32[8,8,32]{2,1,0:T(8,128)S(1)}, f32[8,8,32]{2,1,0:T(8,128)S(1)}, u32[]{:S(2)}, u32[]{:S(2)}) collective-permute-start(f32[8,8,32]{2,1,0:T(8,128)S(1)} %constant_dynamic-slice_fusion.3), channel_id=1, source_target_pairs={{0,1},{1,0},{2,3},{3,2},{4,5},{5,4},{6,7},{7,6},{8,9},{9,8},{10,11... | collective-permute-start | bytes 24584 | tf_op jit(solution)/shard_map/ppermute | solution.py:476
  19.9 3.8 %collective-permute-start.3 = (f32[4,8,32]{2,1,0:T(8,128)S(1)}, f32[4,8,32]{2,1,0:T(8,128)S(1)}, u32[]{:S(2)}, u32[]{:S(2)}) collective-permute-start(f32[4,8,32]{2,1,0:T(8,128)S(1)} %constant_dynamic-slice_fusion.2), channel_id=1, source_target_pairs={{0,2},{1,3},{2,0},{3,1},{4,6},{5,7},{6,4},{7,5},{8,10},{9,11},{10,... | collective-permute-start | bytes 12296 | tf_op jit(solution)/shard_map/ppermute | solution.py:476
  23.7 3.7 %collective-permute-start.4 = (f32[2,8,32]{2,1,0:T(8,128)S(1)}, f32[2,8,32]{2,1,0:T(8,128)S(1)}, u32[]{:S(2)}, u32[]{:S(2)}) collective-permute-start(f32[2,8,32]{2,1,0:T(8,128)S(1)} %constant_dynamic-slice_fusion.1), channel_id=1, source_target_pairs={{0,4},{4,0},{8,12},{12,8},{1,5},{5,1},{9,13},{13,9},{2,6},{6,2},{1... | collective-permute-start | bytes 6152 | tf_op jit(solution)/shard_map/ppermute | solution.py:476
  27.3 4.5 %collective-permute-start.5 = (f32[1,8,32]{2,1,0:T(8,128)S(1)}, f32[1,8,32]{2,1,0:T(8,128)S(1)}, u32[]{:S(2)}, u32[]{:S(2)}) collective-permute-start(f32[1,8,32]{2,1,0:T(8,128)S(1)} %constant_dynamic-slice_fusion), channel_id=1, source_target_pairs={{0,8},{4,12},{8,0},{12,4},{1,9},{5,13},{9,1},{13,5},{2,10},{6,14},... | collective-permute-start | bytes 3080 | tf_op jit(solution)/shard_map/ppermute | solution.py:476

commit v8 on v7

--- a/solution.py
+++ b/solution.py
@@ -17,6 +17,8 @@
 TJ = 256
 SUB = 16
 STEP = 8
+LAST = 32
+LAST_STEP = 16
 LANE = 128
 WIDE = 256
 
@@ -205,25 +207,27 @@
     def values(t, slot):
         i0, j0 = start(t)
 
-        def piece(jj, ii):
-            lanes = pl.ds(j0 + jj * WIDE, WIDE)
+        def piece(jj, top, size, step):
             here = slice(jj * WIDE, (jj + 1) * WIDE)
-            xj = [xj_ref[k : k + 1, lanes] for k in range(4)]
-            rows = pl.ds(ii * SUB, SUB)
-            halves = []
-            for r in range(0, SUB, STEP):
-                xi = [xi_ref[k, pl.ds(i0 + ii * SUB + r, STEP), :] for k in range(3)]
+            xj = [xj_ref[k : k + 1, pl.ds(j0 + jj * WIDE, WIDE)] for k in range(4)]
+            rows = pl.ds(top, size)
+            bands = []
+            for r in range(top, top + size, step):
+                xi = [xi_ref[k, pl.ds(i0 + r, step), :] for k in range(3)]
                 xi = [jnp.concatenate([v, v], axis=1) for v in xi]
-                pr = [prod[slot, k, pl.ds(ii * SUB + r, STEP), here] for k in range(4)]
-                halves.append(pair_chunk(pr, xi, xj[0:3], xj[3]))
-            a, b, c = [jnp.concatenate(parts, axis=0) for parts in zip(*halves)]
+                pr = [prod[slot, k, pl.ds(r, step), here] for k in range(4)]
+                bands.append(pair_chunk(pr, xi, xj[0:3], xj[3]))
+            a, b, c = [jnp.concatenate(parts, axis=0) for parts in zip(*bands)]
             for k, val in ((0, a), (2, c)):
                 hi = val.astype(BF16)
                 abc[slot, k, rows, here] = hi
                 abc[slot, k + 1, rows, here] = (val - hi.astype(F32)).astype(BF16)
             abc[slot, 4, rows, here] = b.astype(BF16)
 
-        return [functools.partial(piece, jj, ii) for jj in range(TJ // WIDE) for ii in range(TI // SUB)]
+        todo = [(jj, top, SUB, STEP) for jj in range(TJ // WIDE) for top in range(0, TI, SUB)]
+        if LAST > SUB:
+            todo = todo[: -(LAST // SUB)] + [(TJ // WIDE - 1, TI - LAST, LAST, LAST_STEP)]
+        return [functools.partial(piece, *args) for args in todo]
 
     def sums(t, slot):
         i0, j0 = start(t)
@@ -260,6 +264,8 @@
                 matrix[done]()
                 done += 1
             todo()
+        for rest in matrix[done:]:
+            rest()
 
     last = count - 1
     for todo in products(0, 0):

time: 32.7 us -> 32.2 us (0.985)
  Pallas kernels: 15.4 us -> 14.9 us
  transfers between devices with their start and end apart: 6 -> 6, of which waited for: 4 -> 4; matrix products, arithmetic and copies ran while one was open for 0% -> 0% of each run, Pallas kernels for 20% -> 19%
where the time goes in v8:
time: 32.2 us; the launch traced here: 32 us
  Pallas kernels  14.9 us (46%)
  starting transfers between devices  9.08 us (28%)
  waiting for transfers between devices  7.24 us (22%)
  local copies, waits for them, and re-layouts  0.64 us (2%)
    ppermute x6, starting transfers between devices, swap(): return lax.ppermute(x, axis, [(k, k ^ bit) for k in range(size)])  9.08 us
    ppermute x6, waiting for transfers between devices, swap(): return lax.ppermute(x, axis, [(k, k ^ bit) for k in range(size)])  7.24 us
    pallas_call x1, Pallas kernels, rest_call(): pl.pallas_call(rest_kernel, out_shape=shape((slots, 8, cp_dev), F32), scr...  6.99 us
    pallas_call x1, Pallas kernels, own_call(): pl.pallas_call(own_kernel, out_shape=[shape((2, 256, total), BF16), shape...  6.17 us
    pallas_call x1, Pallas kernels, pack_call(): pl.pallas_call(pack_kernel, in_specs=[pl.BlockSpec(memory_space=pl.ANY)]...  1.78 us
  transfers between devices with their start and end apart: 6, of which 4 were waited for; matrix products, arithmetic and copies ran while one was open for 0% of the time, Pallas kernels for 19%

profile of v8, /device:TPU:0, one launch (start us, length us, event | category | flops | bytes accessed | tf_op | source)
XLA Modules:
  0.0 32.0 jit_solution(3084608955018242399)
XLA Ops:
  0.0 0.0 copy-start
  0.0 0.0 copy-start.1
  0.0 1.8 %pack.1 = (f32[80,512]{1,0:T(8,128)}, f32[80,512]{1,0:T(8,128)}) custom-call(f32[7,512]{1,0:T(8,128)} %geo_ref.1, f32[64,512]{1,0:T(8,128)} %adj.3, f32[64,512]{1,0:T(8,128)} %fwd.3, s32[4,512]{1,0:T(4,128)} %own.2, f32[4,512]{1,0:T(4,128)} %wt.1), custom_call_target="tpu_custom_call" | custom-call | tf_op jit(solution)/shard_map/pack/pallas_call | solution.py:434
  1.8 0.0 copy-start.2
  1.8 0.5 %collective-permute-start.1 = (f32[80,512]{1,0:T(8,128)}, f32[80,512]{1,0:T(8,128)S(1)}, u32[]{:S(2)}, u32[]{:S(2)}) collective-permute-start(f32[80,512]{1,0:T(8,128)} %get-tuple-element.14), channel_id=1, source_target_pairs={{0,1},{1,0},{2,3},{3,2},{4,5},{5,4},{6,7},{7,6},{8,9},{9,8},{10,11... | collective-permute-start | bytes 491528 | tf_op jit(solution)/shard_map/ppermute | solution.py:482
  2.3 2.6 %collective-permute-start = (f32[80,512]{1,0:T(8,128)}, f32[80,512]{1,0:T(8,128)S(1)}, u32[]{:S(2)}, u32[]{:S(2)}) collective-permute-start(f32[80,512]{1,0:T(8,128)} %get-tuple-element.13.tpack), channel_id=1, source_target_pairs={{0,2},{1,3},{2,0},{3,1},{4,6},{5,7},{6,4},{7,5},{8,10},{9,11},{10,... | collective-permute-start | bytes 491528 | tf_op jit(solution)/shard_map/ppermute | solution.py:482
  4.9 0.0 copy-start.3
  4.9 0.0 collective-permute-done.1.near
  4.9 0.0 copy-done
  4.9 0.0 copy-done.1
  4.9 0.0 copy-done.2
  4.9 6.2 %own.3 = (bf16[2,256,1024]{2,1,0:T(8,128)(2,1)S(1)}, bf16[2,128,1024]{2,1,0:T(8,128)(2,1)S(1)}, f32[8,1024]{1,0:T(8,128)S(1)}, bf16[3,32,1024]{2,1,0:T(8,128)(2,...) custom-call(f32[7,512]{1,0:T(8,128)S(1)} %copy-done.2, f32[64,512]{1,0:T(8,128)S(1)} %copy-done, ...), custom_call_target="tpu_custom_call" | custom-call | flops 8000000000 | bytes 4000000 | tf_op jit(solution)/shard_map/own/pallas_call | solution.py:455
  11.1 0.0 collective-permute-done.far
  11.1 0.0 copy-done.3
  11.1 7.0 %rest.1 = f32[16,8,32]{2,1,0:T(8,128)S(1)} custom-call(f32[80,512]{1,0:T(8,128)S(1)} %copy-done.3, f32[80,512]{1,0:T(8,128)S(1)} %collective-permute-done.far, f32[80,512]{1,0:T(8,128)S(1)} %collective-permute-done.1.near, bf16[2,256,1024]{2,1,0:T(8,128)(2,1)S(1)} %get-tuple-element.15.right, bf16[2,128,1024]{2,1,0:T(8,128)(2,1)S(1)} %get-tuple-element.16.rightn, ...), custom_call_target="tpu_custom_call" | custom-call | flops 8000000000 | bytes 4000000 | tf_op jit(solution)/shard_map/rest/pallas_call | solution.py:470
  18.1 0.2 collective-permute-start.2
  18.3 1.0 %collective-permute-done.2 = f32[8,8,32]{2,1,0:T(8,128)S(1)} collective-permute-done((f32[8,8,32]{2,1,0:T(8,128)S(1)}, f32[8,8,32]{2,1,0:T(8,128)S(1)}, u32[]{:S(2)}, u32[]{:S(2)}) %collective-permute-start.2) | collective-permute-done | bytes 8224 | tf_op jit(solution)/shard_map/ppermute | solution.py:482
  19.4 1.6 %collective-permute-start.3 = (f32[4,8,32]{2,1,0:T(8,128)S(1)}, f32[4,8,32]{2,1,0:T(8,128)S(1)}, u32[]{:S(2)}, u32[]{:S(2)}) collective-permute-start(f32[4,8,32]{2,1,0:T(8,128)S(1)} %constant_dynamic-slice_fusion.2), channel_id=1, source_target_pairs={{0,2},{1,3},{2,0},{3,1},{4,6},{5,7},{6,4},{7,5},{8,10},{9,11},{10,... | collective-permute-start | bytes 12296 | tf_op jit(solution)/shard_map/ppermute | solution.py:482
  21.0 2.2 %collective-permute-done.3 = f32[4,8,32]{2,1,0:T(8,128)S(1)} collective-permute-done((f32[4,8,32]{2,1,0:T(8,128)S(1)}, f32[4,8,32]{2,1,0:T(8,128)S(1)}, u32[]{:S(2)}, u32[]{:S(2)}) %collective-permute-start.3) | collective-permute-done | bytes 4128 | tf_op jit(solution)/shard_map/ppermute | solution.py:482
  23.2 1.6 %collective-permute-start.4 = (f32[2,8,32]{2,1,0:T(8,128)S(1)}, f32[2,8,32]{2,1,0:T(8,128)S(1)}, u32[]{:S(2)}, u32[]{:S(2)}) collective-permute-start(f32[2,8,32]{2,1,0:T(8,128)S(1)} %constant_dynamic-slice_fusion.1), channel_id=1, source_target_pairs={{0,4},{4,0},{8,12},{12,8},{1,5},{5,1},{9,13},{13,9},{2,6},{6,2},{1... | collective-permute-start | bytes 6152 | tf_op jit(solution)/shard_map/ppermute | solution.py:482
  24.8 2.1 %collective-permute-done.4 = f32[2,8,32]{2,1,0:T(8,128)S(1)} collective-permute-done((f32[2,8,32]{2,1,0:T(8,128)S(1)}, f32[2,8,32]{2,1,0:T(8,128)S(1)}, u32[]{:S(2)}, u32[]{:S(2)}) %collective-permute-start.4) | collective-permute-done | bytes 2080 | tf_op jit(solution)/shard_map/ppermute | solution.py:482
  26.9 2.6 %collective-permute-start.5 = (f32[1,8,32]{2,1,0:T(8,128)S(1)}, f32[1,8,32]{2,1,0:T(8,128)S(1)}, u32[]{:S(2)}, u32[]{:S(2)}) collective-permute-start(f32[1,8,32]{2,1,0:T(8,128)S(1)} %constant_dynamic-slice_fusion), channel_id=1, source_target_pairs={{0,8},{4,12},{8,0},{12,4},{1,9},{5,13},{9,1},{13,5},{2,10},{6,14},... | collective-permute-start | bytes 3080 | tf_op jit(solution)/shard_map/ppermute | solution.py:482
  29.5 1.9 %collective-permute-done.5 = f32[1,8,32]{2,1,0:T(8,128)S(1)} collective-permute-done((f32[1,8,32]{2,1,0:T(8,128)S(1)}, f32[1,8,32]{2,1,0:T(8,128)S(1)}, u32[]{:S(2)}, u32[]{:S(2)}) %collective-permute-start.5) | collective-permute-done | bytes 1056 | tf_op jit(solution)/shard_map/ppermute | solution.py:482
  31.4 0.6 %slice_bitcast_fusion = f32[6,32]{1,0:T(8,128)} fusion(f32[1,8,32]{2,1,0:T(8,128)S(1)} %dynamic-slice_add_fusion.3), kind=kLoop, calls=%fused_computation.3 | loop fusion | bytes 1536 | tf_op jit(solution)/shard_map/squeeze | solution.py:495
  (8 shorter events, 0.0 us)
Async XLA Ops:
  0.0 4.9 %copy-start = (f32[64,512]{1,0:T(8,128)S(1)}, f32[64,512]{1,0:T(8,128)}, u32[]{:S(2)}) copy-start(f32[64,512]{1,0:T(8,128)} %adj.3) | copy-start | bytes 393220
  0.0 4.9 %copy-start.1 = (f32[64,512]{1,0:T(8,128)S(1)}, f32[64,512]{1,0:T(8,128)}, u32[]{:S(2)}) copy-start(f32[64,512]{1,0:T(8,128)} %fwd.3) | copy-start | bytes 393220
  1.8 3.1 %copy-start.2 = (f32[7,512]{1,0:T(8,128)S(1)}, f32[7,512]{1,0:T(8,128)}, u32[]{:S(2)}) copy-start(f32[7,512]{1,0:T(8,128)} %geo_ref.1) | copy-start | bytes 43012
  1.8 3.1 %collective-permute-start.1 = (f32[80,512]{1,0:T(8,128)}, f32[80,512]{1,0:T(8,128)S(1)}, u32[]{:S(2)}, u32[]{:S(2)}) collective-permute-start(f32[80,512]{1,0:T(8,128)} %get-tuple-element.14), channel_id=1, source_target_pairs={{0,1},{1,0},{2,3},{3,2},{4,5},{5,4},{6,7},{7,6},{8,9},{9,8},{10,11... | collective-permute-start | bytes 491528 | tf_op jit(solution)/shard_map/ppermute | solution.py:482
  2.3 8.8 %collective-permute-start = (f32[80,512]{1,0:T(8,128)}, f32[80,512]{1,0:T(8,128)S(1)}, u32[]{:S(2)}, u32[]{:S(2)}) collective-permute-start(f32[80,512]{1,0:T(8,128)} %get-tuple-element.13.tpack), channel_id=1, source_target_pairs={{0,2},{1,3},{2,0},{3,1},{4,6},{5,7},{6,4},{7,5},{8,10},{9,11},{10,... | collective-permute-start | bytes 491528 | tf_op jit(solution)/shard_map/ppermute | solution.py:482
  4.9 6.2 %copy-start.3 = (f32[80,512]{1,0:T(8,128)S(1)}, f32[80,512]{1,0:T(8,128)}, u32[]{:S(2)}) copy-start(f32[80,512]{1,0:T(8,128)} %get-tuple-element.13.tpack) | copy-start | bytes 491524
  18.1 1.3 %collective-permute-start.2 = (f32[8,8,32]{2,1,0:T(8,128)S(1)}, f32[8,8,32]{2,1,0:T(8,128)S(1)}, u32[]{:S(2)}, u32[]{:S(2)}) collective-permute-start(f32[8,8,32]{2,1,0:T(8,128)S(1)} %constant_dynamic-slice_fusion.3), channel_id=1, source_target_pairs={{0,1},{1,0},{2,3},{3,2},{4,5},{5,4},{6,7},{7,6},{8,9},{9,8},{10,11... | collective-permute-start | bytes 24584 | tf_op jit(solution)/shard_map/ppermute | solution.py:482
  19.4 3.8 %collective-permute-start.3 = (f32[4,8,32]{2,1,0:T(8,128)S(1)}, f32[4,8,32]{2,1,0:T(8,128)S(1)}, u32[]{:S(2)}, u32[]{:S(2)}) collective-permute-start(f32[4,8,32]{2,1,0:T(8,128)S(1)} %constant_dynamic-slice_fusion.2), channel_id=1, source_target_pairs={{0,2},{1,3},{2,0},{3,1},{4,6},{5,7},{6,4},{7,5},{8,10},{9,11},{10,... | collective-permute-start | bytes 12296 | tf_op jit(solution)/shard_map/ppermute | solution.py:482
  23.2 3.7 %collective-permute-start.4 = (f32[2,8,32]{2,1,0:T(8,128)S(1)}, f32[2,8,32]{2,1,0:T(8,128)S(1)}, u32[]{:S(2)}, u32[]{:S(2)}) collective-permute-start(f32[2,8,32]{2,1,0:T(8,128)S(1)} %constant_dynamic-slice_fusion.1), channel_id=1, source_target_pairs={{0,4},{4,0},{8,12},{12,8},{1,5},{5,1},{9,13},{13,9},{2,6},{6,2},{1... | collective-permute-start | bytes 6152 | tf_op jit(solution)/shard_map/ppermute | solution.py:482
  26.9 4.5 %collective-permute-start.5 = (f32[1,8,32]{2,1,0:T(8,128)S(1)}, f32[1,8,32]{2,1,0:T(8,128)S(1)}, u32[]{:S(2)}, u32[]{:S(2)}) collective-permute-start(f32[1,8,32]{2,1,0:T(8,128)S(1)} %constant_dynamic-slice_fusion), channel_id=1, source_target_pairs={{0,8},{4,12},{8,0},{12,4},{1,9},{5,13},{9,1},{13,5},{2,10},{6,14},... | collective-permute-start | bytes 3080 | tf_op jit(solution)/shard_map/ppermute | solution.py:482

commit v9 on v8

--- a/solution.py
+++ b/solution.py
@@ -164,12 +164,9 @@
     sums = sum_rows(x, m)
     for k in range(3):
         frow[k, :, cols] = sums[k]
-    row = lax.broadcasted_iota(jnp.int32, (128, 3 * LANE), 0)
-    axis = lax.broadcasted_iota(jnp.int32, (128, 3 * LANE), 1) // LANE
-    pick = (row == axis) | (row == axis + 16) | (row == axis + 32)
-    spread = dot(left[cols, 0:128], jnp.where(pick, 1.0, 0.0).astype(BF16))
+    xt = jnp.concatenate([x, m, m[0:2]], axis=0).T
     for k in range(3):
-        xi_ref[k, cols, :] = spread[:, k * LANE : (k + 1) * LANE]
+        xi_ref[k, cols, :] = jnp.broadcast_to(xt[:, k : k + 1], (x.shape[1], LANE))
 
 
 def build_sources(geo, fwd, center, cols, right, rightn, xj_ref, fcol):
@@ -229,10 +226,12 @@
             todo = todo[: -(LAST // SUB)] + [(TJ // WIDE - 1, TI - LAST, LAST, LAST_STEP)]
         return [functools.partial(piece, *args) for args in todo]
 
-    def sums(t, slot):
+    def sums(t, slot, grouped=False):
         i0, j0 = start(t)
         kept = [None, None]
         groups = ((0, (0,)), (0, (1,)), (2, (2,)), (2, (3,)), (1, (4,)))
+        if grouped:
+            groups = ((0, (0, 1)), (2, (2, 3)), (1, (4,)))
 
         def piece(n, k, parts):
             fi = frow[k, :, pl.ds(i0, TI)]
@@ -289,7 +288,7 @@
         return 0
 
     lax.fori_loop(0, count // 2, double, 0)
-    for todo in sums(last, 1):
+    for todo in sums(last, 1, True):
         todo()
 
 

time: 32.2 us -> 32.1 us (level)
  no operation moved by 1% of the time
where the time goes in v9:
time: 32.1 us; the launch traced here: 31.9 us
  Pallas kernels  14.8 us (46%)
  starting transfers between devices  9.11 us (28%)
  waiting for transfers between devices  7.22 us (22%)
  local copies, waits for them, and re-layouts  0.64 us (2%)
    ppermute x6, starting transfers between devices, swap(): return lax.ppermute(x, axis, [(k, k ^ bit) for k in range(size)])  9.11 us
    ppermute x6, waiting for transfers between devices, swap(): return lax.ppermute(x, axis, [(k, k ^ bit) for k in range(size)])  7.22 us
    pallas_call x1, Pallas kernels, rest_call(): pl.pallas_call(rest_kernel, out_shape=shape((slots, 8, cp_dev), F32), scr...  6.92 us
    pallas_call x1, Pallas kernels, own_call(): pl.pallas_call(own_kernel, out_shape=[shape((2, 256, total), BF16), shape...  6.14 us
    pallas_call x1, Pallas kernels, pack_call(): pl.pallas_call(pack_kernel, in_specs=[pl.BlockSpec(memory_space=pl.ANY)]...  1.78 us
  transfers between devices with their start and end apart: 6, of which 4 were waited for; matrix products, arithmetic and copies ran while one was open for 0% of the time, Pallas kernels for 19%

profile of v9, /device:TPU:0, one launch (start us, length us, event | category | flops | bytes accessed | tf_op | source)
XLA Modules:
  0.0 31.9 jit_solution(15830281525763578328)
XLA Ops:
  0.0 0.0 copy-start
  0.0 0.0 copy-start.1
  0.0 1.8 %pack.1 = (f32[80,512]{1,0:T(8,128)}, f32[80,512]{1,0:T(8,128)}) custom-call(f32[7,512]{1,0:T(8,128)} %geo_ref.1, f32[64,512]{1,0:T(8,128)} %adj.3, f32[64,512]{1,0:T(8,128)} %fwd.3, s32[4,512]{1,0:T(4,128)} %own.2, f32[4,512]{1,0:T(4,128)} %wt.1), custom_call_target="tpu_custom_call" | custom-call | tf_op jit(solution)/shard_map/pack/pallas_call | solution.py:433
  1.8 0.0 copy-start.2
  1.8 0.5 %collective-permute-start.1 = (f32[80,512]{1,0:T(8,128)}, f32[80,512]{1,0:T(8,128)S(1)}, u32[]{:S(2)}, u32[]{:S(2)}) collective-permute-start(f32[80,512]{1,0:T(8,128)} %get-tuple-element.14), channel_id=1, source_target_pairs={{0,1},{1,0},{2,3},{3,2},{4,5},{5,4},{6,7},{7,6},{8,9},{9,8},{10,11... | collective-permute-start | bytes 491528 | tf_op jit(solution)/shard_map/ppermute | solution.py:481
  2.3 2.6 %collective-permute-start = (f32[80,512]{1,0:T(8,128)}, f32[80,512]{1,0:T(8,128)S(1)}, u32[]{:S(2)}, u32[]{:S(2)}) collective-permute-start(f32[80,512]{1,0:T(8,128)} %get-tuple-element.13.tpack), channel_id=1, source_target_pairs={{0,2},{1,3},{2,0},{3,1},{4,6},{5,7},{6,4},{7,5},{8,10},{9,11},{10,... | collective-permute-start | bytes 491528 | tf_op jit(solution)/shard_map/ppermute | solution.py:481
  4.9 0.0 copy-start.3
  4.9 0.0 collective-permute-done.1.near
  4.9 0.0 copy-done
  4.9 0.0 copy-done.1
  4.9 0.0 copy-done.2
  4.9 6.1 %own.3 = (bf16[2,256,1024]{2,1,0:T(8,128)(2,1)S(1)}, bf16[2,128,1024]{2,1,0:T(8,128)(2,1)S(1)}, f32[8,1024]{1,0:T(8,128)S(1)}, bf16[3,32,1024]{2,1,0:T(8,128)(2,...) custom-call(f32[7,512]{1,0:T(8,128)S(1)} %copy-done.2, f32[64,512]{1,0:T(8,128)S(1)} %copy-done, ...), custom_call_target="tpu_custom_call" | custom-call | flops 8000000000 | bytes 4000000 | tf_op jit(solution)/shard_map/own/pallas_call | solution.py:454
  11.1 0.0 collective-permute-done.far
  11.1 0.0 copy-done.3
  11.1 6.9 %rest.1 = f32[16,8,32]{2,1,0:T(8,128)S(1)} custom-call(f32[80,512]{1,0:T(8,128)S(1)} %copy-done.3, f32[80,512]{1,0:T(8,128)S(1)} %collective-permute-done.far, f32[80,512]{1,0:T(8,128)S(1)} %collective-permute-done.1.near, bf16[2,256,1024]{2,1,0:T(8,128)(2,1)S(1)} %get-tuple-element.15.right, bf16[2,128,1024]{2,1,0:T(8,128)(2,1)S(1)} %get-tuple-element.16.rightn, ...), custom_call_target="tpu_custom_call" | custom-call | flops 8000000000 | bytes 4000000 | tf_op jit(solution)/shard_map/rest/pallas_call | solution.py:469
  18.0 0.2 collective-permute-start.2
  18.2 1.0 %collective-permute-done.2 = f32[8,8,32]{2,1,0:T(8,128)S(1)} collective-permute-done((f32[8,8,32]{2,1,0:T(8,128)S(1)}, f32[8,8,32]{2,1,0:T(8,128)S(1)}, u32[]{:S(2)}, u32[]{:S(2)}) %collective-permute-start.2) | collective-permute-done | bytes 8224 | tf_op jit(solution)/shard_map/ppermute | solution.py:481
  19.3 1.6 %collective-permute-start.3 = (f32[4,8,32]{2,1,0:T(8,128)S(1)}, f32[4,8,32]{2,1,0:T(8,128)S(1)}, u32[]{:S(2)}, u32[]{:S(2)}) collective-permute-start(f32[4,8,32]{2,1,0:T(8,128)S(1)} %constant_dynamic-slice_fusion.2), channel_id=1, source_target_pairs={{0,2},{1,3},{2,0},{3,1},{4,6},{5,7},{6,4},{7,5},{8,10},{9,11},{10,... | collective-permute-start | bytes 12296 | tf_op jit(solution)/shard_map/ppermute | solution.py:481
  20.9 2.2 %collective-permute-done.3 = f32[4,8,32]{2,1,0:T(8,128)S(1)} collective-permute-done((f32[4,8,32]{2,1,0:T(8,128)S(1)}, f32[4,8,32]{2,1,0:T(8,128)S(1)}, u32[]{:S(2)}, u32[]{:S(2)}) %collective-permute-start.3) | collective-permute-done | bytes 4128 | tf_op jit(solution)/shard_map/ppermute | solution.py:481
  23.1 1.6 %collective-permute-start.4 = (f32[2,8,32]{2,1,0:T(8,128)S(1)}, f32[2,8,32]{2,1,0:T(8,128)S(1)}, u32[]{:S(2)}, u32[]{:S(2)}) collective-permute-start(f32[2,8,32]{2,1,0:T(8,128)S(1)} %constant_dynamic-slice_fusion.1), channel_id=1, source_target_pairs={{0,4},{4,0},{8,12},{12,8},{1,5},{5,1},{9,13},{13,9},{2,6},{6,2},{1... | collective-permute-start | bytes 6152 | tf_op jit(solution)/shard_map/ppermute | solution.py:481
  24.7 2.0 %collective-permute-done.4 = f32[2,8,32]{2,1,0:T(8,128)S(1)} collective-permute-done((f32[2,8,32]{2,1,0:T(8,128)S(1)}, f32[2,8,32]{2,1,0:T(8,128)S(1)}, u32[]{:S(2)}, u32[]{:S(2)}) %collective-permute-start.4) | collective-permute-done | bytes 2080 | tf_op jit(solution)/shard_map/ppermute | solution.py:481
  26.8 2.6 %collective-permute-start.5 = (f32[1,8,32]{2,1,0:T(8,128)S(1)}, f32[1,8,32]{2,1,0:T(8,128)S(1)}, u32[]{:S(2)}, u32[]{:S(2)}) collective-permute-start(f32[1,8,32]{2,1,0:T(8,128)S(1)} %constant_dynamic-slice_fusion), channel_id=1, source_target_pairs={{0,8},{4,12},{8,0},{12,4},{1,9},{5,13},{9,1},{13,5},{2,10},{6,14},... | collective-permute-start | bytes 3080 | tf_op jit(solution)/shard_map/ppermute | solution.py:481
  29.4 1.9 %collective-permute-done.5 = f32[1,8,32]{2,1,0:T(8,128)S(1)} collective-permute-done((f32[1,8,32]{2,1,0:T(8,128)S(1)}, f32[1,8,32]{2,1,0:T(8,128)S(1)}, u32[]{:S(2)}, u32[]{:S(2)}) %collective-permute-start.5) | collective-permute-done | bytes 1056 | tf_op jit(solution)/shard_map/ppermute | solution.py:481
  31.3 0.6 %slice_bitcast_fusion = f32[6,32]{1,0:T(8,128)} fusion(f32[1,8,32]{2,1,0:T(8,128)S(1)} %dynamic-slice_add_fusion.3), kind=kLoop, calls=%fused_computation.3 | loop fusion | bytes 1536 | tf_op jit(solution)/shard_map/squeeze | solution.py:494
  (8 shorter events, 0.0 us)
Async XLA Ops:
  0.0 4.9 %copy-start = (f32[64,512]{1,0:T(8,128)S(1)}, f32[64,512]{1,0:T(8,128)}, u32[]{:S(2)}) copy-start(f32[64,512]{1,0:T(8,128)} %adj.3) | copy-start | bytes 393220
  0.0 4.9 %copy-start.1 = (f32[64,512]{1,0:T(8,128)S(1)}, f32[64,512]{1,0:T(8,128)}, u32[]{:S(2)}) copy-start(f32[64,512]{1,0:T(8,128)} %fwd.3) | copy-start | bytes 393220
  1.8 3.1 %copy-start.2 = (f32[7,512]{1,0:T(8,128)S(1)}, f32[7,512]{1,0:T(8,128)}, u32[]{:S(2)}) copy-start(f32[7,512]{1,0:T(8,128)} %geo_ref.1) | copy-start | bytes 43012
  1.8 3.1 %collective-permute-start.1 = (f32[80,512]{1,0:T(8,128)}, f32[80,512]{1,0:T(8,128)S(1)}, u32[]{:S(2)}, u32[]{:S(2)}) collective-permute-start(f32[80,512]{1,0:T(8,128)} %get-tuple-element.14), channel_id=1, source_target_pairs={{0,1},{1,0},{2,3},{3,2},{4,5},{5,4},{6,7},{7,6},{8,9},{9,8},{10,11... | collective-permute-start | bytes 491528 | tf_op jit(solution)/shard_map/ppermute | solution.py:481
  2.3 8.7 %collective-permute-start = (f32[80,512]{1,0:T(8,128)}, f32[80,512]{1,0:T(8,128)S(1)}, u32[]{:S(2)}, u32[]{:S(2)}) collective-permute-start(f32[80,512]{1,0:T(8,128)} %get-tuple-element.13.tpack), channel_id=1, source_target_pairs={{0,2},{1,3},{2,0},{3,1},{4,6},{5,7},{6,4},{7,5},{8,10},{9,11},{10,... | collective-permute-start | bytes 491528 | tf_op jit(solution)/shard_map/ppermute | solution.py:481
  4.9 6.2 %copy-start.3 = (f32[80,512]{1,0:T(8,128)S(1)}, f32[80,512]{1,0:T(8,128)}, u32[]{:S(2)}) copy-start(f32[80,512]{1,0:T(8,128)} %get-tuple-element.13.tpack) | copy-start | bytes 491524
  18.0 1.3 %collective-permute-start.2 = (f32[8,8,32]{2,1,0:T(8,128)S(1)}, f32[8,8,32]{2,1,0:T(8,128)S(1)}, u32[]{:S(2)}, u32[]{:S(2)}) collective-permute-start(f32[8,8,32]{2,1,0:T(8,128)S(1)} %constant_dynamic-slice_fusion.3), channel_id=1, source_target_pairs={{0,1},{1,0},{2,3},{3,2},{4,5},{5,4},{6,7},{7,6},{8,9},{9,8},{10,11... | collective-permute-start | bytes 24584 | tf_op jit(solution)/shard_map/ppermute | solution.py:481
  19.3 3.8 %collective-permute-start.3 = (f32[4,8,32]{2,1,0:T(8,128)S(1)}, f32[4,8,32]{2,1,0:T(8,128)S(1)}, u32[]{:S(2)}, u32[]{:S(2)}) collective-permute-start(f32[4,8,32]{2,1,0:T(8,128)S(1)} %constant_dynamic-slice_fusion.2), channel_id=1, source_target_pairs={{0,2},{1,3},{2,0},{3,1},{4,6},{5,7},{6,4},{7,5},{8,10},{9,11},{10,... | collective-permute-start | bytes 12296 | tf_op jit(solution)/shard_map/ppermute | solution.py:481
  23.1 3.7 %collective-permute-start.4 = (f32[2,8,32]{2,1,0:T(8,128)S(1)}, f32[2,8,32]{2,1,0:T(8,128)S(1)}, u32[]{:S(2)}, u32[]{:S(2)}) collective-permute-start(f32[2,8,32]{2,1,0:T(8,128)S(1)} %constant_dynamic-slice_fusion.1), channel_id=1, source_target_pairs={{0,4},{4,0},{8,12},{12,8},{1,5},{5,1},{9,13},{13,9},{2,6},{6,2},{1... | collective-permute-start | bytes 6152 | tf_op jit(solution)/shard_map/ppermute | solution.py:481
  26.8 4.5 %collective-permute-start.5 = (f32[1,8,32]{2,1,0:T(8,128)S(1)}, f32[1,8,32]{2,1,0:T(8,128)S(1)}, u32[]{:S(2)}, u32[]{:S(2)}) collective-permute-start(f32[1,8,32]{2,1,0:T(8,128)S(1)} %constant_dynamic-slice_fusion), channel_id=1, source_target_pairs={{0,8},{4,12},{8,0},{12,4},{1,9},{5,13},{9,1},{13,5},{2,10},{6,14},... | collective-permute-start | bytes 3080 | tf_op jit(solution)/shard_map/ppermute | solution.py:481
